TPU v7x, 128 devices: a whole 4x4x4 slice. The times are simulated.
128 devices in a mesh: facet: 64 (over x, y, z_lo, core), rows: 2 (over z_hi).
Axes of the slice: x: 4, y: 4, z: 4 (z_hi: 2, z_lo: 2; z = z_hi * 2 + z_lo), core: 2. Of those that a mesh axis runs over, the one named last changes fastest.
Arguments:
- facets: float32 [64, 2, 8, 16384], P('facet', None, 'rows'), may hold values from -6 to 6
- facet_window: float32 [16384], replicated, may hold values from 0.3 to 3
- band_window: float32 [1024], replicated, may hold values from 0.3 to 3
- facet_order: int32 [64], replicated, may hold values from 0 to 63, each once
- facet_offsets: int32 [64, 2], replicated, may hold values from 0 to 262143
- sub_cols: int32 [64], replicated, may hold values from 0 to 262143
- sub_rows: int32 [64], replicated, may hold values from 0 to 262143
Outputs:
- subgrids: float32 [64, 2, 1024, 1024], P('facet', None, 'rows')
All inputs are finite; a program needn't handle non-finite values.
Results may differ from a plain program's by a relative error of at most 0.0003.
The roundings to bfloat16 on the way count: a program that leaves them out, or rounds other values in their place, can miss the bound.
Values sent between devices are 32-bit elements; how exact they have to be, the bound alone decides.
No kernel may reach another device: no remote copies, remote signals or barrier semaphores. Data moves between devices by JAX's collectives and lax.ppermute only.
A program may use at most 128 MiB of HBM per device.

v0:
```python
import math

import jax
import jax.numpy as jnp
from jax import lax
from jax.sharding import PartitionSpec as P

NIMG = 262144
M = 1024
SUBROWS = 1024


TWO_PI = 2.0 * math.pi


def mulmod(left, right, modulus):
    high = right // 1024
    low = right % 1024
    return (left * high % modulus * 1024 + left * low) % modulus


def per_device(facets, facet_window, band_window, facet_order, facet_offsets, sub_cols, sub_rows):
    scale = TWO_PI / NIMG
    hi = lax.Precision.HIGHEST
    data = facets[0]
    rows_here = data.shape[1]
    width = data.shape[2]
    owners = lax.axis_size("facet")
    slots = jnp.arange(owners, dtype=jnp.int32)
    own_slot = lax.axis_index("facet")
    own_facet = jnp.sum(jnp.where(slots == own_slot, facet_order, 0))
    own_cols = jnp.sum(jnp.where(slots == own_facet, facet_offsets[:, 0], 0))
    match = facet_order[:, None] == slots[None, :]
    row_off = jnp.sum(jnp.where(match, facet_offsets[None, :, 1], 0), 1)
    own_subrow = jnp.sum(jnp.where(slots == own_slot, sub_rows, 0))
    place = (own_cols + jnp.arange(width, dtype=jnp.int32)) % NIMG
    windowed = data * facet_window
    angle = scale * mulmod(place[None, :], sub_cols[:, None], NIMG).astype(jnp.float32)
    cosine = jnp.cos(angle)[:, None, :]
    sine = jnp.sin(angle)[:, None, :]
    real_in = windowed[0][None]
    imag_in = windowed[1][None]
    shift_re = (real_in * cosine + imag_in * sine).astype(jnp.bfloat16).reshape(-1, width)
    shift_im = (imag_in * cosine - real_in * sine).astype(jnp.bfloat16).reshape(-1, width)
    block = min(width, 1024)
    bands = jnp.arange(M, dtype=jnp.int32)
    inner = jnp.arange(block, dtype=jnp.int32)
    tangle = scale * mulmod(inner[:, None], bands[None, :], NIMG).astype(jnp.float32)
    table_c = jnp.cos(tangle).astype(jnp.bfloat16)
    table_s = jnp.sin(tangle).astype(jnp.bfloat16)
    table = jnp.concatenate(
        [jnp.concatenate([table_c, -table_s], 1), jnp.concatenate([table_s, table_c], 1)], 0
    )

    def add_block(step, totals):
        start = step * block
        left = jnp.concatenate(
            [
                lax.dynamic_slice_in_dim(shift_re, start, block, 1),
                lax.dynamic_slice_in_dim(shift_im, start, block, 1),
            ],
            1,
        )
        part = jnp.dot(left, table, preferred_element_type=jnp.float32)
        part_re = part[:, :M]
        part_im = part[:, M:]
        bstart = (own_cols + start) % NIMG
        pangle = scale * mulmod(bstart, bands, NIMG).astype(jnp.float32)
        pcos = jnp.cos(pangle)[None]
        psin = jnp.sin(pangle)[None]
        return (
            totals[0] + (part_re * pcos + part_im * psin),
            totals[1] + (part_im * pcos - part_re * psin),
        )

    empty = jnp.zeros((shift_re.shape[0], M), jnp.float32)
    sum_re, sum_im = lax.fori_loop(0, width // block, add_block, (empty, empty))
    summed = jnp.stack([sum_re, sum_im], 1)
    contrib = jnp.transpose(summed.reshape(owners, rows_here, 2, M), (0, 2, 1, 3)) * band_window
    halves = lax.axis_size("rows")
    share = SUBROWS // halves
    whole = lax.all_gather(
        lax.all_to_all(contrib, "facet", split_axis=0, concat_axis=0, tiled=True),
        "rows",
        axis=2,
        tiled=True,
    )
    all_rows = jnp.arange(whole.shape[2], dtype=jnp.int32)
    targets = lax.axis_index("rows") * share + jnp.arange(share, dtype=jnp.int32)
    place_rows = (row_off[:, None] + all_rows[None, :]) % NIMG
    target = (own_subrow + targets) % NIMG
    rangle = scale * mulmod(place_rows[:, :, None], target[None, None, :], NIMG).astype(jnp.float32)
    rangle = rangle.reshape(-1, target.shape[0])
    left = jnp.concatenate([jnp.cos(rangle).T, jnp.sin(rangle).T], 1)
    count = whole.shape[3]
    real_part = whole[:, 0].reshape(-1, count)
    imag_part = whole[:, 1].reshape(-1, count)
    out_re = jnp.dot(left, jnp.concatenate([real_part, imag_part], 0), precision=hi)
    out_im = jnp.dot(left, jnp.concatenate([imag_part, -real_part], 0), precision=hi)
    result = jnp.stack([out_re, out_im], 0)
    squares = lax.psum(jnp.sum(result * result), "rows")
    mean = squares / (2.0 * SUBROWS * M)
    return (result * lax.rsqrt(mean + 1e-06))[None]


def solution(mesh):
    return jax.shard_map(
        per_device,
        mesh=mesh,
        in_specs=(P("facet", None, "rows", None), P(), P(), P(), P(), P(), P()),
        out_specs=P("facet", None, "rows", None),
        check_vma=False,
    )
```

profile of v0, /device:TPU:1, one launch (start us, length us, event | category | flops | bytes accessed | tf_op | source)
XLA Modules:
  0.0 434.0 jit_solution(17814412148439212618)
XLA Ops:
  6.6 19.9 %sine_convert_fusion = (bf16[1024,1024]{1,0:T(8,128)(2,1)S(1)}, bf16[1024,1024]{1,0:T(8,128)(2,1)}) fusion(s32[1024]{0:T(1024)S(1)} %get-tuple-element.405, s32[1024]{0:T(1024)S(1)} %get-tuple-element.406), kind=kLoop, calls=%fused_computation.82 | loop fusion | flops 31457280 | bytes 4202496 | tf_op jit(solution)/shard_map/convert_element_type | solution.py:50
  26.5 18.7 %fusion.62 = bf16[1024,1024]{1,0:T(8,128)(2,1)} fusion(s32[1024]{0:T(1024)S(1)} %get-tuple-element.405, s32[1024]{0:T(1024)S(1)} %get-tuple-element.406), kind=kLoop, calls=%fused_computation.108 | loop fusion | flops 33554432 | bytes 2105344 | tf_op jit(solution)/shard_map/neg | solution.py:52
  49.0 18.4 %fusion.53 = (f32[64,16384]{1,0:T(8,128)S(1)}, f32[64,16384]{1,0:T(8,128)S(1)}) fusion(s32[64]{0:T(128)S(1)} %get-tuple-element.402, s32[64]{0:T(128)S(1)} %get-tuple-element.401, s32[16384]{0:T(1024)S(1)} %add_select_fusion.9), kind=kLoop, calls=%fused_computation.90 | loop fusion | flops 29360128 | bytes 8454656 | tf_op jit(solution)/shard_map/cos | solution.py:39
  67.5 10.8 %subtract_convert_fusion = (bf16[64,4,16384]{2,1,0:T(4,128)(2,1)}, bf16[64,4,16384]{2,1,0:T(4,128)(2,1)}) fusion(f32[64,16384]{1,0:T(8,128)S(1)} %get-tuple-element.396, f32[4,16384]{1,0:T(4,128)S(1)} %get-tuple-element.394, f32[64,16384]{1,0:T(8,128)S(1)} %get-tuple-element.395, f32[4,16384]{1,0:T(4,128)S(1)} %get-tuple-element.393), kind=kLoop, calls=%fused_computation.39 | loop fusion | flops 33554432 | bytes 25690112 | tf_op jit(solution)/shard_map/convert_element_type | solution.py:44
  78.3 12.6 %convert_element_type.77 = bf16[256,16384]{1,0:T(8,128)(2,1)} reshape(bf16[64,4,16384]{2,1,0:T(4,128)(2,1)} %get-tuple-element.390) | data formatting | bytes 16777216 | tf_op jit(solution)/shard_map/convert_element_type | solution.py:43
  90.8 12.5 %convert_element_type.79 = bf16[256,16384]{1,0:T(8,128)(2,1)} reshape(bf16[64,4,16384]{2,1,0:T(4,128)(2,1)} %get-tuple-element.389) | data formatting | bytes 16777216 | tf_op jit(solution)/shard_map/convert_element_type | solution.py:44
  103.4 13.4 %maximum_maximum_fusion = bf16[2048,2048]{1,0:T(8,128)(2,1)} fusion(bf16[1024,1024]{1,0:T(8,128)(2,1)} %get-tuple-element.398, bf16[1024,1024]{1,0:T(8,128)(2,1)S(1)} %get-tuple-element.397, bf16[1024,1024]{1,0:T(8,128)(2,1)} %fusion.62), kind=kLoop, calls=%fused_computation.41 | loop fusion | flops 33554432 | bytes 14680064 | tf_op jit(solution)/shard_map/concatenate | solution.py:51
  116.8 172.6 %while.21 = (s32[]{:T(128)}, f32[256,1024]{1,0:T(8,128)S(1)}, f32[256,1024]{1,0:T(8,128)}, bf16[256,16384]{1,0:T(8,128)(2,1)}, bf16[256,16384]{1,0:T(8,128)(2,1)...) while((s32[]{:T(128)}, f32[256,1024]{1,0:T(8,128)S(1)}, ...), condition=%wide.region_5.6_spmd.clone.clone, body=%wide.region_4.5_spmd.clone.clone.sunk | while | flops 2152243200 | bytes 19941684 | solution.py:77
  118.8 5.7 %fusion.91 = f32[256,2048]{1,0:T(8,128)S(1)} fusion(bf16[2048,2048]{1,0:T(8,128)(2,1)} %get-tuple-element.493, bf16[256,1024]{1,0:T(8,128)(2,1)S(1)} %get-tuple-element.456, bf16[256,1024]{1,0:T(8,128)(2,1)S(1)} %get-tuple-element.457), kind=kOutput, calls=%fused_computation.4.clone.1 | convolution fusion | flops 2149580800 | bytes 11534336 | tf_op jit(solution)/shard_map/while/body/eval_jaxpr/dot_general | solution.py:64
  139.3 5.7 %fusion.91 = f32[256,2048]{1,0:T(8,128)S(1)} fusion(bf16[2048,2048]{1,0:T(8,128)(2,1)} %get-tuple-element.493, bf16[256,1024]{1,0:T(8,128)(2,1)S(1)} %get-tuple-element.456, bf16[256,1024]{1,0:T(8,128)(2,1)S(1)} %get-tuple-element.457), kind=kOutput, calls=%fused_computation.4.clone.1 | convolution fusion | flops 2149580800 | bytes 11534336 | tf_op jit(solution)/shard_map/while/body/eval_jaxpr/dot_general | solution.py:64
  150.2 5.7 %fusion.91 = f32[256,2048]{1,0:T(8,128)S(1)} fusion(bf16[2048,2048]{1,0:T(8,128)(2,1)} %get-tuple-element.493, bf16[256,1024]{1,0:T(8,128)(2,1)S(1)} %get-tuple-element.456, bf16[256,1024]{1,0:T(8,128)(2,1)S(1)} %get-tuple-element.457), kind=kOutput, calls=%fused_computation.4.clone.1 | convolution fusion | flops 2149580800 | bytes 11534336 | tf_op jit(solution)/shard_map/while/body/eval_jaxpr/dot_general | solution.py:64
  161.0 5.7 %fusion.91 = f32[256,2048]{1,0:T(8,128)S(1)} fusion(bf16[2048,2048]{1,0:T(8,128)(2,1)} %get-tuple-element.493, bf16[256,1024]{1,0:T(8,128)(2,1)S(1)} %get-tuple-element.456, bf16[256,1024]{1,0:T(8,128)(2,1)S(1)} %get-tuple-element.457), kind=kOutput, calls=%fused_computation.4.clone.1 | convolution fusion | flops 2149580800 | bytes 11534336 | tf_op jit(solution)/shard_map/while/body/eval_jaxpr/dot_general | solution.py:64
  193.6 5.7 %fusion.91 = f32[256,2048]{1,0:T(8,128)S(1)} fusion(bf16[2048,2048]{1,0:T(8,128)(2,1)} %get-tuple-element.493, bf16[256,1024]{1,0:T(8,128)(2,1)S(1)} %get-tuple-element.456, bf16[256,1024]{1,0:T(8,128)(2,1)S(1)} %get-tuple-element.457), kind=kOutput, calls=%fused_computation.4.clone.1 | convolution fusion | flops 2149580800 | bytes 11534336 | tf_op jit(solution)/shard_map/while/body/eval_jaxpr/dot_general | solution.py:64
  204.5 5.7 %fusion.91 = f32[256,2048]{1,0:T(8,128)S(1)} fusion(bf16[2048,2048]{1,0:T(8,128)(2,1)} %get-tuple-element.493, bf16[256,1024]{1,0:T(8,128)(2,1)S(1)} %get-tuple-element.456, bf16[256,1024]{1,0:T(8,128)(2,1)S(1)} %get-tuple-element.457), kind=kOutput, calls=%fused_computation.4.clone.1 | convolution fusion | flops 2149580800 | bytes 11534336 | tf_op jit(solution)/shard_map/while/body/eval_jaxpr/dot_general | solution.py:64
  215.3 5.7 %fusion.91 = f32[256,2048]{1,0:T(8,128)S(1)} fusion(bf16[2048,2048]{1,0:T(8,128)(2,1)} %get-tuple-element.493, bf16[256,1024]{1,0:T(8,128)(2,1)S(1)} %get-tuple-element.456, bf16[256,1024]{1,0:T(8,128)(2,1)S(1)} %get-tuple-element.457), kind=kOutput, calls=%fused_computation.4.clone.1 | convolution fusion | flops 2149580800 | bytes 11534336 | tf_op jit(solution)/shard_map/while/body/eval_jaxpr/dot_general | solution.py:64
  247.9 5.7 %fusion.91 = f32[256,2048]{1,0:T(8,128)S(1)} fusion(bf16[2048,2048]{1,0:T(8,128)(2,1)} %get-tuple-element.493, bf16[256,1024]{1,0:T(8,128)(2,1)S(1)} %get-tuple-element.456, bf16[256,1024]{1,0:T(8,128)(2,1)S(1)} %get-tuple-element.457), kind=kOutput, calls=%fused_computation.4.clone.1 | convolution fusion | flops 2149580800 | bytes 11534336 | tf_op jit(solution)/shard_map/while/body/eval_jaxpr/dot_general | solution.py:64
  258.8 5.7 %fusion.91 = f32[256,2048]{1,0:T(8,128)S(1)} fusion(bf16[2048,2048]{1,0:T(8,128)(2,1)} %get-tuple-element.493, bf16[256,1024]{1,0:T(8,128)(2,1)S(1)} %get-tuple-element.456, bf16[256,1024]{1,0:T(8,128)(2,1)S(1)} %get-tuple-element.457), kind=kOutput, calls=%fused_computation.4.clone.1 | convolution fusion | flops 2149580800 | bytes 11534336 | tf_op jit(solution)/shard_map/while/body/eval_jaxpr/dot_general | solution.py:64
  269.6 5.7 %fusion.91 = f32[256,2048]{1,0:T(8,128)S(1)} fusion(bf16[2048,2048]{1,0:T(8,128)(2,1)} %get-tuple-element.493, bf16[256,1024]{1,0:T(8,128)(2,1)S(1)} %get-tuple-element.456, bf16[256,1024]{1,0:T(8,128)(2,1)S(1)} %get-tuple-element.457), kind=kOutput, calls=%fused_computation.4.clone.1 | convolution fusion | flops 2149580800 | bytes 11534336 | tf_op jit(solution)/shard_map/while/body/eval_jaxpr/dot_general | solution.py:64
  291.8 39.2 %all_to_all.5 = f32[64,2,4,1024]{3,2,1,0:T(4,128)S(1)} all-to-all(f32[64,2,4,1024]{3,2,1,0:T(4,128)S(1)} %fusion.51), channel_id=1, replica_groups=mesh['facet'=64,'rows'=2] {'facet'}, dimensions={0} | all-to-all | bytes 4194304 | tf_op jit(solution)/shard_map/all_to_all | solution.py:83
  335.0 6.3 %fusion.61 = (f32[512,512]{1,0:T(8,128)S(1)}, f32[512,512]{1,0:T(8,128)}) fusion(s32[512]{0:T(512)S(1)} %add_select_fusion.11, s32[512]{0:T(512)S(1)} %add_select_fusion.12, s32[512]{0:T(512)S(1)} %add_select_fusion.14), kind=kLoop, calls=%fused_computation.107 | loop fusion | flops 7340032 | bytes 2103296 | tf_op jit(solution)/shard_map/cos | solution.py:94
  341.2 51.6 %all-gather.2.cloned.1.call-done = f32[64,2,8,1024]{3,0,1,2:T(8,128)} async-done(((f32[64,2,4,1024]{3,0,1,2:T(8,128)}), f32[64,2,8,1024]{3,0,1,2:T(8,128)}) %all-gather.2.cloned.1.call-update) | async-done | bytes 4194320 | tf_op jit(solution)/shard_map/all_gather | solution.py:82
  399.2 6.9 %fusion.42 = f32[512,1024]{1,0:T(8,128)S(1)} fusion(f32[512,1024]{1,0:T(8,128)S(1)} %bitcast.32, f32[512,1024]{1,0:T(8,128)S(1)} %bitcast.34, f32[512,512]{1,0:T(8,128)S(1)} %copy-done.1, f32[512,512]{1,0:T(8,128)S(1)} %get-tuple-element.399), kind=kOutput, calls=%fused_computation.71 | convolution fusion | flops 6444023808 | bytes 8388608 | tf_op jit(solution)/shard_map/dot_general | solution.py:98
  406.1 7.1 %fusion.46 = f32[512,1024]{1,0:T(8,128)S(1)} fusion(f32[512,1024]{1,0:T(8,128)S(1)} %fusion.82, f32[512,1024]{1,0:T(8,128)S(1)} %bitcast.33, f32[512,512]{1,0:T(8,128)S(1)} %copy-done.1, f32[512,512]{1,0:T(8,128)S(1)} %get-tuple-element.399), kind=kOutput, calls=%fused_computation.75 | convolution fusion | flops 6444023808 | bytes 8388608 | tf_op jit(solution)/shard_map/dot_general | solution.py:99
  416.2 5.9 %psum.7 = f32[]{:T(128)} all-reduce(f32[]{:T(128)} %fusion.50), channel_id=1, replica_groups=mesh['facet'=64,'rows'=2] {'rows'}, use_global_device_ids=true, to_apply=%region_7.8 | all-reduce | flops 1 | bytes 8 | tf_op jit(solution)/shard_map/psum | solution.py:101
  (114 shorter events, 128.4 us)
Async XLA Ops:
  6.5 38.7 %copy-start.5 = (s32[64]{0:T(128)S(1)}, s32[64]{0:T(128)}, u32[]{:S(2)}) copy-start(s32[64]{0:T(128)} %param.12) | copy-start | bytes 772
  6.5 38.7 %copy-start.4 = (s32[64]{0:T(128)S(1)}, s32[64]{0:T(128)}, u32[]{:S(2)}) copy-start(s32[64]{0:T(128)} %param.15) | copy-start | bytes 772
  6.5 39.3 %copy-start.6 = (s32[64,2]{0,1:T(2,128)S(1)}, s32[64,2]{0,1:T(2,128)}, u32[]{:S(2)}) copy-start(s32[64,2]{0,1:T(2,128)} %param.13) | copy-start | bytes 1540
  6.5 41.2 %copy-start.7 = (s32[64]{0:T(128)S(1)}, s32[64]{0:T(128)}, u32[]{:S(2)}) copy-start(s32[64]{0:T(128)} %param.14) | copy-start | bytes 772
  6.5 41.3 %copy-start.2 = (f32[16384]{0:T(1024)S(1)}, f32[16384]{0:T(1024)}, u32[]{:S(2)}) copy-start(f32[16384]{0:T(1024)} %param.10) | copy-start | bytes 196612
  6.5 386.3 %all-gather.2.cloned.1.call-start = ((), (), s32[]{:S(2)}) async-start(), calls=%async_computation.1 | async-start | bytes 6291456 | tf_op jit(solution)/shard_map/all_gather | solution.py:82
  289.4 1.8 copy-start.3
  396.6 2.6 copy-start.1
  413.2 1.3 copy-start
Sparse Core Ops, SparseCore 0:
  333.6 59.1 all-gather.1
where the time goes:
time: 440 us; the launch traced here: 434 us
  other arithmetic  150 us (34%)
  matrix products  106 us (24%)
  local copies, waits for them, and re-layouts  56.4 us (13%)
  waiting for transfers between devices  51.6 us (12%)
  blocking collectives  45.1 us (10%)
  between operations  14.5 us (3%)
  loops' own time  10.6 us (2%)
    dot_general x16, matrix products, add_block(): part = jnp.dot(left, table, preferred_element_type=jnp.float32)  91.8 us
    all_gather x1, waiting for transfers between devices, per_device(): lax.all_gather(lax.all_to_all(contrib, 'facet', split_axis=0, concat_axis...  51.6 us
    add x16, other arithmetic, add_block(): totals[1] + (part_im * pcos - part_re * psin)  48.2 us
    all_to_all x1, blocking collectives, per_device(): lax.all_to_all(contrib, 'facet', split_axis=0, concat_axis=0, tiled=True)  39.2 us
    dynamic_slice x16, local copies, waits for them, and re-layouts, add_block(): lax.dynamic_slice_in_dim(shift_im, start, block, 1)  20.4 us
    convert_element_type x1, other arithmetic, per_device(): table_s = jnp.sin(tangle).astype(jnp.bfloat16)  19.9 us
    neg x1, other arithmetic, per_device(): -table_s  18.7 us
    cos x1, other arithmetic, per_device(): cosine = jnp.cos(angle)[:, None, :]  18.4 us
  transfers between devices with their start and end apart: 1, of which 1 were waited for; matrix products, arithmetic and copies ran while one was open for 2% of the time, Pallas kernels for 0%

commit v1 on v0

v1 whole, which is shorter than its diff:
```python
import functools
import math

import jax
import jax.numpy as jnp
import ml_dtypes
import numpy as np
from jax import lax
from jax.experimental import pallas as pl
from jax.experimental.pallas import tpu as pltpu
from jax.sharding import PartitionSpec as P

NIMG = 262144
M = 1024
SUBROWS = 1024
TWO_PI = 2.0 * math.pi

BLOCK = 1024
SPAN = 4096
NODES = 32
RANK = 4
ERANK = 2
ROW_SCALE = 4.0

f32 = jnp.float32
bf16 = jnp.bfloat16


def _split(values):
    high = values.astype(np.float32).astype(ml_dtypes.bfloat16)
    low = (values - high.astype(np.float64)).astype(np.float32).astype(ml_dtypes.bfloat16)
    return high, low


def _kernel_sum(x, count):
    den = np.sin(np.pi * x / NIMG)
    zero = np.abs(den) < 1e-14
    return np.where(zero, float(count), np.sin(np.pi * x * count / NIMG) / np.where(zero, 1.0, den))


def _solve(gram, right):
    gram, right = gram.copy(), right.copy()
    n = len(gram)
    for i in range(n):
        for j in range(i + 1, n):
            factor = gram[j, i] / gram[i, i]
            gram[j] = gram[j] - factor * gram[i]
            right[j] = right[j] - factor * right[i]
    out = np.zeros_like(right)
    for i in range(n - 1, -1, -1):
        total = right[i].copy()
        for j in range(i + 1, n):
            total = total - gram[i, j] * out[j]
        out[i] = total / gram[i, i]
    return out


@functools.lru_cache(maxsize=None)
def _tables():
    scale = TWO_PI / NIMG
    bands = np.arange(M)
    product = (np.arange(BLOCK)[:, None] * bands[None, :]) % NIMG
    angle = (np.float32(scale) * product.astype(np.float32)).astype(np.float64)
    exact = scale * product
    resid_c = np.cos(angle).astype(np.float32).astype(ml_dtypes.bfloat16).astype(np.float64) - np.cos(exact)
    resid_s = np.sin(angle).astype(np.float32).astype(ml_dtypes.bfloat16).astype(np.float64) - np.sin(exact)
    half = M // 2
    resid = np.stack(
        [np.concatenate([resid_c[:, h * half:(h + 1) * half], resid_s[:, h * half:(h + 1) * half]], 1) for h in range(2)]
    ).astype(np.float32).astype(ml_dtypes.bfloat16)
    i = np.arange(NODES)
    nodes = 511.5 + 512 * 1.05 * (0.25 * ((2 * i + 1) / NODES - 1) - 0.75 * np.cos(np.pi * (i + 0.5) / NODES))
    gram = _kernel_sum(nodes[:, None] - nodes[None, :], SPAN) + 1e-13 * SPAN * np.eye(NODES)
    interp = _solve(gram, _kernel_sum(nodes[:, None] - bands[None, :], SPAN))
    centre = (SPAN - 1) / 2
    at = scale * (np.arange(SPAN) - centre)[:, None] * nodes[None, :]
    sample = np.concatenate([np.cos(at), -np.sin(at)], 1)
    sample = np.concatenate(_split(sample), 1)
    rows = []
    for span in range(16384 // SPAN):
        turn = scale * (span * SPAN + centre) * bands
        re, im = interp * np.cos(turn), -interp * np.sin(turn)
        rows.append(np.concatenate([re, im], 1))
        rows.append(np.concatenate([-im, re], 1))
    weave = np.concatenate(rows, 0)
    weave_hi, weave_lo = _split(weave)
    turn = TWO_PI * ((np.arange(16)[:, None] * (bands[None, :half] % 256)) % 256) / 256
    return dict(
        resid=resid, sample=sample, weave_hi=weave_hi, weave_lo=weave_lo,
        turn_c=np.cos(turn).astype(np.float32), turn_s=np.sin(turn).astype(np.float32),
    )


COL_A, COL_L8, COL_P8, COL_ROW = 384, 400, 408, 416


def _pick(table, index):
    lane = lax.broadcasted_iota(jnp.int32, table.shape, 1)
    return jnp.sum(jnp.where(lane == index, table, 0.0), axis=1, keepdims=True)


def _fill_columns(cos_ref, sin_ref, lc_ref, ls_ref):
    low_c, low_s = cos_ref[:, 0:128], sin_ref[:, 0:128]
    for i in range(8):
        c, s = cos_ref[:, COL_L8 + i:COL_L8 + i + 1], sin_ref[:, COL_L8 + i:COL_L8 + i + 1]
        lc_ref[:, i * 128:(i + 1) * 128] = c * low_c - s * low_s
        ls_ref[:, i * 128:(i + 1) * 128] = s * low_c + c * low_s


def _exact_kernel(data_ref, window_ref, cos_ref, sin_ref, sample_ref, out_ref, lc_ref, ls_ref, acc_ref):
    step = pl.program_id(0)

    @pl.when(step == 0)
    def _():
        _fill_columns(cos_ref, sin_ref, lc_ref, ls_ref)

    block_c = _pick(cos_ref[:, 384:512], step)
    block_s = _pick(sin_ref[:, 384:512], step)
    span = step // 4
    total = None
    width = 256
    for i in range(BLOCK // width):
        cols = slice(i * width, (i + 1) * width)
        lc, ls = lc_ref[:, cols], ls_ref[:, cols]
        ec = block_c * lc - block_s * ls
        es = block_s * lc + block_c * ls
        data = data_ref[:, cols] * window_ref[:, cols]
        re, im = [], []
        for r in range(4):
            dr, di = data[r:r + 1], data[4 + r:5 + r]
            re.append((dr * ec + di * es).astype(bf16))
            im.append((di * ec - dr * es).astype(bf16))
        shifted = jnp.concatenate(re + im, 0)
        part = jnp.dot(shifted, sample_ref[cols, :], preferred_element_type=f32)
        total = part if total is None else total + part

    @pl.when(step % 4 == 0)
    def _():
        acc_ref[span] = total

    @pl.when(step % 4 != 0)
    def _():
        acc_ref[span] = acc_ref[span] + total

    @pl.when(step == 15)
    def _():
        lane = lax.broadcasted_iota(jnp.int32, (64, 128), 1)
        sign = jnp.where(lane & 32 == 0, -1.0, 1.0).astype(f32)
        sums = [[None] * 4 for _ in range(RANK)]
        for sp in range(4):
            for r in range(4):
                ar = acc_ref[sp, r * 64:(r + 1) * 64]
                ai = acc_ref[sp, 256 + r * 64:256 + (r + 1) * 64]
                ar = ar + pltpu.roll(ar, 64, 1)
                ai = ai + pltpu.roll(ai, 64, 1)
                value = ar + sign * pltpu.roll(ai, 32, 1)
                turned = sign * pltpu.roll(value, 32, 1)
                for n in range(RANK):
                    col = COL_ROW + n * 8 + r
                    term = cos_ref[:, col:col + 1] * value + sin_ref[:, col:col + 1] * turned
                    sums[n][sp] = term if sums[n][sp] is None else sums[n][sp] + term
        for n in range(RANK):
            out_ref[:, n * 256:n * 256 + 128] = jnp.where(lane < 64, sums[n][0], sums[n][1])
            out_ref[:, n * 256 + 128:n * 256 + 256] = jnp.where(lane < 64, sums[n][2], sums[n][3])


def _resid_kernel(half_ref, own_ref, peer_ref, window_ref, cos_ref, sin_ref, combine_ref, table_ref, tc_ref, ts_ref,
                  out_ref, lc_ref, ls_ref, mixed_ref):
    step = pl.program_id(0)

    @pl.when(step == 0)
    def _():
        _fill_columns(cos_ref, sin_ref, lc_ref, ls_ref)
        out_ref[...] = jnp.zeros_like(out_ref)

    for j in range(4):
        block = step * 4 + j
        block_c = _pick(cos_ref[:, 384:512], block)
        block_s = _pick(sin_ref[:, 384:512], block)
        for i in range(4):
            cols = slice(i * 256, (i + 1) * 256)
            here = slice(j * BLOCK + i * 256, j * BLOCK + (i + 1) * 256)
            window = window_ref[:, here]
            data = jnp.concatenate([own_ref[:, here] * window, peer_ref[:, here] * window], 0).astype(bf16)
            rows = jnp.dot(combine_ref[...], data, preferred_element_type=f32)
            lc, ls = lc_ref[:, cols], ls_ref[:, cols]
            ec = block_c * lc - block_s * ls
            es = block_s * lc + block_c * ls
            for n in range(ERANK):
                gr, gi = rows[n * 64:(n + 1) * 64], rows[128 + n * 64:128 + (n + 1) * 64]
                mixed_ref[j * 256 + n * 64:j * 256 + (n + 1) * 64, cols] = (gr * ec + gi * es).astype(bf16)
                mixed_ref[j * 256 + 128 + n * 64:j * 256 + 128 + (n + 1) * 64, cols] = (gi * ec - gr * es).astype(bf16)
    for kc in range(2):
        cols = slice(kc * 256, (kc + 1) * 256)
        by_c = jnp.dot(mixed_ref[...], table_ref[0, :, kc * 256:(kc + 1) * 256], preferred_element_type=f32)
        by_s = jnp.dot(mixed_ref[...], table_ref[0, :, 512 + kc * 256:512 + (kc + 1) * 256], preferred_element_type=f32)
        sum_re, sum_im = out_ref[0, :, cols], out_ref[1, :, cols]
        for j in range(4):
            re = by_c[j * 256:j * 256 + 128] + by_s[j * 256 + 128:j * 256 + 256]
            im = by_c[j * 256 + 128:j * 256 + 256] - by_s[j * 256:j * 256 + 128]
            tc = tc_ref[pl.ds(step * 4 + j, 1), cols]
            ts = ts_ref[pl.ds(step * 4 + j, 1), cols]
            sum_re = sum_re + (re * tc + im * ts)
            sum_im = sum_im + (im * tc - re * ts)
        out_ref[0, :, cols] = sum_re
        out_ref[1, :, cols] = sum_im


def _halves(value):
    high = value.astype(bf16)
    return high, (value - high.astype(f32)).astype(bf16)


def _rows_kernel(nodes_ref, resid_ref, cos_ref, sin_ref, band_ref, left_ref, wh_ref, wl_ref, out_ref,
                 right_ref, lcat_ref):
    lh, ll = _halves(left_ref[...])
    lcat_ref[:, 0:512] = lh
    lcat_ref[:, 512:1024] = lh
    lcat_ref[:, 1024:1536] = ll
    nh, nl = _halves(nodes_ref[...])
    low_c, low_s = cos_ref[:, 128:256], sin_ref[:, 128:256]
    for i in range(4):
        cols = slice(i * 256, (i + 1) * 256)
        vals = []
        for part in range(2):
            wcols = slice(part * 1024 + i * 256, part * 1024 + (i + 1) * 256)
            wh, wl = wh_ref[:, wcols], wl_ref[:, wcols]
            vals.append(
                jnp.dot(nh, wh, preferred_element_type=f32)
                + (jnp.dot(nh, wl, preferred_element_type=f32) + jnp.dot(nl, wh, preferred_element_type=f32))
            )
        pcs, pss = [], []
        for m in range(2):
            col = COL_P8 + i * 2 + m
            c, s = cos_ref[:, col:col + 1], sin_ref[:, col:col + 1]
            pcs.append(c * low_c - s * low_s)
            pss.append(s * low_c + c * low_s)
        band = band_ref[:, cols]
        pc = jnp.concatenate(pcs, 1) * band
        ps = jnp.concatenate(pss, 1) * band
        for n in range(RANK):
            vr, vi = vals[0][n * 64:(n + 1) * 64], vals[1][n * 64:(n + 1) * 64]
            if n < ERANK:
                vr = vr + resid_ref[n, 0, :, cols]
                vi = vi + resid_ref[n, 1, :, cols]
            cr = vr * pc + vi * ps
            ci = vi * pc - vr * ps
            for value, row, col in ((cr, 0, 0), (ci, 256, 0), (ci, 0, 1024), (-cr, 256, 1024)):
                high, low = _halves(value)
                base = row + n * 64
                ccols = slice(col + i * 256, col + (i + 1) * 256)
                right_ref[base:base + 64, ccols] = high
                right_ref[512 + base:512 + base + 64, ccols] = low
                right_ref[1024 + base:1024 + base + 64, ccols] = high

    total = jnp.zeros((8, 512), f32)
    for part in range(2):
        for i in range(2):
            cols = slice(part * 1024 + i * 512, part * 1024 + (i + 1) * 512)
            result = jnp.dot(lcat_ref[...], right_ref[:, cols], preferred_element_type=f32)
            out_ref[0, part, :, i * 512:(i + 1) * 512] = result[:512]
            total = total + jnp.sum((result * result).reshape(128, 8, 512), 0)
    mean = jnp.sum(total) / (2.0 * SUBROWS * M)
    factor = lax.rsqrt(jnp.full((8, 128), mean, f32) + 1e-06)[0:1, 0:1]
    for part in range(2):
        out_ref[0, part] = out_ref[0, part] * factor


def _angle(product):
    turns = lax.bitwise_and(product + NIMG, 2 * NIMG - 1) - NIMG
    return turns.astype(f32) * (math.pi / NIMG)


def per_device(facets, facet_window, band_window, facet_order, facet_offsets, sub_cols, sub_rows):
    tables = _tables()
    own = facets.reshape(8, 16384)
    rows_at = lax.axis_index("rows")
    peer = lax.ppermute(own, "rows", [(0, 1), (1, 0)])
    slots = jnp.arange(64, dtype=jnp.int32)
    own_slot = lax.axis_index("facet")
    match = facet_order[:, None] == slots[None, :]
    col_off = jnp.sum(jnp.where(match, facet_offsets[None, :, 0], 0), 1)
    row_off = jnp.sum(jnp.where(match, facet_offsets[None, :, 1], 0), 1)
    own_cols = jnp.sum(jnp.where(slots == own_slot, col_off, 0))
    own_subrow = jnp.sum(jnp.where(slots == own_slot, sub_rows, 0))

    lanes = jnp.arange(128, dtype=jnp.int32)
    rows8 = (4 * rows_at + jnp.arange(8, dtype=jnp.int32)) % 8
    small = jnp.arange(8, dtype=jnp.int32) * 128
    products = jnp.concatenate(
        [
            2 * lanes[None, :] * sub_cols[:, None],
            2 * lanes[None, :] * col_off[:, None],
            jnp.zeros((64, 128), jnp.int32),
            2 * (own_cols + 1024 * jnp.arange(16, dtype=jnp.int32))[None, :] * sub_cols[:, None],
            2 * small[None, :] * sub_cols[:, None],
            2 * small[None, :] * col_off[:, None],
            jnp.tile((2 * rows8 - 7)[None, :] * (sub_rows[:, None] + 512), (1, 4)),
            jnp.zeros((64, 64), jnp.int32),
        ],
        1,
    )
    angles = _angle(products)
    rho = (2 * rows8 - 7).astype(f32) / (2.0 * ROW_SCALE)
    powers = jnp.concatenate([jnp.ones(8, f32), rho, rho * rho, rho * rho * rho])
    scales = jnp.concatenate([jnp.ones(COL_ROW, f32), powers, jnp.ones(64, f32)])[None, :]
    signs = jnp.where((jnp.arange(512) >= COL_ROW) & (jnp.arange(512) < COL_ROW + 32), -1.0, 1.0).astype(f32)[None, :]
    tab_c = jnp.cos(angles) * scales
    tab_s = jnp.sin(angles) * (scales * signs)

    turn_c = tab_c[:, COL_ROW:COL_ROW + 16].reshape(64, ERANK, 2, 4)
    turn_s = tab_s[:, COL_ROW:COL_ROW + 16].reshape(64, ERANK, 2, 4)
    to_re = jnp.stack([turn_c, -turn_s], 3)
    to_im = jnp.stack([turn_s, turn_c], 3)
    combine = jnp.stack([to_re, to_im], 0).transpose(0, 2, 1, 3, 4, 5).reshape(256, 16).astype(bf16)

    q = (rows_at * 512 + jnp.arange(1024, dtype=jnp.int32)) % 1024
    turn = _angle((2 * row_off + 7)[None, :] * (own_subrow + q)[:, None])
    c, s = jnp.cos(turn), jnp.sin(turn)
    g = ((q - 512).astype(f32) * (TWO_PI / NIMG * ROW_SCALE))[:, None]
    g2, g3 = g * g * 0.5, g * g * g * (1.0 / 6.0)
    left = jnp.concatenate([c, -g * s, -g2 * c, g3 * s, s, g * c, -g2 * s, -g3 * c], 1)

    window = facet_window.reshape(1, 16384)
    whole = lambda shape: pl.BlockSpec(shape, lambda *_: (0,) * len(shape))
    params = dict(vmem_limit_bytes=56 * 1024 * 1024)
    nodes = pl.pallas_call(
        _exact_kernel,
        grid=(16,),
        in_specs=[
            pl.BlockSpec((8, BLOCK), lambda b: (0, b)),
            pl.BlockSpec((1, BLOCK), lambda b: (0, b)),
            whole((64, 512)),
            whole((64, 512)),
            pl.BlockSpec((BLOCK, 128), lambda b: (b % 4, 0)),
        ],
        out_specs=whole((64, 1024)),
        out_shape=jax.ShapeDtypeStruct((64, 1024), f32),
        scratch_shapes=[
            pltpu.VMEM((64, 1024), f32),
            pltpu.VMEM((64, 1024), f32),
            pltpu.VMEM((4, 512, 128), f32),
        ],
        compiler_params=pltpu.CompilerParams(dimension_semantics=("arbitrary",), **params),
        cost_estimate=pl.CostEstimate(flops=8 * 10**9, bytes_accessed=2 * 10**6, transcendentals=0),
        name="exact_part",
    )(own, window, tab_c, tab_s, jnp.asarray(tables["sample"]))

    resid = pl.pallas_call(
        _resid_kernel,
        grid_spec=pltpu.PrefetchScalarGridSpec(
            num_scalar_prefetch=1,
            grid=(4,),
            in_specs=[
                pl.BlockSpec((8, 4096), lambda b, h: (0, b)),
                pl.BlockSpec((8, 4096), lambda b, h: (0, b)),
                pl.BlockSpec((1, 4096), lambda b, h: (0, b)),
                whole((64, 512)),
                whole((64, 512)),
                whole((256, 16)),
                pl.BlockSpec((1, 1024, 1024), lambda b, h: (h[0], 0, 0)),
                whole((16, 512)),
                whole((16, 512)),
            ],
            out_specs=whole((2, 128, 512)),
            scratch_shapes=[
                pltpu.VMEM((64, 1024), f32),
                pltpu.VMEM((64, 1024), f32),
                pltpu.VMEM((1024, 1024), bf16),
            ],
        ),
        out_shape=jax.ShapeDtypeStruct((2, 128, 512), f32),
        compiler_params=pltpu.CompilerParams(dimension_semantics=("arbitrary",), **params),
        cost_estimate=pl.CostEstimate(flops=9 * 10**9, bytes_accessed=4 * 10**6, transcendentals=0),
        name="residual_part",
    )(
        rows_at.reshape(1).astype(jnp.int32), own, peer, window, tab_c, tab_s, combine,
        jnp.asarray(tables["resid"]), jnp.asarray(tables["turn_c"]), jnp.asarray(tables["turn_s"]),
    )

    send = jnp.concatenate(
        [
            resid.reshape(2, ERANK, 64, 512).transpose(2, 1, 0, 3).reshape(64, 16, 128),
            nodes.reshape(64, 8, 128),
        ],
        1,
    )
    send = jnp.broadcast_to(send[:, None], (64, 2, 24, 128)).reshape(128, 24, 128)
    got = lax.all_to_all(send, ("facet", "rows"), split_axis=0, concat_axis=0, tiled=True)
    got = got.reshape(64, 2, 24, 128)
    resid_got = got[:, :, :16].reshape(64, 2, ERANK, 2, 512).transpose(2, 3, 0, 1, 4).reshape(ERANK, 2, 64, 1024)
    nodes_got = (got[:, 0, 16:] + got[:, 1, 16:]).reshape(64, RANK, 256).transpose(1, 0, 2).reshape(256, 256)

    return pl.pallas_call(
        _rows_kernel,
        out_shape=jax.ShapeDtypeStruct((1, 2, 512, 1024), f32),
        scratch_shapes=[pltpu.VMEM((1536, 2048), bf16), pltpu.VMEM((1024, 1536), bf16)],
        compiler_params=pltpu.CompilerParams(**params),
        cost_estimate=pl.CostEstimate(flops=7 * 10**9, bytes_accessed=12 * 10**6, transcendentals=0),
        name="row_transform",
    )(
        nodes_got, resid_got, tab_c, tab_s, band_window.reshape(1, M), left,
        jnp.asarray(tables["weave_hi"]), jnp.asarray(tables["weave_lo"]),
    )


def solution(mesh):
    return jax.shard_map(
        per_device,
        mesh=mesh,
        in_specs=(P("facet", None, "rows", None), P(), P(), P(), P(), P(), P()),
        out_specs=P("facet", None, "rows", None),
        check_vma=False,
    )
```

time: 440 us -> 102 us (0.23); the launches traced: 434 us -> 101 us
  other arithmetic: 150 us -> 10.8 us
  matrix products: 106 us -> 0 us
  Pallas kernels: 0 us -> 45.1 us
  blocking collectives: 45.1 us -> 0 us
  local copies, waits for them, and re-layouts: 56.4 us -> 16.7 us
  waiting for transfers between devices: 51.6 us -> 15.7 us
  between operations: 14.5 us -> 0.23 us
  starting transfers between devices: 0.04 us -> 12.4 us
  loops' own time: 10.6 us -> 0 us
    dot_general x18 -> x0, matrix products: 106 us -> none  [the longest x16 91.8 us: add_block(): part = jnp.dot(left, table, preferred_element_type=jnp.float32)]
    all_gather x1 -> x0, waiting for transfers between devices: 51.6 us -> none  [per_device(): lax.all_gather(lax.all_to_all(contrib, 'facet', split_axis=0, concat_axis...]
    add x17 -> x2, other arithmetic: 48.3 us -> 0.72 us  [the longest x1 0.7 us: per_device(): turn = _angle((2 * row_off + 7)[None, :] * (own_subrow + q)[:, None])]
    pallas_call x0 -> x3, Pallas kernels: none -> 45.1 us  [the longest x1 16.6 us: per_device(): pl.pallas_call(_exact_kernel, grid=(16,), in_specs=[pl.BlockSpec((8, BLOC...]
    all_to_all x1 -> x0, blocking collectives: 39.2 us -> none  [per_device(): lax.all_to_all(contrib, 'facet', split_axis=0, concat_axis=0, tiled=True)]
    convert_element_type x2 -> x1, other arithmetic: 30.7 us -> 0.02 us  [per_device(): jnp.stack([to_re, to_im], 0).transpose(0, 2, 1, 3, 4, 5).reshape(256, 16)]
    cos x18 -> x0, other arithmetic: 25.8 us -> none  [the longest x1 18.4 us: per_device(): cosine = jnp.cos(angle)[:, None, :]]
    convert_element_type x2 -> x3, local copies, waits for them, and re-layouts: 25.1 us -> 0.83 us  [per_device(): jnp.stack([to_re, to_im], 0).transpose(0, 2, 1, 3, 4, 5).reshape(256, 16)]
  transfers between devices with their start and end apart: 1 -> 2, of which waited for: 1 -> 1; matrix products, arithmetic and copies ran while one was open for 2% -> 18% of each run, Pallas kernels for 0% -> 16%
where the time goes in v1:
time: 102 us; the launch traced here: 101 us
  Pallas kernels  45.1 us (44%)
  local copies, waits for them, and re-layouts  16.7 us (16%)
  waiting for transfers between devices  15.7 us (15%)
  starting transfers between devices  12.4 us (12%)
  other arithmetic  10.8 us (11%)
    pallas_call x1, Pallas kernels, per_device(): pl.pallas_call(_exact_kernel, grid=(16,), in_specs=[pl.BlockSpec((8, BLOC...  16.6 us
    pallas_call x1, Pallas kernels, per_device(): pl.pallas_call(_resid_kernel, grid_spec=pltpu.PrefetchScalarGridSpec(num_...  15.7 us
    all_to_all x1, waiting for transfers between devices, per_device(): lax.all_to_all(send, ('facet', 'rows'), split_axis=0, concat_axis=0, tile...  15.7 us
    pallas_call x1, Pallas kernels, per_device(): pl.pallas_call(_rows_kernel, out_shape=jax.ShapeDtypeStruct((1, 2, 512, 1...  12.8 us
    all_to_all x1, starting transfers between devices, per_device(): lax.all_to_all(send, ('facet', 'rows'), split_axis=0, concat_axis=0, tile...  7.94 us
    ppermute x1, starting transfers between devices, per_device(): peer = lax.ppermute(own, 'rows', [(0, 1), (1, 0)])  4.51 us
    concatenate x1, local copies, waits for them, and re-layouts, per_device(): jnp.concatenate([c, -g * s, -g2 * c, g3 * s, s, g * c, -g2 * s, -g3 * c], 1)  4.33 us
    mul x1, other arithmetic, per_device(): -g3 * c  3.56 us
  transfers between devices with their start and end apart: 2, of which 1 were waited for; matrix products, arithmetic and copies ran while one was open for 18% of the time, Pallas kernels for 16%

profile of v1, /device:TPU:1, one launch (start us, length us, event | category | flops | bytes accessed | tf_op | source)
XLA Modules:
  0.0 100.9 jit_solution(1097127905300551253)
XLA Ops:
  0.0 1.2 %reshape.216.own_ref.data_ref = f32[8,16384]{1,0:T(8,128)S(1)} reshape(f32[1,2,4,16384]{3,2,1,0:T(4,128)} %param.13) | data formatting | bytes 1048576 | tf_op jit(solution)/shard_map/reshape | solution.py:276
  1.2 4.5 %collective-permute-start = (f32[8,16384]{1,0:T(8,128)S(1)}, f32[8,16384]{1,0:T(8,128)S(1)}, u32[]{:S(2)}, u32[]{:S(2)}) collective-permute-start(f32[8,16384]{1,0:T(8,128)S(1)} %reshape.216.own_ref.data_ref), channel_id=1, source_target_pairs={{0,1},{1,0},{2,3},{3,2},{4,5},{5,4},{6,7},{7,6},{8,9},{9,8},{10,11... | collective-permute-start | bytes 1572872 | tf_op jit(solution)/shard_map/ppermute | solution.py:278
  5.8 0.8 slice_bitcast_fusion.1
  6.6 0.8 select_reduce_fusion
  7.4 0.6 fusion.12
  8.6 1.4 %fusion.13 = (s32[]{:T(128)}, s32[64]{0:T(128)S(1)}) fusion(s32[64]{0:T(128)} %param.19, s32[]{:T(128)S(6)} %axis_index.25), kind=kLoop, calls=%fused_computation.56 | loop fusion | flops 255 | bytes 520 | tf_op jit(solution)/shard_map/reduce_sum | solution.py:285
  10.2 0.7 broadcast_multiply_fusion.8
  11.0 0.7 broadcast_multiply_fusion.6
  11.7 0.7 broadcast_multiply_fusion.9
  13.8 0.7 copy.31.combine_ref
  14.5 16.6 %exact_part.1 = f32[64,1024]{1,0:T(8,128)} custom-call(f32[8,16384]{1,0:T(8,128)} %copy-done, f32[1,16384]{1,0:T(1,128)} %bitcast.47, f32[64,512]{1,0:T(8,128)} %copy-done.2, f32[64,512]{1,0:T(8,128)} %copy-done.1, bf16[4096,128]{1,0:T(8,128)(2,1)} %constant.108.clone.sample_ref), custom_call_target="tpu_custom_call" | custom-call | flops 8000000000 | bytes 2000000 | tf_op jit(solution)/shard_map/exact_part/pallas_call | solution.py:327
  31.1 1.0 copy.36
  32.2 0.8 copy-done.3
  32.9 15.7 %residual_part.1 = f32[2,128,512]{2,1,0:T(8,128)} custom-call(s32[1]{0:T(128)} %bitcast.half_ref, f32[8,16384]{1,0:T(8,128)} %copy-done, f32[8,16384]{1,0:T(8,128)} %copy-done.3, f32[1,16384]{1,0:T(1,128)} %bitcast.48, f32[64,512]{1,0:T(8,128)} %copy-done.2, f32[64,512]{1,0:T(8,128)} %copy-done.1, bf16[256,16]{1,0:T(8,128)(2,1)} %copy.31.combine_ref, ...), custom_call_target="tpu_custom_call" | custom-call | flops 8999999488 | bytes 4000000 | tf_op jit(solution)/shard_map/residual_part/pallas_call | solution.py:349
  48.7 1.4 %copy.38 = f32[2,2,64,512]{3,0,1,2:T(2,128)S(1)} copy(f32[2,2,64,512]{3,2,1,0:T(8,128)} %bitcast.41) | data formatting | bytes 1048576 | tf_op jit(solution)/shard_map/reshape | solution.py:383
  50.6 1.2 %broadcast_in_dim.79 = f32[64,2,24,128]{3,2,1,0:T(8,128)} broadcast(f32[64,24,128]{2,1,0:T(8,128)S(1)} %pad_maximum_fusion), dimensions={0,2,3} | broadcast | bytes 2359296 | tf_op jit(solution)/shard_map/broadcast_in_dim | solution.py:388
  51.9 7.9 %all-to-all-start = ((f32[128,24,128]{2,1,0:T(8,128)}), f32[128,24,128]{2,1,0:T(8,128)S(1)}, u32[]{:S(2)}, u32[]{:S(2)}) async-start(f32[128,24,128]{2,1,0:T(8,128)} %bitcast.12), calls=%async_computation | async-start | bytes 3145728 | tf_op jit(solution)/shard_map/all_to_all | solution.py:389
  59.8 0.7 fusion.8
  60.6 3.6 %broadcast_multiply_fusion = (f32[1024,64]{1,0:T(8,128)S(1)}, f32[1024,64]{1,0:T(8,128)S(1)}, f32[1024,64]{1,0:T(8,128)S(1)}, f32[1024,64]{1,0:T(8,128)}, f32[10...) fusion(f32[1024]{0:T(1024)S(1)} %fusion.11, s32[1024]{0:T(1024)S(1)} %fusion.8, ...), kind=kLoop, calls=%fused_computation.6 | loop fusion | flops 786432 | bytes 2121984 | tf_op jit(solution)/shard_map/mul | solution.py:322
  64.1 4.3 %concatenate.19.left_ref = f32[1024,512]{1,0:T(8,128)} concatenate(f32[1024,64]{1,0:T(8,128)} %get-tuple-element.18, f32[1024,64]{1,0:T(8,128)S(1)} %get-tuple-element.12, f32[1024,64]{1,0:T(8,128)} %get-tuple-element.14, f32[1024,64]{1,0:T(8,128)S(1)} %get-tuple-element.13, f32[1024,64]{1,0:T(8,128)} %get-tuple-element.17, f32[1024,64]{1,0:T(8,128)} %get-tuple-element.16, ...), dimensions={1} | concatenate | bytes 4194304 | tf_op jit(solution)/shard_map/concatenate | solution.py:322
  68.5 15.7 %all-to-all-done = f32[128,24,128]{2,1,0:T(8,128)S(1)} async-done(((f32[128,24,128]{2,1,0:T(8,128)}), f32[128,24,128]{2,1,0:T(8,128)S(1)}, u32[]{:S(2)}, u32[]{:S(2)}) %all-to-all-start) | async-done | bytes 1572896 | tf_op jit(solution)/shard_map/all_to_all | solution.py:389
  85.4 1.9 %reshape.226.resid_ref = f32[2,2,64,1024]{3,2,1,0:T(8,128)} reshape(f32[2,2,64,2,512]{4,3,2,1,0:T(2,128)S(1)} %copy.34) | data formatting | bytes 2097152 | tf_op jit(solution)/shard_map/reshape | solution.py:391
  87.4 0.7 copy.33
  88.2 12.8 %row_transform.1 = f32[1,2,512,1024]{3,2,1,0:T(8,128)} custom-call(f32[256,256]{1,0:T(8,128)} %bitcast.42, f32[2,2,64,1024]{3,2,1,0:T(8,128)} %reshape.226.resid_ref, f32[64,512]{1,0:T(8,128)} %copy-done.2, f32[64,512]{1,0:T(8,128)} %copy-done.1, f32[1,1024]{1,0:T(1,128)} %bitcast.49, f32[1024,512]{1,0:T(8,128)} %concatenate.19.left_ref, ...), custom_call_target="tpu_custom_call" | custom-call | flops 7000000000 | bytes 12000000 | tf_op jit(solution)/shard_map/row_transform/pallas_call | solution.py:394
  (46 shorter events, 4.0 us)
Async XLA Ops:
  1.2 13.3 %copy-start = (f32[8,16384]{1,0:T(8,128)}, f32[8,16384]{1,0:T(8,128)S(1)}, u32[]{:S(2)}) copy-start(f32[8,16384]{1,0:T(8,128)S(1)} %reshape.216.own_ref.data_ref) | copy-start | bytes 1572868
  1.2 30.9 %collective-permute-start = (f32[8,16384]{1,0:T(8,128)S(1)}, f32[8,16384]{1,0:T(8,128)S(1)}, u32[]{:S(2)}, u32[]{:S(2)}) collective-permute-start(f32[8,16384]{1,0:T(8,128)S(1)} %reshape.216.own_ref.data_ref), channel_id=1, source_target_pairs={{0,1},{1,0},{2,3},{3,2},{4,5},{5,4},{6,7},{7,6},{8,9},{9,8},{10,11... | collective-permute-start | bytes 1572872 | tf_op jit(solution)/shard_map/ppermute | solution.py:278
  13.1 1.4 %copy-start.1 = (f32[64,512]{1,0:T(8,128)}, f32[64,512]{1,0:T(8,128)S(1)}, u32[]{:S(2)}) copy-start(f32[64,512]{1,0:T(8,128)S(1)} %get-tuple-element.7.sin_ref) | copy-start | bytes 393220
  13.1 1.4 %copy-start.2 = (f32[64,512]{1,0:T(8,128)}, f32[64,512]{1,0:T(8,128)S(1)}, u32[]{:S(2)}) copy-start(f32[64,512]{1,0:T(8,128)S(1)} %get-tuple-element.8.cos_ref) | copy-start | bytes 393220
  32.1 0.8 copy-start.3
  51.9 32.3 %all-to-all-start = ((f32[128,24,128]{2,1,0:T(8,128)}), f32[128,24,128]{2,1,0:T(8,128)S(1)}, u32[]{:S(2)}, u32[]{:S(2)}) async-start(f32[128,24,128]{2,1,0:T(8,128)} %bitcast.12), calls=%async_computation | async-start | bytes 3145728 | tf_op jit(solution)/shard_map/all_to_all | solution.py:389

commit v2 on v0

v2 whole, which is shorter than its diff:
```python
import functools
import math

import jax
import jax.numpy as jnp
import ml_dtypes
import numpy as np
from jax import lax
from jax.experimental import pallas as pl
from jax.experimental.pallas import tpu as pltpu
from jax.sharding import PartitionSpec as P

NIMG = 262144
M = 1024
SUBROWS = 1024
TWO_PI = 2.0 * math.pi

BLOCK = 1024
SPAN = 4096
NODES = 32
RANK = 4
ERANK = 2
ROW_SCALE = 4.0

f32 = jnp.float32
bf16 = jnp.bfloat16


def _split(values):
    high = values.astype(np.float32).astype(ml_dtypes.bfloat16)
    low = (values - high.astype(np.float64)).astype(np.float32).astype(ml_dtypes.bfloat16)
    return high, low


def _kernel_sum(x, count):
    den = np.sin(np.pi * x / NIMG)
    zero = np.abs(den) < 1e-14
    return np.where(zero, float(count), np.sin(np.pi * x * count / NIMG) / np.where(zero, 1.0, den))


def _solve(gram, right):
    gram, right = gram.copy(), right.copy()
    n = len(gram)
    for i in range(n):
        for j in range(i + 1, n):
            factor = gram[j, i] / gram[i, i]
            gram[j] = gram[j] - factor * gram[i]
            right[j] = right[j] - factor * right[i]
    out = np.zeros_like(right)
    for i in range(n - 1, -1, -1):
        total = right[i].copy()
        for j in range(i + 1, n):
            total = total - gram[i, j] * out[j]
        out[i] = total / gram[i, i]
    return out


@functools.lru_cache(maxsize=None)
def _tables():
    scale = TWO_PI / NIMG
    bands = np.arange(M)
    product = (np.arange(BLOCK)[:, None] * bands[None, :]) % NIMG
    angle = (np.float32(scale) * product.astype(np.float32)).astype(np.float64)
    exact = scale * product
    resid_c = np.cos(angle).astype(np.float32).astype(ml_dtypes.bfloat16).astype(np.float64) - np.cos(exact)
    resid_s = np.sin(angle).astype(np.float32).astype(ml_dtypes.bfloat16).astype(np.float64) - np.sin(exact)
    half = M // 2
    resid = np.stack(
        [np.concatenate([resid_c[:, h * half:(h + 1) * half], resid_s[:, h * half:(h + 1) * half]], 1) for h in range(2)]
    ).astype(np.float32).astype(ml_dtypes.bfloat16)
    i = np.arange(NODES)
    nodes = 511.5 + 512 * 1.05 * (0.25 * ((2 * i + 1) / NODES - 1) - 0.75 * np.cos(np.pi * (i + 0.5) / NODES))
    gram = _kernel_sum(nodes[:, None] - nodes[None, :], SPAN) + 1e-13 * SPAN * np.eye(NODES)
    interp = _solve(gram, _kernel_sum(nodes[:, None] - bands[None, :], SPAN))
    centre = (SPAN - 1) / 2
    at = scale * (np.arange(SPAN) - centre)[:, None] * nodes[None, :]
    sample = np.concatenate([np.cos(at), -np.sin(at)], 1)
    sample = np.concatenate(_split(sample), 1)
    rows = []
    for span in range(16384 // SPAN):
        turn = scale * (span * SPAN + centre) * bands
        re, im = interp * np.cos(turn), -interp * np.sin(turn)
        rows.append(np.concatenate([re, im], 1))
        rows.append(np.concatenate([-im, re], 1))
    weave = np.concatenate(rows, 0)
    weave_hi, weave_lo = _split(weave)
    turn = TWO_PI * ((np.arange(16)[:, None] * (bands[None, :half] % 256)) % 256) / 256
    return dict(
        resid=resid, sample=sample, weave_hi=weave_hi, weave_lo=weave_lo,
        turn_c=np.cos(turn).astype(np.float32), turn_s=np.sin(turn).astype(np.float32),
    )


COL_A, COL_SC8, COL_CF8, COL_ROW = 0, 16, 24, 32
CHUNKS = 24


def _angle(product):
    turns = lax.bitwise_and(product + NIMG, 2 * NIMG - 1) - NIMG
    return turns.astype(f32) * (math.pi / NIMG)


def _offset_row(order_ref, offsets_ref, which):
    slots = lax.broadcasted_iota(jnp.int32, (64, 64), 0)
    offsets = offsets_ref[:, which:which + 1].astype(f32)
    return jnp.sum(jnp.where(slots == order_ref[...], offsets, 0.0), axis=0, keepdims=True)


def _to_column(row):
    at = lax.broadcasted_iota(jnp.int32, (64, 64), 0) == lax.broadcasted_iota(jnp.int32, (64, 64), 1)
    return jnp.sum(jnp.where(at, row, 0.0), axis=1, keepdims=True)


def _pick(row, index):
    lane = lax.broadcasted_iota(jnp.int32, row.shape, 1)
    return jnp.sum(jnp.where(lane == index, row, 0.0), axis=1, keepdims=True)


def _prepare_kernel(where_ref, order_ref, offsets_ref, cols_ref, rows_ref, band_ref,
                    lc_ref, ls_ref, pc_ref, ps_ref, mc_ref, ms_ref, wc_ref, ws_ref, combine_ref):
    slot, half = where_ref[0], where_ref[1]
    cf_row = _offset_row(order_ref, offsets_ref, 0)
    own_cf = _pick(cf_row, slot).astype(jnp.int32)
    cf = _to_column(cf_row).astype(jnp.int32)
    sc = _to_column(cols_ref[...].astype(f32)).astype(jnp.int32)
    sr = _to_column(rows_ref[...].astype(f32)).astype(jnp.int32)
    lane = lax.broadcasted_iota(jnp.int32, (64, 128), 1)
    row = lax.bitwise_and(4 * half + 4 * lax.bitwise_and(lane // 8, 1) + lax.bitwise_and(lane, 3), 7)
    odd = 2 * row - 7
    factor = jnp.where(
        lane < COL_SC8, 2 * (own_cf + 1024 * lane),
        jnp.where(lane < COL_CF8, 256 * (lane - COL_SC8), jnp.where(lane < COL_ROW, 256 * (lane - COL_CF8), odd)),
    )
    other = jnp.where(lane < COL_CF8, sc, jnp.where(lane < COL_ROW, cf, sr + 512))
    angle = _angle(factor * other)
    mc, ms = jnp.cos(angle), jnp.sin(angle)
    mc_ref[...] = mc
    ms_ref[...] = ms
    angle = _angle(2 * lane * sc)
    low_c, low_s = jnp.cos(angle), jnp.sin(angle)
    for i in range(8):
        c, s = mc[:, COL_SC8 + i:COL_SC8 + i + 1], ms[:, COL_SC8 + i:COL_SC8 + i + 1]
        lc_ref[:, i * 128:(i + 1) * 128] = c * low_c - s * low_s
        ls_ref[:, i * 128:(i + 1) * 128] = s * low_c + c * low_s
    angle = _angle(2 * lane * cf)
    low_c, low_s = jnp.cos(angle), jnp.sin(angle)
    for i in range(8):
        c, s = mc[:, COL_CF8 + i:COL_CF8 + i + 1], ms[:, COL_CF8 + i:COL_CF8 + i + 1]
        band = band_ref[:, i * 128:(i + 1) * 128]
        pc_ref[:, i * 128:(i + 1) * 128] = (c * low_c - s * low_s) * band
        ps_ref[:, i * 128:(i + 1) * 128] = (s * low_c + c * low_s) * band
    rho = odd.astype(f32) * (0.5 / ROW_SCALE)
    power = jnp.ones((64, 128), f32)
    first = lax.bitwise_and(lane, 4) == 0
    to_re, to_im = jnp.where(first, mc, ms), jnp.where(first, -ms, mc)
    for n in range(RANK):
        wc_ref[n] = mc * power
        ws_ref[n] = ms * power
        if n < ERANK:
            for part, value in ((0, to_re), (1, to_im)):
                base = part * 128 + n * 64
                combine_ref[base:base + 64, :] = (value * power)[:, COL_ROW:COL_ROW + 16].astype(bf16)
        power = power * rho


def _exact_kernel(data_ref, window_ref, lc_ref, ls_ref, mc_ref, ms_ref, wc_ref, ws_ref, sample_ref, out_ref,
                  even_ref, odd_ref, acc_ref):
    def build(block, x_ref):
        bc, bs = _pick(mc_ref[...], block), _pick(ms_ref[...], block)
        for i in range(4):
            cols = slice(i * 256, (i + 1) * 256)
            here = pl.ds(pl.multiple_of(block * BLOCK + i * 256, 256), 256)
            window = window_ref[:, here]
            re_rows = data_ref[0, 0, :, here] * window
            im_rows = data_ref[0, 1, :, here] * window
            for g in range(4):
                rows = slice(g * 16, (g + 1) * 16)
                lc, ls = lc_ref[rows, cols], ls_ref[rows, cols]
                c, s = bc[rows], bs[rows]
                ec = c * lc - s * ls
                es = s * lc + c * ls
                for r in range(4):
                    dr, di = re_rows[r:r + 1], im_rows[r:r + 1]
                    at = r * 64 + g * 16
                    x_ref[at:at + 16, cols] = (dr * ec + di * es).astype(bf16)
                    x_ref[256 + at:256 + at + 16, cols] = (di * ec - dr * es).astype(bf16)

    def add(block, x_ref):
        rows = pl.ds(pl.multiple_of((block % 4) * BLOCK, BLOCK), BLOCK)
        part = jnp.dot(x_ref[...], sample_ref[rows, :], preferred_element_type=f32)
        acc_ref[block // 4] = acc_ref[block // 4] + part

    acc_ref[...] = jnp.zeros_like(acc_ref)
    build(0, even_ref)

    def body(pair, carry):
        add(2 * pair, even_ref)
        build(2 * pair + 1, odd_ref)
        add(2 * pair + 1, odd_ref)
        build((2 * pair + 2) % 16, even_ref)
        return carry

    lax.fori_loop(0, 8, body, 0)

    lane = lax.broadcasted_iota(jnp.int32, (64, 128), 1)
    sign = jnp.where(lax.bitwise_and(lane, 32) == 0, -1.0, 1.0).astype(f32)
    sums = [[None] * 4 for _ in range(RANK)]
    for span in range(4):
        for r in range(4):
            re = acc_ref[span, r * 64:(r + 1) * 64]
            im = acc_ref[span, 256 + r * 64:256 + (r + 1) * 64]
            re = re + pltpu.roll(re, 64, 1)
            im = im + pltpu.roll(im, 64, 1)
            value = re + sign * pltpu.roll(im, 32, 1)
            turned = sign * pltpu.roll(value, 32, 1)
            for n in range(RANK):
                col = slice(COL_ROW + r, COL_ROW + r + 1)
                term = wc_ref[n, :, col] * value - ws_ref[n, :, col] * turned
                sums[n][span] = term if sums[n][span] is None else sums[n][span] + term
    for n in range(RANK):
        out_ref[:, n * 256:n * 256 + 128] = jnp.where(lane < 64, sums[n][0], sums[n][1])
        out_ref[:, n * 256 + 128:n * 256 + 256] = jnp.where(lane < 64, sums[n][2], sums[n][3])


def _residual_kernel(half_ref, own_ref, peer_ref, window_ref, lc_ref, ls_ref, mc_ref, ms_ref, combine_ref, table_ref,
                     tc_ref, ts_ref, nodes_ref, out_ref, even_ref, odd_ref, sum_ref):
    def build(group, z_ref):
        for j in range(4):
            block = group * 4 + j
            bc, bs = _pick(mc_ref[...], block), _pick(ms_ref[...], block)
            for i in range(4):
                cols = slice(i * 256, (i + 1) * 256)
                here = pl.ds(pl.multiple_of(block * BLOCK + i * 256, 256), 256)
                window = window_ref[:, here]
                data = jnp.concatenate(
                    [own_ref[0, 0, :, here], own_ref[0, 1, :, here], peer_ref[0, 0, :, here], peer_ref[0, 1, :, here]], 0
                )
                data = (data * window).astype(bf16)
                rows = jnp.dot(combine_ref[...], data, preferred_element_type=f32)
                lc, ls = lc_ref[:, cols], ls_ref[:, cols]
                ec = bc * lc - bs * ls
                es = bs * lc + bc * ls
                for n in range(ERANK):
                    gr, gi = rows[n * 64:(n + 1) * 64], rows[128 + n * 64:128 + (n + 1) * 64]
                    at = j * 256 + n * 64
                    z_ref[at:at + 64, cols] = (gr * ec + gi * es).astype(bf16)
                    z_ref[at + 128:at + 192, cols] = (gi * ec - gr * es).astype(bf16)

    def add(group, z_ref):
        for kc in range(2):
            cols = slice(kc * 256, (kc + 1) * 256)
            by_c = jnp.dot(z_ref[...], table_ref[0, :, cols], preferred_element_type=f32)
            by_s = jnp.dot(z_ref[...], table_ref[0, :, 512 + kc * 256:768 + kc * 256], preferred_element_type=f32)
            sum_re, sum_im = sum_ref[0, :, cols], sum_ref[1, :, cols]
            for j in range(4):
                re = by_c[j * 256:j * 256 + 128] + by_s[j * 256 + 128:j * 256 + 256]
                im = by_c[j * 256 + 128:j * 256 + 256] - by_s[j * 256:j * 256 + 128]
                tc = tc_ref[pl.ds(group * 4 + j, 1), cols]
                ts = ts_ref[pl.ds(group * 4 + j, 1), cols]
                sum_re = sum_re + (re * tc + im * ts)
                sum_im = sum_im + (im * tc - re * ts)
            sum_ref[0, :, cols] = sum_re
            sum_ref[1, :, cols] = sum_im

    sum_ref[...] = jnp.zeros_like(sum_ref)
    build(0, even_ref)

    def body(pair, carry):
        add(2 * pair, even_ref)
        build(2 * pair + 1, odd_ref)
        add(2 * pair + 1, odd_ref)
        build((2 * pair + 2) % 4, even_ref)
        return carry

    lax.fori_loop(0, 2, body, 0)

    for copy in range(2):
        for n in range(ERANK):
            for part in range(2):
                for kc in range(4):
                    at = copy * CHUNKS + n * 8 + part * 4 + kc
                    out_ref[pl.ds(at, 64, stride=2 * CHUNKS), :] = (
                        sum_ref[part, n * 64:(n + 1) * 64, kc * 128:(kc + 1) * 128]
                    )
        for i in range(8):
            out_ref[pl.ds(copy * CHUNKS + 16 + i, 64, stride=2 * CHUNKS), :] = nodes_ref[:, i * 128:(i + 1) * 128]


def _halves(value):
    high = value.astype(bf16)
    return high, (value - high.astype(f32)).astype(bf16)


def _phase_kernel(where_ref, order_ref, offsets_ref, rows_ref, out_ref):
    slot, half = where_ref[0], where_ref[1]
    rf = _offset_row(order_ref, offsets_ref, 1).astype(jnp.int32)
    own_sr = _pick(rows_ref[...].astype(f32), slot).astype(jnp.int32)
    odd = jnp.concatenate([2 * rf + 7, 2 * rf + 7], 1)
    lane = lax.broadcasted_iota(jnp.int32, (128, 128), 1)
    quarter = jnp.where(lane < 64, 0, -(NIMG // 2))
    sign = jnp.where(lane < 64, -1.0, 1.0).astype(f32)
    for i in range(8):
        here = slice(i * 128, (i + 1) * 128)
        q = lax.broadcasted_iota(jnp.int32, (128, 128), 0) + i * 128 + half * 512
        q = lax.bitwise_and(q, 1023)
        turn = jnp.cos(_angle(odd * (own_sr + q) + quarter))
        other = sign * pltpu.roll(turn, 64, 1)
        g = (q - 512).astype(f32) * (TWO_PI / NIMG * ROW_SCALE)
        g2, g3 = g * g * 0.5, g * g * g * (1.0 / 6.0)
        for n, value in ((0, turn), (1, g * other)):
            high, low = _halves(value)
            out_ref[here, n * 128:(n + 1) * 128] = high
            out_ref[here, 256 + n * 128:256 + (n + 1) * 128] = high
            out_ref[here, 512 + n * 128:512 + (n + 1) * 128] = low
        out_ref[here, 768:896] = (-g2 * turn).astype(bf16)
        out_ref[here, 896:1024] = (-g3 * other).astype(bf16)


def _rows_kernel(got_ref, pc_ref, ps_ref, left_ref, wh_ref, wl_ref, out_ref, right_ref, high_ref, low_ref):
    for n in range(RANK):
        for i in range(2):
            chunk = 16 + n * 2 + i
            value = (
                got_ref[pl.ds(chunk, 64, stride=2 * CHUNKS), :]
                + got_ref[pl.ds(CHUNKS + chunk, 64, stride=2 * CHUNKS), :]
            )
            high, low = _halves(value)
            high_ref[n * 64:(n + 1) * 64, i * 128:(i + 1) * 128] = high
            if n < 2:
                low_ref[n * 64:(n + 1) * 64, i * 128:(i + 1) * 128] = low
    for i in range(4):
        cols = slice(i * 256, (i + 1) * 256)
        vals = []
        for part in range(2):
            wcols = slice(part * 1024 + i * 256, part * 1024 + (i + 1) * 256)
            wh, wl = wh_ref[:, wcols], wl_ref[:, wcols]
            main = jnp.dot(high_ref[...], wh, preferred_element_type=f32)
            rest = (
                jnp.dot(high_ref[0:128], wl, preferred_element_type=f32)
                + jnp.dot(low_ref[...], wh, preferred_element_type=f32)
            )
            vals.append((main, rest))
        pc, ps = pc_ref[:, cols], ps_ref[:, cols]
        for n in range(RANK):
            rows = slice(n * 64, (n + 1) * 64)
            vr, vi = vals[0][0][rows], vals[1][0][rows]
            if n < ERANK:
                parts = []
                for part in range(2):
                    at = (i // 2) * CHUNKS + n * 8 + part * 4 + 2 * (i % 2)
                    parts.append(jnp.concatenate(
                        [got_ref[pl.ds(at + m, 64, stride=2 * CHUNKS), :] for m in range(2)], 1))
                vr = vr + vals[0][1][rows] + parts[0]
                vi = vi + vals[1][1][rows] + parts[1]
            cr = vr * pc + vi * ps
            ci = vi * pc - vr * ps
            for value, part, col in ((cr, 0, 0), (ci, 1, 0), (ci, 0, 1024), (-cr, 1, 1024)):
                ccols = slice(col + i * 256, col + (i + 1) * 256)
                at = n * 128 + part * 64
                if n < 2:
                    high, low = _halves(value)
                    right_ref[at:at + 64, ccols] = high
                    right_ref[256 + at:256 + at + 64, ccols] = low
                    right_ref[512 + at:512 + at + 64, ccols] = high
                else:
                    right_ref[512 + at:512 + at + 64, ccols] = value.astype(bf16)

    total = jnp.zeros((8, 512), f32)
    for part in range(2):
        for i in range(2):
            cols = slice(part * 1024 + i * 512, part * 1024 + (i + 1) * 512)
            result = jnp.dot(left_ref[...], right_ref[:, cols], preferred_element_type=f32)
            out_ref[0, part, :, i * 512:(i + 1) * 512] = result[:512]
            total = total + jnp.sum((result * result).reshape(128, 8, 512), 0)
    mean = jnp.sum(total) / (2.0 * SUBROWS * M)
    factor = lax.rsqrt(jnp.full((8, 128), mean, f32) + 1e-06)[0:1, 0:1]
    for part in range(2):
        out_ref[0, part] = out_ref[0, part] * factor


def per_device(facets, facet_window, band_window, facet_order, facet_offsets, sub_cols, sub_rows):
    tables = _tables()
    peer = lax.ppermute(facets, "rows", [(0, 1), (1, 0)])
    where = jnp.stack([lax.axis_index("facet"), lax.axis_index("rows")]).astype(jnp.int32)
    order, cols, rows = (v.reshape(1, 64) for v in (facet_order, sub_cols, sub_rows))
    window = facet_window.reshape(1, 16384)
    scalars = pl.BlockSpec(memory_space=pltpu.SMEM)
    vmem = pl.BlockSpec(memory_space=pltpu.VMEM)
    shape = jax.ShapeDtypeStruct

    def params(mib):
        return pltpu.CompilerParams(vmem_limit_bytes=mib * 1024 * 1024)

    wide, narrow = shape((64, 1024), f32), shape((64, 128), f32)
    lc, ls, pc, ps, mc, ms, wc, ws, combine = pl.pallas_call(
        _prepare_kernel,
        in_specs=[scalars] + [vmem] * 5,
        out_shape=[wide, wide, wide, wide, narrow, narrow, shape((RANK, 64, 128), f32), shape((RANK, 64, 128), f32),
                   shape((256, 16), bf16)],
        compiler_params=params(16),
        cost_estimate=pl.CostEstimate(flops=10**6, bytes_accessed=10**6, transcendentals=5 * 10**4),
        name="prepare",
    )(where, order, facet_offsets, cols, rows, band_window.reshape(1, M))

    nodes = pl.pallas_call(
        _exact_kernel,
        in_specs=[vmem] * 9,
        out_shape=wide,
        scratch_shapes=[pltpu.VMEM((512, BLOCK), bf16), pltpu.VMEM((512, BLOCK), bf16), pltpu.VMEM((4, 512, 128), f32)],
        compiler_params=params(24),
        cost_estimate=pl.CostEstimate(flops=8 * 10**9, bytes_accessed=2 * 10**6, transcendentals=0),
        name="exact_part",
    )(facets, window, lc, ls, mc, ms, wc, ws, jnp.asarray(tables["sample"]))

    whole = lambda *sizes: pl.BlockSpec(sizes, lambda b, h: (0,) * len(sizes))
    send = pl.pallas_call(
        _residual_kernel,
        grid_spec=pltpu.PrefetchScalarGridSpec(
            num_scalar_prefetch=1,
            grid=(1,),
            in_specs=[
                whole(1, 2, 4, 16384), whole(1, 2, 4, 16384), whole(1, 16384),
                whole(64, 1024), whole(64, 1024), whole(64, 128), whole(64, 128), whole(256, 16),
                pl.BlockSpec((1, 1024, 1024), lambda b, h: (h[1], 0, 0)),
                whole(16, 512), whole(16, 512), whole(64, 1024),
            ],
            out_specs=whole(128 * CHUNKS, 128),
            scratch_shapes=[pltpu.VMEM((1024, 1024), bf16), pltpu.VMEM((1024, 1024), bf16),
                            pltpu.VMEM((2, 128, 512), f32)],
        ),
        out_shape=shape((128 * CHUNKS, 128), f32),
        compiler_params=params(48),
        cost_estimate=pl.CostEstimate(flops=9 * 10**9, bytes_accessed=4 * 10**6, transcendentals=0),
        name="residual_part",
    )(
        where, facets, peer, window, lc, ls, mc, ms, combine,
        jnp.asarray(tables["resid"]), jnp.asarray(tables["turn_c"]), jnp.asarray(tables["turn_s"]), nodes,
    )

    got = lax.all_to_all(send.reshape(128, CHUNKS, 128), ("facet", "rows"), split_axis=0, concat_axis=0, tiled=True)
    left = pl.pallas_call(
        _phase_kernel,
        in_specs=[scalars] + [vmem] * 3,
        out_shape=shape((1024, 1024), bf16),
        compiler_params=params(16),
        cost_estimate=pl.CostEstimate(flops=10**9, bytes_accessed=2 * 10**6, transcendentals=2 * 10**5),
        name="row_phases",
    )(where, order, facet_offsets, rows)

    return pl.pallas_call(
        _rows_kernel,
        in_specs=[vmem] * 6,
        out_shape=shape((1, 2, 512, 1024), f32),
        scratch_shapes=[pltpu.VMEM((1024, 2048), bf16), pltpu.VMEM((256, 256), bf16), pltpu.VMEM((128, 256), bf16)],
        compiler_params=params(40),
        cost_estimate=pl.CostEstimate(flops=5 * 10**9, bytes_accessed=12 * 10**6, transcendentals=0),
        name="row_transform",
    )(got.reshape(128 * CHUNKS, 128), pc, ps, left, jnp.asarray(tables["weave_hi"]), jnp.asarray(tables["weave_lo"]))


def solution(mesh):
    return jax.shard_map(
        per_device,
        mesh=mesh,
        in_specs=(P("facet", None, "rows", None), P(), P(), P(), P(), P(), P()),
        out_specs=P("facet", None, "rows", None),
        check_vma=False,
    )
```

time: 440 us -> 86.7 us (0.20); the launches traced: 434 us -> 86.2 us
  other arithmetic: 150 us -> 0.07 us
  matrix products: 106 us -> 0 us
  local copies, waits for them, and re-layouts: 56.4 us -> 10.7 us
  blocking collectives: 45.1 us -> 0 us
  Pallas kernels: 0 us -> 43.2 us
  waiting for transfers between devices: 51.6 us -> 19.7 us
  between operations: 14.5 us -> 0.12 us
  starting transfers between devices: 0.04 us -> 12.4 us
  loops' own time: 10.6 us -> 0 us
    dot_general x18 -> x0, matrix products: 106 us -> none  [the longest x16 91.8 us: add_block(): part = jnp.dot(left, table, preferred_element_type=jnp.float32)]
    all_gather x1 -> x0, waiting for transfers between devices: 51.6 us -> none  [per_device(): lax.all_gather(lax.all_to_all(contrib, 'facet', split_axis=0, concat_axis...]
    add x17 -> x0, other arithmetic: 48.3 us -> none  [the longest x16 48.2 us: add_block(): totals[1] + (part_im * pcos - part_re * psin)]
    pallas_call x0 -> x5, Pallas kernels: none -> 43.2 us  [the longest x1 19.1 us: per_device(): pl.pallas_call(_residual_kernel, grid_spec=pltpu.PrefetchScalarGridSpec(n...]
    all_to_all x1 -> x0, blocking collectives: 39.2 us -> none  [per_device(): lax.all_to_all(contrib, 'facet', split_axis=0, concat_axis=0, tiled=True)]
    convert_element_type x2 -> x0, other arithmetic: 30.7 us -> none  [the longest x1 19.9 us: per_device(): table_s = jnp.sin(tangle).astype(jnp.bfloat16)]
    cos x18 -> x0, other arithmetic: 25.8 us -> none  [the longest x1 18.4 us: per_device(): cosine = jnp.cos(angle)[:, None, :]]
    convert_element_type x2 -> x0, local copies, waits for them, and re-layouts: 25.1 us -> none  [the longest x1 12.6 us: per_device(): (real_in * cosine + imag_in * sine).astype(jnp.bfloat16).reshape(-1, width)]
  transfers between devices with their start and end apart: 1 -> 2, of which waited for: 1 -> 1; matrix products, arithmetic and copies ran while one was open for 2% -> 1% of each run, Pallas kernels for 0% -> 19%
where the time goes in v2:
time: 86.7 us; the launch traced here: 86.2 us
  Pallas kernels  43.2 us (50%)
  waiting for transfers between devices  19.7 us (23%)
  starting transfers between devices  12.4 us (14%)
  local copies, waits for them, and re-layouts  10.7 us (12%)
    all_to_all x1, waiting for transfers between devices, per_device(): lax.all_to_all(send.reshape(128, CHUNKS, 128), ('facet', 'rows'), split_a...  19.7 us
    pallas_call x1, Pallas kernels, per_device(): pl.pallas_call(_residual_kernel, grid_spec=pltpu.PrefetchScalarGridSpec(n...  19.1 us
    pallas_call x1, Pallas kernels, per_device(): pl.pallas_call(_exact_kernel, in_specs=[vmem] * 9, out_shape=wide, scratc...  11.4 us
    unnamed x35, local copies, waits for them, and re-layouts  10.7 us
    pallas_call x1, Pallas kernels, per_device(): pl.pallas_call(_rows_kernel, in_specs=[vmem] * 6, out_shape=shape((1, 2,...  8.16 us
    all_to_all x1, starting transfers between devices, per_device(): lax.all_to_all(send.reshape(128, CHUNKS, 128), ('facet', 'rows'), split_a...  7.93 us
    ppermute x1, starting transfers between devices, per_device(): peer = lax.ppermute(facets, 'rows', [(0, 1), (1, 0)])  4.43 us
    pallas_call x1, Pallas kernels, per_device(): pl.pallas_call(_phase_kernel, in_specs=[scalars] + [vmem] * 3, out_shape=...  3.21 us
  transfers between devices with their start and end apart: 2, of which 1 were waited for; matrix products, arithmetic and copies ran while one was open for 1% of the time, Pallas kernels for 19%

profile of v2, /device:TPU:1, one launch (start us, length us, event | category | flops | bytes accessed | tf_op | source)
XLA Modules:
  0.0 86.2 jit_solution(12695410026500079698)
XLA Ops:
  0.0 4.4 %collective-permute-start = (f32[1,2,4,16384]{3,2,1,0:T(4,128)}, f32[1,2,4,16384]{3,2,1,0:T(4,128)S(1)}, u32[]{:S(2)}, u32[]{:S(2)}) collective-permute-start(f32[1,2,4,16384]{3,2,1,0:T(4,128)} %own_ref.1), channel_id=1, source_target_pairs={{0,1},{1,0},{2,3},{3,2},{4,5},{5,4},{6,7},{7,6},{8,9},{9,8},{10,11... | collective-permute-start | bytes 1572872 | tf_op jit(solution)/shard_map/ppermute | solution.py:383
  4.4 0.8 copy.14.offsets_ref
  5.2 0.1 pad_add_fusion.where_ref.half_ref
  5.3 0.7 copy-done.4
  6.0 0.7 copy-done.5
  6.6 0.7 copy-done.6
  7.3 0.7 copy-done.8
  7.9 1.4 %prepare.1 = (f32[64,1024]{1,0:T(8,128)S(1)}, f32[64,1024]{1,0:T(8,128)S(1)}, f32[64,1024]{1,0:T(8,128)S(1)}, f32[64,1024]{1,0:T(8,128)S(1)}, f32[64,128]{1,0:T(...) custom-call(s32[2]{0:T(128)S(1)} %pad_add_fusion.where_ref.half_ref,, ...), custom_call_target="tpu_custom_call" | custom-call | flops 1000000 | bytes 1000000 | tf_op jit(solution)/shard_map/prepare/pallas_call | solution.py:395
  9.3 0.0 copy-start
  9.3 1.0 %copy-done = f32[1,2,4,16384]{3,2,1,0:T(4,128)S(1)} copy-done((f32[1,2,4,16384]{3,2,1,0:T(4,128)S(1)}, f32[1,2,4,16384]{3,2,1,0:T(4,128)}, u32[]{:S(2)}) %copy-start) | copy-done | bytes 524312
  10.3 0.8 copy-done.2
  11.2 1.2 %copy-done.12 = bf16[4096,128]{1,0:T(8,128)(2,1)S(1)} copy-done((bf16[4096,128]{1,0:T(8,128)(2,1)S(1)}, bf16[4096,128]{1,0:T(8,128)(2,1)}, u32[]{:S(2)}) %copy-start.12) | copy-done | bytes 1048600
  12.4 11.4 %exact_part.1.nodes_ref = f32[64,1024]{1,0:T(8,128)S(1)} custom-call(f32[1,2,4,16384]{3,2,1,0:T(4,128)S(1)} %copy-done, f32[1,16384]{1,0:T(1,128)S(1)} %bitcast.10, f32[64,1024]{1,0:T(8,128)S(1)} %get-tuple-element.14.lc_ref, f32[64,1024]{1,0:T(8,128)S(1)} %get-tuple-element.15.ls_ref, f32[64,128]{1,0:T(8,128)S(1)} %get-tuple-element.16.mc_ref, ...), custom_call_target="tpu_custom_call" | custom-call | flops 8000000000 | bytes 2000000 | tf_op jit(solution)/shard_map/exact_part/pallas_call | solution.py:405
  23.8 0.0 collective-permute-done.peer_ref
  23.9 19.1 %residual_part.1 = f32[3072,128]{1,0:T(8,128)} custom-call(s32[2]{0:T(128)S(1)} %pad_add_fusion.where_ref.half_ref, f32[1,2,4,16384]{3,2,1,0:T(4,128)S(1)} %copy-done.1, f32[1,2,4,16384]{3,2,1,0:T(4,128)S(1)} %collective-permute-done.peer_ref, f32[1,16384]{1,0:T(1,128)S(1)} %bitcast.11, f32[64,1024]{1,0:T(8,128)S(1)} %get-tuple-element.14.lc_ref, ...), custom_call_target="tpu_custom_call" | custom-call | flops 8999999488 | bytes 4000000 | tf_op jit(solution)/shard_map/residual_part/pallas_call | solution.py:416
  43.0 7.9 %all-to-all-start = ((f32[128,24,128]{2,1,0:T(8,128)}), f32[128,24,128]{2,1,0:T(8,128)S(1)}, u32[]{:S(2)}, u32[]{:S(2)}) async-start(f32[128,24,128]{2,1,0:T(8,128)} %bitcast.7), calls=%async_computation | async-start | bytes 3145728 | tf_op jit(solution)/shard_map/all_to_all | solution.py:440
  50.9 0.0 copy-start.10
  50.9 3.2 %row_phases.1.left_ref = bf16[1024,1024]{1,0:T(8,128)(2,1)S(1)} custom-call(s32[2]{0:T(128)S(1)} %pad_add_fusion.where_ref.half_ref, s32[1,64]{1,0:T(1,128)S(1)} %bitcast.15, s32[64,2]{1,0:T(8,128)S(1)} %copy.14.offsets_ref, s32[1,64]{1,0:T(1,128)S(1)} %bitcast.17), custom_call_target="tpu_custom_call" | custom-call | flops 1000000000 | bytes 2000000 | tf_op jit(solution)/shard_map/row_phases/pallas_call | solution.py:441
  54.2 0.0 copy-start.15
  54.2 1.3 %copy-done.15 = bf16[1024,1024]{1,0:T(8,128)(2,1)} copy-done((bf16[1024,1024]{1,0:T(8,128)(2,1)}, bf16[1024,1024]{1,0:T(8,128)(2,1)S(1)}, u32[]{:S(2)}) %copy-start.15) | copy-done | bytes 2097176
  55.5 19.7 %all-to-all-done = f32[128,24,128]{2,1,0:T(8,128)S(1)} async-done(((f32[128,24,128]{2,1,0:T(8,128)}), f32[128,24,128]{2,1,0:T(8,128)S(1)}, u32[]{:S(2)}, u32[]{:S(2)}) %all-to-all-start) | async-done | bytes 1572896 | tf_op jit(solution)/shard_map/all_to_all | solution.py:440
  75.2 1.2 %copy-done.11 = bf16[256,2048]{1,0:T(8,128)(2,1)S(1)} copy-done((bf16[256,2048]{1,0:T(8,128)(2,1)S(1)}, bf16[256,2048]{1,0:T(8,128)(2,1)}, u32[]{:S(2)}) %copy-start.11) | copy-done | bytes 1048600
  76.5 1.6 %copy-done.16 = bf16[1024,1024]{1,0:T(8,128)(2,1)S(1)} copy-done((bf16[1024,1024]{1,0:T(8,128)(2,1)S(1)}, bf16[1024,1024]{1,0:T(8,128)(2,1)}, u32[]{:S(2)}) %copy-start.16) | copy-done | bytes 2097176
  78.0 8.2 %row_transform.1 = f32[1,2,512,1024]{3,2,1,0:T(8,128)} custom-call(f32[3072,128]{1,0:T(8,128)S(1)} %bitcast.9, f32[64,1024]{1,0:T(8,128)S(1)} %get-tuple-element.21.pc_ref, f32[64,1024]{1,0:T(8,128)S(1)} %get-tuple-element.22.ps_ref, bf16[1024,1024]{1,0:T(8,128)(2,1)S(1)} %copy-done.16, bf16[256,2048]{1,0:T(8,128)(2,1)S(1)} %copy-done.11, ...), custom_call_target="tpu_custom_call" | custom-call | flops 5000000000 | bytes 12000000 | tf_op jit(solution)/shard_map/row_transform/pallas_call | solution.py:450
  (21 shorter events, 0.0 us)
Async XLA Ops:
  0.0 23.8 %collective-permute-start = (f32[1,2,4,16384]{3,2,1,0:T(4,128)}, f32[1,2,4,16384]{3,2,1,0:T(4,128)S(1)}, u32[]{:S(2)}, u32[]{:S(2)}) collective-permute-start(f32[1,2,4,16384]{3,2,1,0:T(4,128)} %own_ref.1), channel_id=1, source_target_pairs={{0,1},{1,0},{2,3},{3,2},{4,5},{5,4},{6,7},{7,6},{8,9},{9,8},{10,11... | collective-permute-start | bytes 1572872 | tf_op jit(solution)/shard_map/ppermute | solution.py:383
  5.3 0.7 copy-start.4
  6.0 0.7 copy-start.5
  6.6 0.7 copy-start.6
  7.3 0.7 copy-start.8
  9.3 1.0 %copy-start = (f32[1,2,4,16384]{3,2,1,0:T(4,128)S(1)}, f32[1,2,4,16384]{3,2,1,0:T(4,128)}, u32[]{:S(2)}) copy-start(f32[1,2,4,16384]{3,2,1,0:T(4,128)} %own_ref.1) | copy-start | bytes 1572868
  10.3 0.8 copy-start.2
  11.2 1.2 %copy-start.12 = (bf16[4096,128]{1,0:T(8,128)(2,1)S(1)}, bf16[4096,128]{1,0:T(8,128)(2,1)}, u32[]{:S(2)}) copy-start(bf16[4096,128]{1,0:T(8,128)(2,1)} %constant.20.clone.sample_ref) | copy-start | bytes 3145732
  12.4 11.4 %copy-start.1 = (f32[1,2,4,16384]{3,2,1,0:T(4,128)S(1)}, f32[1,2,4,16384]{3,2,1,0:T(4,128)}, u32[]{:S(2)}) copy-start(f32[1,2,4,16384]{3,2,1,0:T(4,128)} %own_ref.1) | copy-start | bytes 1572868
  12.4 11.4 %copy-start.3 = (f32[16384]{0:T(1024)S(1)}, f32[16384]{0:T(1024)}, u32[]{:S(2)}) copy-start(f32[16384]{0:T(1024)} %param.14) | copy-start | bytes 196612
  12.4 11.4 %copy-start.13 = (f32[16,512]{1,0:T(8,128)S(1)}, f32[16,512]{1,0:T(8,128)}, u32[]{:S(2)}) copy-start(f32[16,512]{1,0:T(8,128)} %constant.23.clone.ts_ref) | copy-start | bytes 98308
  12.4 11.4 %copy-start.14 = (f32[16,512]{1,0:T(8,128)S(1)}, f32[16,512]{1,0:T(8,128)}, u32[]{:S(2)}) copy-start(f32[16,512]{1,0:T(8,128)} %constant.22.clone.tc_ref) | copy-start | bytes 98308
  43.0 7.9 %copy-start.7 = (s32[64]{0:T(128)S(1)}, s32[64]{0:T(128)}, u32[]{:S(2)}) copy-start(s32[64]{0:T(128)} %param.16) | copy-start | bytes 772
  43.0 8.0 %copy-start.9 = (s32[64]{0:T(128)S(1)}, s32[64]{0:T(128)}, u32[]{:S(2)}) copy-start(s32[64]{0:T(128)} %param.19) | copy-start | bytes 772
  43.0 32.3 %all-to-all-start = ((f32[128,24,128]{2,1,0:T(8,128)}), f32[128,24,128]{2,1,0:T(8,128)S(1)}, u32[]{:S(2)}, u32[]{:S(2)}) async-start(f32[128,24,128]{2,1,0:T(8,128)} %bitcast.7), calls=%async_computation | async-start | bytes 3145728 | tf_op jit(solution)/shard_map/all_to_all | solution.py:440
  50.9 24.3 %copy-start.10 = (bf16[256,2048]{1,0:T(8,128)(2,1)S(1)}, bf16[256,2048]{1,0:T(8,128)(2,1)}, u32[]{:S(2)}) copy-start(bf16[256,2048]{1,0:T(8,128)(2,1)} %constant.25.clone.wl_ref) | copy-start | bytes 3145732
  54.2 1.3 %copy-start.15 = (bf16[1024,1024]{1,0:T(8,128)(2,1)}, bf16[1024,1024]{1,0:T(8,128)(2,1)S(1)}, u32[]{:S(2)}) copy-start(bf16[1024,1024]{1,0:T(8,128)(2,1)S(1)} %row_phases.1.left_ref) | copy-start | bytes 6291460
  75.2 1.2 %copy-start.11 = (bf16[256,2048]{1,0:T(8,128)(2,1)S(1)}, bf16[256,2048]{1,0:T(8,128)(2,1)}, u32[]{:S(2)}) copy-start(bf16[256,2048]{1,0:T(8,128)(2,1)} %constant.24.clone.wh_ref) | copy-start | bytes 3145732
  76.5 1.6 %copy-start.16 = (bf16[1024,1024]{1,0:T(8,128)(2,1)S(1)}, bf16[1024,1024]{1,0:T(8,128)(2,1)}, u32[]{:S(2)}) copy-start(bf16[1024,1024]{1,0:T(8,128)(2,1)} %copy-done.15) | copy-start | bytes 6291460

commit v3 on v2

v3 whole, which is shorter than its diff:
```python
import functools
import math

import jax
import jax.numpy as jnp
import ml_dtypes
import numpy as np
from jax import lax
from jax.experimental import pallas as pl
from jax.experimental.pallas import tpu as pltpu
from jax.sharding import PartitionSpec as P

NIMG = 262144
M = 1024
SUBROWS = 1024
TWO_PI = 2.0 * math.pi

BLOCK = 1024
SPAN = 4096
NODES = 32
RANK = 4
ERANK = 2
ROW_SCALE = 4.0
TABLE_SCALE = 32768.0
DATA_SCALE = 16.0

f32 = jnp.float32
bf16 = jnp.bfloat16
f8 = jnp.float8_e4m3fn


def _split(values):
    high = values.astype(np.float32).astype(ml_dtypes.bfloat16)
    low = (values - high.astype(np.float64)).astype(np.float32).astype(ml_dtypes.bfloat16)
    return high, low


def _kernel_sum(x, count):
    den = np.sin(np.pi * x / NIMG)
    zero = np.abs(den) < 1e-14
    return np.where(zero, float(count), np.sin(np.pi * x * count / NIMG) / np.where(zero, 1.0, den))


def _solve(gram, right):
    gram, right = gram.copy(), right.copy()
    n = len(gram)
    for i in range(n):
        for j in range(i + 1, n):
            factor = gram[j, i] / gram[i, i]
            gram[j] = gram[j] - factor * gram[i]
            right[j] = right[j] - factor * right[i]
    out = np.zeros_like(right)
    for i in range(n - 1, -1, -1):
        total = right[i].copy()
        for j in range(i + 1, n):
            total = total - gram[i, j] * out[j]
        out[i] = total / gram[i, i]
    return out


@functools.lru_cache(maxsize=None)
def _tables():
    scale = TWO_PI / NIMG
    bands = np.arange(M)
    product = (np.arange(BLOCK)[:, None] * bands[None, :]) % NIMG
    angle = (np.float32(scale) * product.astype(np.float32)).astype(np.float64)
    exact = scale * product
    resid_c = np.cos(angle).astype(np.float32).astype(ml_dtypes.bfloat16).astype(np.float64) - np.cos(exact)
    resid_s = np.sin(angle).astype(np.float32).astype(ml_dtypes.bfloat16).astype(np.float64) - np.sin(exact)
    half = M // 2
    resid = np.stack(
        [np.concatenate([resid_c[:, h * half:(h + 1) * half], resid_s[:, h * half:(h + 1) * half]], 1) for h in range(2)]
    )
    resid = (resid * TABLE_SCALE).astype(np.float32).astype(ml_dtypes.float8_e4m3fn)
    i = np.arange(NODES)
    nodes = 511.5 + 512 * 1.05 * (0.25 * ((2 * i + 1) / NODES - 1) - 0.75 * np.cos(np.pi * (i + 0.5) / NODES))
    gram = _kernel_sum(nodes[:, None] - nodes[None, :], SPAN) + 1e-13 * SPAN * np.eye(NODES)
    interp = _solve(gram, _kernel_sum(nodes[:, None] - bands[None, :], SPAN))
    centre = (SPAN - 1) / 2
    at = scale * (np.arange(SPAN) - centre)[:, None] * nodes[None, :]
    sample = np.concatenate([np.cos(at), -np.sin(at)], 1)
    sample = np.concatenate(_split(sample), 1)
    rows = []
    for span in range(16384 // SPAN):
        turn = scale * (span * SPAN + centre) * bands
        re, im = interp * np.cos(turn), -interp * np.sin(turn)
        rows.append(np.concatenate([re, im], 1))
        rows.append(np.concatenate([-im, re], 1))
    weave = np.concatenate(rows, 0)
    weave_hi, weave_lo = _split(weave)
    turn = TWO_PI * ((np.arange(16)[:, None] * (bands[None, :half] % 256)) % 256) / 256
    return dict(
        resid=resid, sample=sample, weave_hi=weave_hi, weave_lo=weave_lo,
        turn_c=np.cos(turn).astype(np.float32), turn_s=np.sin(turn).astype(np.float32),
    )


COL_A, COL_SC8, COL_CF8, COL_ROW = 0, 16, 24, 32
CHUNKS = 24


def _angle(product):
    turns = lax.bitwise_and(product + NIMG, 2 * NIMG - 1) - NIMG
    return turns.astype(f32) * (math.pi / NIMG)


def _offset_row(order_ref, offsets_ref, which):
    slots = lax.broadcasted_iota(jnp.int32, (64, 64), 0)
    offsets = _to_column(offsets_ref[which:which + 1, :].astype(f32))
    return jnp.sum(jnp.where(slots == order_ref[...], offsets, 0.0), axis=0, keepdims=True)


def _to_column(row):
    at = lax.broadcasted_iota(jnp.int32, (64, 64), 0) == lax.broadcasted_iota(jnp.int32, (64, 64), 1)
    return jnp.sum(jnp.where(at, row, 0.0), axis=1, keepdims=True)


def _pick(row, index):
    lane = lax.broadcasted_iota(jnp.int32, row.shape, 1)
    return jnp.sum(jnp.where(lane == index, row, 0.0), axis=1, keepdims=True)


def _prepare(slot, half, order_ref, offsets_ref, cols_ref, rows_ref, band_ref,
             lc_ref, ls_ref, pc_ref, ps_ref, mc_ref, ms_ref, combine_ref, wc_ref, ws_ref):
    cf_row = _offset_row(order_ref, offsets_ref, 0)
    own_cf = _pick(cf_row, slot).astype(jnp.int32)
    cf = _to_column(cf_row).astype(jnp.int32)
    sc = _to_column(cols_ref[...].astype(f32)).astype(jnp.int32)
    sr = _to_column(rows_ref[...].astype(f32)).astype(jnp.int32)
    lane = lax.broadcasted_iota(jnp.int32, (64, 128), 1)
    row = lax.bitwise_and(4 * half + 4 * lax.bitwise_and(lane // 8, 1) + lax.bitwise_and(lane, 3), 7)
    odd = 2 * row - 7
    factor = jnp.where(
        lane < COL_SC8, 2 * (own_cf + 1024 * lane),
        jnp.where(lane < COL_CF8, 256 * (lane - COL_SC8), jnp.where(lane < COL_ROW, 256 * (lane - COL_CF8), odd)),
    )
    other = jnp.where(lane < COL_CF8, sc, jnp.where(lane < COL_ROW, cf, sr + 512))
    angle = _angle(factor * other)
    mc, ms = jnp.cos(angle), jnp.sin(angle)
    mc_ref[...] = mc
    ms_ref[...] = ms
    angle = _angle(2 * lane * sc)
    low_c, low_s = jnp.cos(angle), jnp.sin(angle)
    for i in range(8):
        c, s = mc[:, COL_SC8 + i:COL_SC8 + i + 1], ms[:, COL_SC8 + i:COL_SC8 + i + 1]
        lc_ref[:, i * 128:(i + 1) * 128] = c * low_c - s * low_s
        ls_ref[:, i * 128:(i + 1) * 128] = s * low_c + c * low_s
    angle = _angle(2 * lane * cf)
    low_c, low_s = jnp.cos(angle), jnp.sin(angle)
    for i in range(8):
        c, s = mc[:, COL_CF8 + i:COL_CF8 + i + 1], ms[:, COL_CF8 + i:COL_CF8 + i + 1]
        band = band_ref[:, i * 128:(i + 1) * 128]
        pc_ref[:, i * 128:(i + 1) * 128] = (c * low_c - s * low_s) * band
        ps_ref[:, i * 128:(i + 1) * 128] = (s * low_c + c * low_s) * band
    rho = odd.astype(f32) * (0.5 / ROW_SCALE)
    power = jnp.ones((64, 128), f32)
    first = lax.bitwise_and(lane, 4) == 0
    to_re, to_im = jnp.where(first, mc, ms), jnp.where(first, -ms, mc)
    for n in range(RANK):
        wc_ref[n] = mc * power
        ws_ref[n] = ms * power
        if n < ERANK:
            for part, value in ((0, to_re), (1, to_im)):
                base = part * 128 + n * 64
                combine_ref[base:base + 64, :] = (value * power)[:, COL_ROW:COL_ROW + 16].astype(bf16)
        power = power * rho


def _exact_kernel(order_hbm, offsets_hbm, cols_hbm, rows_hbm, band_hbm, data_hbm, window_hbm, sample_hbm,
                  lc_ref, ls_ref, pc_ref, ps_ref, mc_ref, ms_ref, combine_ref, out_ref,
                  order_ref, offsets_ref, cols_ref, rows_ref, band_ref, data_ref, window_ref, sample_ref,
                  wc_ref, ws_ref, even_ref, odd_ref, acc_ref, sems):
    loads = [
        pltpu.make_async_copy(source, target, sems.at[i])
        for i, (source, target) in enumerate((
            (order_hbm, order_ref), (offsets_hbm, offsets_ref), (cols_hbm, cols_ref), (rows_hbm, rows_ref),
            (band_hbm, band_ref), (data_hbm, data_ref), (window_hbm, window_ref), (sample_hbm, sample_ref),
        ))
    ]
    for load in loads:
        load.start()
    for load in loads[:5]:
        load.wait()
    acc_ref[...] = jnp.zeros_like(acc_ref)
    _prepare(lax.axis_index("facet"), lax.axis_index("rows"), order_ref, offsets_ref, cols_ref, rows_ref, band_ref,
             lc_ref, ls_ref, pc_ref, ps_ref, mc_ref, ms_ref, combine_ref, wc_ref, ws_ref)
    for load in loads[5:]:
        load.wait()

    def build(block, x_ref, bc, bs, i):
        cols = slice(i * 256, (i + 1) * 256)
        here = pl.ds(pl.multiple_of(block * BLOCK + i * 256, 256), 256)
        window = window_ref[:, here]
        re_rows = data_ref[0, 0, :, here] * window
        im_rows = data_ref[0, 1, :, here] * window
        for g in range(4):
            rows = slice(g * 16, (g + 1) * 16)
            lc, ls = lc_ref[rows, cols], ls_ref[rows, cols]
            c, s = bc[rows], bs[rows]
            ec = c * lc - s * ls
            es = s * lc + c * ls
            for r in range(4):
                dr, di = re_rows[r:r + 1], im_rows[r:r + 1]
                at = r * 64 + g * 16
                x_ref[at:at + 16, cols] = (dr * ec + di * es).astype(bf16)
                x_ref[256 + at:256 + at + 16, cols] = (di * ec - dr * es).astype(bf16)

    def turns(block):
        return _pick(mc_ref[...], block), _pick(ms_ref[...], block)

    def stage(block, x_ref, following, next_ref):
        bc, bs = turns(following)
        rows = pl.ds(pl.multiple_of(lax.rem(block, 4) * BLOCK, BLOCK), BLOCK)
        span = block // 4
        for p in range(2):
            half = slice(p * 256, (p + 1) * 256)
            part = jnp.dot(x_ref[half, :], sample_ref[rows, :], preferred_element_type=f32)
            build(following, next_ref, bc, bs, 2 * p)
            build(following, next_ref, bc, bs, 2 * p + 1)
            acc_ref[span, half, :] = acc_ref[span, half, :] + part

    bc, bs = turns(0)
    for i in range(4):
        build(0, even_ref, bc, bs, i)

    def body(pair, carry):
        stage(2 * pair, even_ref, 2 * pair + 1, odd_ref)
        stage(2 * pair + 1, odd_ref, lax.rem(2 * pair + 2, 16), even_ref)
        return carry

    lax.fori_loop(0, 8, body, 0)

    lane = lax.broadcasted_iota(jnp.int32, (64, 128), 1)
    sign = jnp.where(lax.bitwise_and(lane, 32) == 0, -1.0, 1.0).astype(f32)
    sums = [[None] * 4 for _ in range(RANK)]
    for span in range(4):
        for r in range(4):
            re = acc_ref[span, r * 64:(r + 1) * 64]
            im = acc_ref[span, 256 + r * 64:256 + (r + 1) * 64]
            re = re + pltpu.roll(re, 64, 1)
            im = im + pltpu.roll(im, 64, 1)
            value = re + sign * pltpu.roll(im, 32, 1)
            turned = sign * pltpu.roll(value, 32, 1)
            for n in range(RANK):
                col = slice(COL_ROW + r, COL_ROW + r + 1)
                term = wc_ref[n, :, col] * value - ws_ref[n, :, col] * turned
                sums[n][span] = term if sums[n][span] is None else sums[n][span] + term
    for n in range(RANK):
        out_ref[:, n * 256:n * 256 + 128] = jnp.where(lane < 64, sums[n][0], sums[n][1])
        out_ref[:, n * 256 + 128:n * 256 + 256] = jnp.where(lane < 64, sums[n][2], sums[n][3])


def _residual_kernel(own_hbm, peer_hbm, window_hbm, lc_hbm, ls_hbm, mc_hbm, ms_hbm, combine_hbm,
                     table_hbm, tc_hbm, ts_hbm, nodes_hbm, out_ref,
                     own_ref, peer_ref, window_ref, lc_ref, ls_ref, mc_ref, ms_ref, combine_ref,
                     table_ref, tc_ref, ts_ref, nodes_ref, even_ref, odd_ref, sum_ref, sems):
    loads = [
        pltpu.make_async_copy(source, target, sems.at[i])
        for i, (source, target) in enumerate((
            (own_hbm, own_ref), (peer_hbm, peer_ref), (window_hbm, window_ref), (lc_hbm, lc_ref), (ls_hbm, ls_ref),
            (mc_hbm, mc_ref), (ms_hbm, ms_ref), (combine_hbm, combine_ref),
            (table_hbm.at[lax.axis_index("rows")], table_ref), (tc_hbm, tc_ref), (ts_hbm, ts_ref),
            (nodes_hbm, nodes_ref),
        ))
    ]
    for load in loads:
        load.start()
    sum_ref[...] = jnp.zeros_like(sum_ref)
    for load in loads[:3]:
        load.wait()
    largest = jnp.zeros((4, 2048), f32)
    for i in range(8):
        here = slice(i * 2048, (i + 1) * 2048)
        window = window_ref[:, here]
        for ref in (own_ref, peer_ref):
            for part in range(2):
                largest = jnp.maximum(largest, jnp.abs(ref[0, part, :, here] * window))
    largest = jnp.maximum(jnp.max(jnp.max(largest, axis=1, keepdims=True), axis=0, keepdims=True), 1e-30)
    scale_in = DATA_SCALE / largest
    scale_out = largest * (1.0 / (DATA_SCALE * TABLE_SCALE))
    for load in loads[3:8]:
        load.wait()

    def mix(block, i):
        here = pl.ds(pl.multiple_of(block * BLOCK + i * 256, 256), 256)
        window = window_ref[:, here] * scale_in
        data = jnp.concatenate(
            [own_ref[0, 0, :, here], own_ref[0, 1, :, here], peer_ref[0, 0, :, here], peer_ref[0, 1, :, here]], 0
        )
        return jnp.dot(combine_ref[...], (data * window).astype(bf16), preferred_element_type=f32)

    def build(z_ref, j, i, rows, bc, bs):
        cols = slice(i * 256, (i + 1) * 256)
        lc, ls = lc_ref[:, cols], ls_ref[:, cols]
        ec = bc * lc - bs * ls
        es = bs * lc + bc * ls
        for n in range(ERANK):
            gr, gi = rows[n * 64:(n + 1) * 64], rows[128 + n * 64:128 + (n + 1) * 64]
            at = j * 256 + n * 64
            z_ref[at:at + 64, cols] = (gr * ec + gi * es).astype(z_ref.dtype)
            z_ref[at + 128:at + 192, cols] = (gi * ec - gr * es).astype(z_ref.dtype)

    def turns(block):
        return _pick(mc_ref[...], block), _pick(ms_ref[...], block)

    def stage(group, z_ref, following, next_ref):
        tasks = [(j, i) for j in range(2) for i in range(4)]
        spins = [turns(following * 2 + j) for j in range(2)]
        ready = mix(following * 2, 0)
        at = 0
        for j in range(2):
            for kc in range(2):
                cols = slice(kc * 256, (kc + 1) * 256)
                z = z_ref[j * 256:(j + 1) * 256, :]
                by_c = jnp.dot(z, table_ref[:, cols], preferred_element_type=f32)
                by_s = jnp.dot(z, table_ref[:, 512 + kc * 256:768 + kc * 256], preferred_element_type=f32)
                for _ in range(2):
                    bj, bi = tasks[at]
                    at += 1
                    coming = mix(following * 2 + tasks[at][0], tasks[at][1]) if at < 8 else None
                    build(next_ref, bj, bi, ready, *spins[bj])
                    ready = coming
                re = by_c[0:128] + by_s[128:256]
                im = by_c[128:256] - by_s[0:128]
                tc = tc_ref[pl.ds(group * 2 + j, 1), cols]
                ts = ts_ref[pl.ds(group * 2 + j, 1), cols]
                sum_ref[0, :, cols] = sum_ref[0, :, cols] + (re * tc + im * ts)
                sum_ref[1, :, cols] = sum_ref[1, :, cols] + (im * tc - re * ts)

    for j in range(2):
        spin = turns(j)
        for i in range(4):
            build(even_ref, j, i, mix(j, i), *spin)
    for load in loads[8:]:
        load.wait()

    def body(pair, carry):
        stage(2 * pair, even_ref, 2 * pair + 1, odd_ref)
        stage(2 * pair + 1, odd_ref, lax.rem(2 * pair + 2, 8), even_ref)
        return carry

    lax.fori_loop(0, 4, body, 0)

    for copy in range(2):
        for i in range(8):
            out_ref[pl.ds(copy * CHUNKS + 16 + i, 64, stride=2 * CHUNKS), :] = nodes_ref[:, i * 128:(i + 1) * 128]
        for n in range(ERANK):
            for part in range(2):
                for kc in range(4):
                    at = copy * CHUNKS + n * 8 + part * 4 + kc
                    out_ref[pl.ds(at, 64, stride=2 * CHUNKS), :] = (
                        sum_ref[part, n * 64:(n + 1) * 64, kc * 128:(kc + 1) * 128] * scale_out
                    )


def _halves(value):
    high = value.astype(bf16)
    return high, (value - high.astype(f32)).astype(bf16)


def _phase_kernel(order_ref, offsets_ref, rows_ref, left_ref, gram_ref, all_ref, turned_ref):
    slot, half = lax.axis_index("facet"), lax.axis_index("rows")
    rf = _offset_row(order_ref, offsets_ref, 1).astype(jnp.int32)
    own_sr = _pick(rows_ref[...].astype(f32), slot).astype(jnp.int32)
    odd = jnp.concatenate([2 * rf + 7, 2 * rf + 7], 1)
    lane = lax.broadcasted_iota(jnp.int32, (128, 128), 1)
    quarter = jnp.where(lane < 64, 0, -(NIMG // 2))
    sign = jnp.where(lane < 64, -1.0, 1.0).astype(f32)
    for i in range(8):
        here = slice(i * 128, (i + 1) * 128)
        q = lax.broadcasted_iota(jnp.int32, (128, 128), 0) + i * 128 + half * 512
        q = lax.bitwise_and(q, 1023)
        turn = jnp.cos(_angle(odd * (own_sr + q) + quarter))
        other = sign * pltpu.roll(turn, 64, 1)
        g = (q - 512).astype(f32) * (TWO_PI / NIMG * ROW_SCALE)
        g2, g3 = g * g * 0.5, g * g * g * (1.0 / 6.0)
        for n, value in enumerate((turn, g * other, -g2 * turn, -g3 * other)):
            high, low = _halves(value)
            cols = slice(n * 128, (n + 1) * 128)
            all_ref[0, here, cols] = high
            all_ref[1, here, cols] = low
            high_t, low_t = _halves(sign * pltpu.roll(value, 64, 1))
            turned_ref[0, here, cols] = high_t
            turned_ref[1, here, cols] = low_t
            if i < 4 and n < 2:
                left_ref[here, n * 128:(n + 1) * 128] = high
                left_ref[here, 256 + n * 128:256 + (n + 1) * 128] = high
                left_ref[here, 512 + n * 128:512 + (n + 1) * 128] = low
            elif i < 4:
                left_ref[here, 512 + n * 128:512 + (n + 1) * 128] = high
    over_rows = (((0,), (0,)), ((), ()))
    gram = None
    for ref in (all_ref, turned_ref):
        for a, b in ((0, 0), (0, 1), (1, 0)):
            part = lax.dot_general(ref[a], ref[b], over_rows, preferred_element_type=f32)
            gram = part if gram is None else gram + part
    high, low = _halves(gram)
    gram_ref[:, 0:256] = high[:, 0:256]
    gram_ref[:, 256:512] = high[:, 0:256]
    gram_ref[:, 512:768] = low[:, 0:256]
    gram_ref[:, 768:1024] = high[:, 256:512]


def _rows_kernel(got_any, wh_hbm, wl_hbm, pc_hbm, ps_hbm, gram_hbm, left_hbm, out_hbm,
                 got_ref, wh_ref, wl_ref, pc_ref, ps_ref, gram_ref, left_ref, right_ref, value_ref, high_ref, low_ref,
                 out_ref, sems, out_sems):
    loads = [
        pltpu.make_async_copy(source, target, sems.at[i])
        for i, (source, target) in enumerate((
            (got_any, got_ref), (wh_hbm, wh_ref), (wl_hbm, wl_ref), (pc_hbm, pc_ref), (ps_hbm, ps_ref),
            (gram_hbm, gram_ref), (left_hbm, left_ref),
        ))
    ]
    for load in loads:
        load.start()
    loads[0].wait()
    for n in range(RANK):
        for i in range(2):
            chunk = 16 + n * 2 + i
            value = (
                got_ref[pl.ds(chunk, 64, stride=2 * CHUNKS), :]
                + got_ref[pl.ds(CHUNKS + chunk, 64, stride=2 * CHUNKS), :]
            )
            high, low = _halves(value)
            high_ref[n * 64:(n + 1) * 64, i * 128:(i + 1) * 128] = high
            if n < 2:
                low_ref[n * 64:(n + 1) * 64, i * 128:(i + 1) * 128] = low
    for load in loads[1:5]:
        load.wait()
    for i in range(4):
        cols = slice(i * 256, (i + 1) * 256)
        vals = []
        for part in range(2):
            wcols = slice(part * 1024 + i * 256, part * 1024 + (i + 1) * 256)
            wh, wl = wh_ref[:, wcols], wl_ref[:, wcols]
            main = jnp.dot(high_ref[...], wh, preferred_element_type=f32)
            rest = (
                jnp.dot(high_ref[0:128], wl, preferred_element_type=f32)
                + jnp.dot(low_ref[...], wh, preferred_element_type=f32)
            )
            vals.append((main, rest))
        pc, ps = pc_ref[:, cols], ps_ref[:, cols]
        for n in range(RANK):
            rows = slice(n * 64, (n + 1) * 64)
            vr, vi = vals[0][0][rows], vals[1][0][rows]
            if n < ERANK:
                parts = []
                for part in range(2):
                    at = (i // 2) * CHUNKS + n * 8 + part * 4 + 2 * (i % 2)
                    parts.append(jnp.concatenate(
                        [got_ref[pl.ds(at + m, 64, stride=2 * CHUNKS), :] for m in range(2)], 1))
                vr = vr + vals[0][1][rows] + parts[0]
                vi = vi + vals[1][1][rows] + parts[1]
            cr = vr * pc + vi * ps
            ci = vi * pc - vr * ps
            at = n * 128
            value_ref[at:at + 64, cols] = cr
            value_ref[at + 64:at + 128, cols] = ci
            turned = slice(1024 + i * 256, 1024 + (i + 1) * 256)
            cr_high, ci_high = cr.astype(bf16), ci.astype(bf16)
            bases = (0, 512) if n < 2 else (512,)
            for base in bases:
                right_ref[base + at:base + at + 64, cols] = cr_high
                right_ref[base + at + 64:base + at + 128, cols] = ci_high
                right_ref[base + at:base + at + 64, turned] = ci_high
                right_ref[base + at + 64:base + at + 128, turned] = -cr_high
            if n < 2:
                cr_low = (cr - cr_high.astype(f32)).astype(bf16)
                ci_low = (ci - ci_high.astype(f32)).astype(bf16)
                right_ref[256 + at:256 + at + 64, cols] = cr_low
                right_ref[256 + at + 64:256 + at + 128, cols] = ci_low
                right_ref[256 + at:256 + at + 64, turned] = ci_low
                right_ref[256 + at + 64:256 + at + 128, turned] = -cr_low

    loads[5].wait()
    total = jnp.zeros((8, 256), f32)
    for i in range(4):
        cols = slice(i * 256, (i + 1) * 256)
        product = jnp.dot(gram_ref[...], right_ref[:, cols], preferred_element_type=f32) * value_ref[:, cols]
        total = total + jnp.sum(product.reshape(64, 8, 256), 0)
    mean = jnp.maximum(jnp.sum(total), 0.0) / (2.0 * SUBROWS * M)
    factor = lax.rsqrt(jnp.full((8, 128), mean, f32) + 1e-06)[0:1, 0:1]

    loads[6].wait()
    stores = []
    for part in range(2):
        for i in range(4):
            cols = slice(i * 256, (i + 1) * 256)
            right = right_ref[:, part * 1024 + i * 256:part * 1024 + (i + 1) * 256]
            out_ref[part, :, cols] = jnp.dot(left_ref[...], right, preferred_element_type=f32) * factor
            store = pltpu.make_async_copy(
                out_ref.at[part, :, cols], out_hbm.at[0, part, :, cols], out_sems.at[part * 4 + i])
            store.start()
            stores.append(store)
    for store in stores:
        store.wait()


def per_device(facets, facet_window, band_window, facet_order, facet_offsets, sub_cols, sub_rows):
    tables = _tables()
    peer = lax.ppermute(facets, "rows", [(0, 1), (1, 0)])
    order, cols, rows = (v.reshape(1, 64) for v in (facet_order, sub_cols, sub_rows))
    offsets = facet_offsets.T
    window = facet_window.reshape(1, 16384)
    hbm = pl.BlockSpec(memory_space=pltpu.HBM)
    anywhere = pl.BlockSpec(memory_space=pl.ANY)
    vmem = pl.BlockSpec(memory_space=pltpu.VMEM)
    shape = jax.ShapeDtypeStruct

    def params(mib):
        return pltpu.CompilerParams(vmem_limit_bytes=mib * 1024 * 1024)

    wide, narrow = shape((64, 1024), f32), shape((64, 128), f32)
    lc, ls, pc, ps, mc, ms, combine, nodes = pl.pallas_call(
        _exact_kernel,
        in_specs=[hbm] * 8,
        out_shape=[wide, wide, wide, wide, narrow, narrow, shape((256, 16), bf16), wide],
        scratch_shapes=[
            pltpu.VMEM((1, 64), jnp.int32), pltpu.VMEM((2, 64), jnp.int32), pltpu.VMEM((1, 64), jnp.int32),
            pltpu.VMEM((1, 64), jnp.int32), pltpu.VMEM((1, M), f32), pltpu.VMEM((1, 2, 4, 16384), f32),
            pltpu.VMEM((1, 16384), f32), pltpu.VMEM((SPAN, 128), bf16),
            pltpu.VMEM((RANK, 64, 128), f32), pltpu.VMEM((RANK, 64, 128), f32),
            pltpu.VMEM((512, BLOCK), bf16), pltpu.VMEM((512, BLOCK), bf16), pltpu.VMEM((4, 512, 128), f32),
            pltpu.SemaphoreType.DMA((8,)),
        ],
        compiler_params=params(60),
        cost_estimate=pl.CostEstimate(flops=8 * 10**9, bytes_accessed=2 * 10**6, transcendentals=0),
        name="exact_part",
    )(order, offsets, cols, rows, band_window.reshape(1, M), facets, window, jnp.asarray(tables["sample"]))

    send = pl.pallas_call(
        _residual_kernel,
        in_specs=[hbm, anywhere] + [hbm] * 10,
        out_shape=shape((128 * CHUNKS, 128), f32),
        scratch_shapes=[
            pltpu.VMEM((1, 2, 4, 16384), f32), pltpu.VMEM((1, 2, 4, 16384), f32), pltpu.VMEM((1, 16384), f32),
            pltpu.VMEM((64, 1024), f32), pltpu.VMEM((64, 1024), f32), pltpu.VMEM((64, 128), f32),
            pltpu.VMEM((64, 128), f32), pltpu.VMEM((256, 16), bf16),
            pltpu.VMEM((1024, 1024), f8), pltpu.VMEM((16, 512), f32), pltpu.VMEM((16, 512), f32),
            pltpu.VMEM((64, 1024), f32),
            pltpu.VMEM((512, 1024), f8), pltpu.VMEM((512, 1024), f8), pltpu.VMEM((2, 128, 512), f32),
            pltpu.SemaphoreType.DMA((12,)),
        ],
        compiler_params=params(60),
        cost_estimate=pl.CostEstimate(flops=9 * 10**9, bytes_accessed=4 * 10**6, transcendentals=0),
        name="residual_part",
    )(
        facets, peer, window, lc, ls, mc, ms, combine, jnp.asarray(tables["resid"]), jnp.asarray(tables["turn_c"]),
        jnp.asarray(tables["turn_s"]), nodes,
    )

    got = lax.all_to_all(send.reshape(128, CHUNKS, 128), ("facet", "rows"), split_axis=0, concat_axis=0, tiled=True)
    left, gram = pl.pallas_call(
        _phase_kernel,
        in_specs=[vmem] * 3,
        out_shape=[shape((512, 1024), bf16), shape((512, 1024), bf16)],
        scratch_shapes=[pltpu.VMEM((2, 1024, 512), bf16), pltpu.VMEM((2, 1024, 512), bf16)],
        compiler_params=params(60),
        cost_estimate=pl.CostEstimate(flops=3 * 10**9, bytes_accessed=2 * 10**6, transcendentals=2 * 10**5),
        name="row_phases",
    )(order, offsets, rows)

    return pl.pallas_call(
        _rows_kernel,
        in_specs=[anywhere] + [hbm] * 6,
        out_specs=hbm,
        out_shape=shape((1, 2, 512, 1024), f32),
        scratch_shapes=[
            pltpu.VMEM((128 * CHUNKS, 128), f32), pltpu.VMEM((256, 2048), bf16), pltpu.VMEM((256, 2048), bf16),
            pltpu.VMEM((64, 1024), f32), pltpu.VMEM((64, 1024), f32), pltpu.VMEM((512, 1024), bf16),
            pltpu.VMEM((512, 1024), bf16), pltpu.VMEM((1024, 2048), bf16), pltpu.VMEM((512, 1024), f32),
            pltpu.VMEM((256, 256), bf16), pltpu.VMEM((128, 256), bf16), pltpu.VMEM((2, 512, 1024), f32),
            pltpu.SemaphoreType.DMA((7,)), pltpu.SemaphoreType.DMA((8,)),
        ],
        compiler_params=params(60),
        cost_estimate=pl.CostEstimate(flops=5 * 10**9, bytes_accessed=12 * 10**6, transcendentals=0),
        name="row_transform",
    )(got.reshape(128 * CHUNKS, 128), jnp.asarray(tables["weave_hi"]), jnp.asarray(tables["weave_lo"]), pc, ps, gram, left)


def solution(mesh):
    return jax.shard_map(
        per_device,
        mesh=mesh,
        in_specs=(P("facet", None, "rows", None), P(), P(), P(), P(), P(), P()),
        out_specs=P("facet", None, "rows", None),
        check_vma=False,
    )
```

time: 86.7 us -> 74.2 us (0.86)
  local copies, waits for them, and re-layouts: 10.7 us -> 1.94 us
  waiting for transfers between devices: 19.7 us -> 16.7 us
    unnamed x35 -> x4, local copies, waits for them, and re-layouts: 10.7 us -> 1.94 us
    all_to_all x1, waiting for transfers between devices: 19.7 us -> 16.7 us  [per_device(): lax.all_to_all(send.reshape(128, CHUNKS, 128), ('facet', 'rows'), split_a...]
    pallas_call x5 -> x4, Pallas kernels: 43.2 us -> 42.6 us  [the longest x1 14.3 us: per_device(): pl.pallas_call(_exact_kernel, in_specs=[hbm] * 8, out_shape=[wide, wide,...]
  transfers between devices with their start and end apart: 2 -> 2, of which waited for: 1 -> 1; matrix products, arithmetic and copies ran while one was open for 1% -> 0% of each run, Pallas kernels for 19% -> 30%
where the time goes in v3:
time: 74.2 us; the launch traced here: 74 us
  Pallas kernels  42.6 us (57%)
  waiting for transfers between devices  16.7 us (23%)
  starting transfers between devices  12.6 us (17%)
  local copies, waits for them, and re-layouts  1.94 us (3%)
    all_to_all x1, waiting for transfers between devices, per_device(): lax.all_to_all(send.reshape(128, CHUNKS, 128), ('facet', 'rows'), split_a...  16.7 us
    pallas_call x1, Pallas kernels, per_device(): pl.pallas_call(_exact_kernel, in_specs=[hbm] * 8, out_shape=[wide, wide,...  14.3 us
    pallas_call x1, Pallas kernels, per_device(): pl.pallas_call(_residual_kernel, in_specs=[hbm, anywhere] + [hbm] * 10, o...  12.5 us
    pallas_call x1, Pallas kernels, per_device(): pl.pallas_call(_rows_kernel, in_specs=[anywhere] + [hbm] * 6, out_specs=h...  8.19 us
    all_to_all x1, starting transfers between devices, per_device(): lax.all_to_all(send.reshape(128, CHUNKS, 128), ('facet', 'rows'), split_a...  8.14 us
    pallas_call x1, Pallas kernels, per_device(): pl.pallas_call(_phase_kernel, in_specs=[vmem] * 3, out_shape=[shape((512,...  7.59 us
    ppermute x1, starting transfers between devices, per_device(): peer = lax.ppermute(facets, 'rows', [(0, 1), (1, 0)])  4.43 us
    unnamed x4, local copies, waits for them, and re-layouts  1.94 us
  transfers between devices with their start and end apart: 2, of which 1 were waited for; matrix products, arithmetic and copies ran while one was open for 0% of the time, Pallas kernels for 30%

profile of v3, /device:TPU:1, one launch (start us, length us, event | category | flops | bytes accessed | tf_op | source)
XLA Modules:
  0.0 74.0 jit_solution(845273858322695005)
XLA Ops:
  0.0 4.4 %collective-permute-start = (f32[1,2,4,16384]{3,2,1,0:T(4,128)}, f32[1,2,4,16384]{3,2,1,0:T(4,128)S(1)}, u32[]{:S(2)}, u32[]{:S(2)}) collective-permute-start(f32[1,2,4,16384]{3,2,1,0:T(4,128)} %own_hbm.1), channel_id=1, source_target_pairs={{0,1},{1,0},{2,3},{3,2},{4,5},{5,4},{6,7},{7,6},{8,9},{9,8},{10,11... | collective-permute-start | bytes 1572872 | tf_op jit(solution)/shard_map/ppermute | solution.py:501
  4.4 14.3 %exact_part.1 = (f32[64,1024]{1,0:T(8,128)}, f32[64,1024]{1,0:T(8,128)}, f32[64,1024]{1,0:T(8,128)}, f32[64,1024]{1,0:T(8,128)}, f32[64,128]{1,0:T(8,128)}, /*in...) custom-call(s32[1,64]{1,0:T(1,128)} %bitcast.16, s32[2,64]{1,0:T(2,128)} %bitcast.13, ...), custom_call_target="tpu_custom_call" | custom-call | flops 8000000000 | bytes 2000000 | tf_op jit(solution)/shard_map/exact_part/pallas_call | solution.py:514
  18.7 0.0 collective-permute-done.peer_hbm
  18.8 0.0 copy-start.1
  18.8 0.8 %copy-done.1 = f32[1,2,4,16384]{3,2,1,0:T(4,128)} copy-done((f32[1,2,4,16384]{3,2,1,0:T(4,128)}, f32[1,2,4,16384]{3,2,1,0:T(4,128)S(1)}, u32[]{:S(2)}) %copy-start.1) | copy-done | bytes 524312
  19.5 12.5 %residual_part.1 = f32[3072,128]{1,0:T(8,128)} custom-call(f32[1,2,4,16384]{3,2,1,0:T(4,128)} %own_hbm.1, f32[1,2,4,16384]{3,2,1,0:T(4,128)} %copy-done.1, f32[1,16384]{1,0:T(1,128)} %bitcast.11, f32[64,1024]{1,0:T(8,128)} %get-tuple-element.15.lc_hbm, f32[64,1024]{1,0:T(8,128)} %get-tuple-element.16.ls_hbm, f32[64,128]{1,0:T(8,128)} %get-tuple-element.17.mc_hbm, ...), custom_call_target="tpu_custom_call" | custom-call | flops 8999999488 | bytes 4000000 | tf_op jit(solution)/shard_map/residual_part/pallas_call | solution.py:531
  32.0 8.1 %all-to-all-start = ((f32[128,24,128]{2,1,0:T(8,128)}), f32[128,24,128]{2,1,0:T(8,128)S(1)}, u32[]{:S(2)}, u32[]{:S(2)}) async-start(f32[128,24,128]{2,1,0:T(8,128)} %bitcast.9), calls=%async_computation | async-start | bytes 3145728 | tf_op jit(solution)/shard_map/all_to_all | solution.py:552
  40.2 7.6 %row_phases.1 = (bf16[512,1024]{1,0:T(8,128)(2,1)}, bf16[512,1024]{1,0:T(8,128)(2,1)}) custom-call(s32[1,64]{1,0:T(1,128)} %bitcast.17, s32[2,64]{1,0:T(2,128)} %bitcast.14, s32[1,64]{1,0:T(1,128)} %bitcast.19), custom_call_target="tpu_custom_call" | custom-call | flops 3000000000 | bytes 2000000 | tf_op jit(solution)/shard_map/row_phases/pallas_call | solution.py:553
  47.8 16.7 %all-to-all-done = f32[128,24,128]{2,1,0:T(8,128)S(1)} async-done(((f32[128,24,128]{2,1,0:T(8,128)}), f32[128,24,128]{2,1,0:T(8,128)S(1)}, u32[]{:S(2)}, u32[]{:S(2)}) %all-to-all-start) | async-done | bytes 1572896 | tf_op jit(solution)/shard_map/all_to_all | solution.py:552
  64.5 0.0 copy-start
  64.5 1.2 %copy-done = f32[128,24,128]{2,1,0:T(8,128)} copy-done((f32[128,24,128]{2,1,0:T(8,128)}, f32[128,24,128]{2,1,0:T(8,128)S(1)}, u32[]{:S(2)}) %copy-start) | copy-done | bytes 1572888
  65.7 8.2 %row_transform.1 = f32[1,2,512,1024]{3,2,1,0:T(8,128)} custom-call(f32[3072,128]{1,0:T(8,128)} %bitcast.8, bf16[256,2048]{1,0:T(8,128)(2,1)} %constant.16.clone.wh_hbm, bf16[256,2048]{1,0:T(8,128)(2,1)} %constant.17.clone.wl_hbm, f32[64,1024]{1,0:T(8,128)} %get-tuple-element.21.pc_hbm, f32[64,1024]{1,0:T(8,128)} %get-tuple-element.22.ps_hbm, ...), custom_call_target="tpu_custom_call" | custom-call | flops 5000000000 | bytes 12000000 | tf_op jit(solution)/shard_map/row_transform/pallas_call | solution.py:563
Async XLA Ops:
  0.0 18.7 %collective-permute-start = (f32[1,2,4,16384]{3,2,1,0:T(4,128)}, f32[1,2,4,16384]{3,2,1,0:T(4,128)S(1)}, u32[]{:S(2)}, u32[]{:S(2)}) collective-permute-start(f32[1,2,4,16384]{3,2,1,0:T(4,128)} %own_hbm.1), channel_id=1, source_target_pairs={{0,1},{1,0},{2,3},{3,2},{4,5},{5,4},{6,7},{7,6},{8,9},{9,8},{10,11... | collective-permute-start | bytes 1572872 | tf_op jit(solution)/shard_map/ppermute | solution.py:501
  18.8 0.8 %copy-start.1 = (f32[1,2,4,16384]{3,2,1,0:T(4,128)}, f32[1,2,4,16384]{3,2,1,0:T(4,128)S(1)}, u32[]{:S(2)}) copy-start(f32[1,2,4,16384]{3,2,1,0:T(4,128)S(1)} %collective-permute-done.peer_hbm) | copy-start | bytes 1572868
  32.0 32.5 %all-to-all-start = ((f32[128,24,128]{2,1,0:T(8,128)}), f32[128,24,128]{2,1,0:T(8,128)S(1)}, u32[]{:S(2)}, u32[]{:S(2)}) async-start(f32[128,24,128]{2,1,0:T(8,128)} %bitcast.9), calls=%async_computation | async-start | bytes 3145728 | tf_op jit(solution)/shard_map/all_to_all | solution.py:552
  64.5 1.2 %copy-start = (f32[128,24,128]{2,1,0:T(8,128)}, f32[128,24,128]{2,1,0:T(8,128)S(1)}, u32[]{:S(2)}) copy-start(f32[128,24,128]{2,1,0:T(8,128)S(1)} %all-to-all-done) | copy-start | bytes 4718596

commit v4 on v3

--- a/solution.py
+++ b/solution.py
@@ -83,9 +83,7 @@
     rows = []
     for span in range(16384 // SPAN):
         turn = scale * (span * SPAN + centre) * bands
-        re, im = interp * np.cos(turn), -interp * np.sin(turn)
-        rows.append(np.concatenate([re, im], 1))
-        rows.append(np.concatenate([-im, re], 1))
+        rows += [interp * np.cos(turn), interp * np.sin(turn)]
     weave = np.concatenate(rows, 0)
     weave_hi, weave_lo = _split(weave)
     turn = TWO_PI * ((np.arange(16)[:, None] * (bands[None, :half] % 256)) % 256) / 256
@@ -121,7 +119,7 @@
 
 
 def _prepare(slot, half, order_ref, offsets_ref, cols_ref, rows_ref, band_ref,
-             lc_ref, ls_ref, pc_ref, ps_ref, mc_ref, ms_ref, combine_ref, wc_ref, ws_ref):
+             lc_ref, ls_ref, pc_ref, ps_ref, mc_ref, ms_ref, combine_ref):
     cf_row = _offset_row(order_ref, offsets_ref, 0)
     own_cf = _pick(cf_row, slot).astype(jnp.int32)
     cf = _to_column(cf_row).astype(jnp.int32)
@@ -156,20 +154,18 @@
     power = jnp.ones((64, 128), f32)
     first = lax.bitwise_and(lane, 4) == 0
     to_re, to_im = jnp.where(first, mc, ms), jnp.where(first, -ms, mc)
-    for n in range(RANK):
-        wc_ref[n] = mc * power
-        ws_ref[n] = ms * power
-        if n < ERANK:
-            for part, value in ((0, to_re), (1, to_im)):
-                base = part * 128 + n * 64
-                combine_ref[base:base + 64, :] = (value * power)[:, COL_ROW:COL_ROW + 16].astype(bf16)
+    for n in range(ERANK):
+        for part, value in ((0, to_re), (1, to_im)):
+            base = part * 128 + n * 64
+            combine_ref[base:base + 64, :] = (value * power)[:, COL_ROW:COL_ROW + 16].astype(bf16)
         power = power * rho
 
 
 def _exact_kernel(order_hbm, offsets_hbm, cols_hbm, rows_hbm, band_hbm, data_hbm, window_hbm, sample_hbm,
-                  lc_ref, ls_ref, pc_ref, ps_ref, mc_ref, ms_ref, combine_ref, out_ref,
+                  lc_hbm, ls_hbm, pc_hbm, ps_hbm, mc_hbm, ms_hbm, combine_hbm, out_ref,
                   order_ref, offsets_ref, cols_ref, rows_ref, band_ref, data_ref, window_ref, sample_ref,
-                  wc_ref, ws_ref, even_ref, odd_ref, acc_ref, sems):
+                  lc_ref, ls_ref, pc_ref, ps_ref, mc_ref, ms_ref, combine_ref,
+                  even_ref, odd_ref, acc_ref, sems, out_sems):
     loads = [
         pltpu.make_async_copy(source, target, sems.at[i])
         for i, (source, target) in enumerate((
@@ -183,7 +179,16 @@
         load.wait()
     acc_ref[...] = jnp.zeros_like(acc_ref)
     _prepare(lax.axis_index("facet"), lax.axis_index("rows"), order_ref, offsets_ref, cols_ref, rows_ref, band_ref,
-             lc_ref, ls_ref, pc_ref, ps_ref, mc_ref, ms_ref, combine_ref, wc_ref, ws_ref)
+             lc_ref, ls_ref, pc_ref, ps_ref, mc_ref, ms_ref, combine_ref)
+    stores = [
+        pltpu.make_async_copy(source, target, out_sems.at[i])
+        for i, (source, target) in enumerate((
+            (lc_ref, lc_hbm), (ls_ref, ls_hbm), (pc_ref, pc_hbm), (ps_ref, ps_hbm), (mc_ref, mc_hbm), (ms_ref, ms_hbm),
+            (combine_ref, combine_hbm),
+        ))
+    ]
+    for store in stores:
+        store.start()
     for load in loads[5:]:
         load.wait()
 
@@ -210,14 +215,12 @@
 
     def stage(block, x_ref, following, next_ref):
         bc, bs = turns(following)
-        rows = pl.ds(pl.multiple_of(lax.rem(block, 4) * BLOCK, BLOCK), BLOCK)
         span = block // 4
-        for p in range(2):
-            half = slice(p * 256, (p + 1) * 256)
-            part = jnp.dot(x_ref[half, :], sample_ref[rows, :], preferred_element_type=f32)
-            build(following, next_ref, bc, bs, 2 * p)
-            build(following, next_ref, bc, bs, 2 * p + 1)
-            acc_ref[span, half, :] = acc_ref[span, half, :] + part
+        for i in range(4):
+            rows = pl.ds(pl.multiple_of(lax.rem(block, 4) * BLOCK + i * 256, 256), 256)
+            part = jnp.dot(x_ref[:, i * 256:(i + 1) * 256], sample_ref[rows, :], preferred_element_type=f32)
+            build(following, next_ref, bc, bs, i)
+            acc_ref[span] = acc_ref[span] + part
 
     bc, bs = turns(0)
     for i in range(4):
@@ -230,34 +233,48 @@
 
     lax.fori_loop(0, 8, body, 0)
 
+    first = lax.broadcasted_iota(jnp.int32, (64, 128), 1) < 64
     lane = lax.broadcasted_iota(jnp.int32, (64, 128), 1)
     sign = jnp.where(lax.bitwise_and(lane, 32) == 0, -1.0, 1.0).astype(f32)
-    sums = [[None] * 4 for _ in range(RANK)]
-    for span in range(4):
-        for r in range(4):
-            re = acc_ref[span, r * 64:(r + 1) * 64]
-            im = acc_ref[span, 256 + r * 64:256 + (r + 1) * 64]
-            re = re + pltpu.roll(re, 64, 1)
-            im = im + pltpu.roll(im, 64, 1)
-            value = re + sign * pltpu.roll(im, 32, 1)
-            turned = sign * pltpu.roll(value, 32, 1)
-            for n in range(RANK):
-                col = slice(COL_ROW + r, COL_ROW + r + 1)
-                term = wc_ref[n, :, col] * value - ws_ref[n, :, col] * turned
-                sums[n][span] = term if sums[n][span] is None else sums[n][span] + term
-    for n in range(RANK):
-        out_ref[:, n * 256:n * 256 + 128] = jnp.where(lane < 64, sums[n][0], sums[n][1])
-        out_ref[:, n * 256 + 128:n * 256 + 256] = jnp.where(lane < 64, sums[n][2], sums[n][3])
-
-
-def _residual_kernel(own_hbm, peer_hbm, window_hbm, lc_hbm, ls_hbm, mc_hbm, ms_hbm, combine_hbm,
+    half = lax.axis_index("rows")
+    places = [(8 * half + 2 * r - 7).astype(f32) * (0.5 / ROW_SCALE) for r in range(4)]
+    spins = [
+        [jnp.broadcast_to(ref[:, COL_ROW + r:COL_ROW + r + 1], (64, 128)) for ref in (mc_ref, ms_ref)] for r in range(4)
+    ]
+    for pair in range(2):
+        sums = []
+        for span in (2 * pair, 2 * pair + 1):
+            direct, across = [None] * RANK, [None] * RANK
+            for r in range(4):
+                c, s = spins[r]
+                re = acc_ref[span, r * 64:(r + 1) * 64]
+                im = acc_ref[span, 256 + r * 64:256 + (r + 1) * 64]
+                one, two = c * re + s * im, c * im - s * re
+                for n in range(RANK):
+                    direct[n] = one if r == 0 else direct[n] + one
+                    across[n] = two if r == 0 else across[n] + two
+                    one, two = one * places[r], two * places[r]
+            sums.append((direct, across))
+        for n in range(RANK):
+            folded = []
+            for which in range(2):
+                a, b = sums[0][which][n], sums[1][which][n]
+                folded.append(jnp.where(first, a, b) + pltpu.roll(jnp.where(first, b, a), 64, 1))
+            at = n * 256 + pair * 128
+            out_ref[:, at:at + 128] = folded[0] + jnp.where(
+                sign < 0, -pltpu.roll(folded[1], 96, 1), pltpu.roll(folded[1], 32, 1))
+    for store in stores:
+        store.wait()
+
+
+def _residual_kernel(own_hbm, peer_any, window_hbm, lc_hbm, ls_hbm, mc_hbm, ms_hbm, combine_hbm,
                      table_hbm, tc_hbm, ts_hbm, nodes_hbm, out_ref,
                      own_ref, peer_ref, window_ref, lc_ref, ls_ref, mc_ref, ms_ref, combine_ref,
-                     table_ref, tc_ref, ts_ref, nodes_ref, even_ref, odd_ref, sum_ref, sems):
+                     table_ref, tc_ref, ts_ref, nodes_ref, cos_ref, sin_ref, even_ref, odd_ref, sum_ref, sems):
     loads = [
         pltpu.make_async_copy(source, target, sems.at[i])
         for i, (source, target) in enumerate((
-            (own_hbm, own_ref), (peer_hbm, peer_ref), (window_hbm, window_ref), (lc_hbm, lc_ref), (ls_hbm, ls_ref),
+            (own_hbm, own_ref), (peer_any, peer_ref), (window_hbm, window_ref), (lc_hbm, lc_ref), (ls_hbm, ls_ref),
             (mc_hbm, mc_ref), (ms_hbm, ms_ref), (combine_hbm, combine_ref),
             (table_hbm.at[lax.axis_index("rows")], table_ref), (tc_hbm, tc_ref), (ts_hbm, ts_ref),
             (nodes_hbm, nodes_ref),
@@ -280,6 +297,8 @@
     scale_out = largest * (1.0 / (DATA_SCALE * TABLE_SCALE))
     for load in loads[3:8]:
         load.wait()
+    cos_ref[...] = lc_ref[...].astype(bf16)
+    sin_ref[...] = ls_ref[...].astype(bf16)
 
     def mix(block, i):
         here = pl.ds(pl.multiple_of(block * BLOCK + i * 256, 256), 256)
@@ -291,9 +310,10 @@
 
     def build(z_ref, j, i, rows, bc, bs):
         cols = slice(i * 256, (i + 1) * 256)
-        lc, ls = lc_ref[:, cols], ls_ref[:, cols]
+        lc, ls = cos_ref[:, cols], sin_ref[:, cols]
         ec = bc * lc - bs * ls
         es = bs * lc + bc * ls
+        rows = rows.astype(bf16)
         for n in range(ERANK):
             gr, gi = rows[n * 64:(n + 1) * 64], rows[128 + n * 64:128 + (n + 1) * 64]
             at = j * 256 + n * 64
@@ -301,7 +321,9 @@
             z_ref[at + 128:at + 192, cols] = (gi * ec - gr * es).astype(z_ref.dtype)
 
     def turns(block):
-        return _pick(mc_ref[...], block), _pick(ms_ref[...], block)
+        return tuple(
+            jnp.broadcast_to(_pick(ref[...], block), (64, 256)).astype(bf16) for ref in (mc_ref, ms_ref)
+        )
 
     def stage(group, z_ref, following, next_ref):
         tasks = [(j, i) for j in range(2) for i in range(4)]
@@ -414,6 +436,7 @@
     for load in loads:
         load.start()
     loads[0].wait()
+    second = lax.bitwise_and(lax.broadcasted_iota(jnp.int32, (64, 128), 1), 32) != 0
     for n in range(RANK):
         for i in range(2):
             chunk = 16 + n * 2 + i
@@ -422,21 +445,24 @@
                 + got_ref[pl.ds(CHUNKS + chunk, 64, stride=2 * CHUNKS), :]
             )
             high, low = _halves(value)
-            high_ref[n * 64:(n + 1) * 64, i * 128:(i + 1) * 128] = high
-            if n < 2:
-                low_ref[n * 64:(n + 1) * 64, i * 128:(i + 1) * 128] = low
+            for part in range(2):
+                high_ref[part, n * 64:(n + 1) * 64, i * 128:(i + 1) * 128] = high.astype(bf16)
+                if n < 2:
+                    low_ref[part, n * 64:(n + 1) * 64, i * 128:(i + 1) * 128] = low.astype(bf16)
+                high, low = (
+                    jnp.where(second, -pltpu.roll(v.astype(f32), 32, 1), pltpu.roll(v.astype(f32), 96, 1)) for v in (high, low)
+                )
     for load in loads[1:5]:
         load.wait()
     for i in range(4):
         cols = slice(i * 256, (i + 1) * 256)
         vals = []
         for part in range(2):
-            wcols = slice(part * 1024 + i * 256, part * 1024 + (i + 1) * 256)
-            wh, wl = wh_ref[:, wcols], wl_ref[:, wcols]
-            main = jnp.dot(high_ref[...], wh, preferred_element_type=f32)
+            wh, wl = wh_ref[:, cols], wl_ref[:, cols]
+            main = jnp.dot(high_ref[part], wh, preferred_element_type=f32)
             rest = (
-                jnp.dot(high_ref[0:128], wl, preferred_element_type=f32)
-                + jnp.dot(low_ref[...], wh, preferred_element_type=f32)
+                jnp.dot(high_ref[part, 0:128], wl, preferred_element_type=f32)
+                + jnp.dot(low_ref[part], wh, preferred_element_type=f32)
             )
             vals.append((main, rest))
         pc, ps = pc_ref[:, cols], ps_ref[:, cols]
@@ -514,14 +540,17 @@
     lc, ls, pc, ps, mc, ms, combine, nodes = pl.pallas_call(
         _exact_kernel,
         in_specs=[hbm] * 8,
+        out_specs=[hbm] * 7 + [vmem],
         out_shape=[wide, wide, wide, wide, narrow, narrow, shape((256, 16), bf16), wide],
         scratch_shapes=[
             pltpu.VMEM((1, 64), jnp.int32), pltpu.VMEM((2, 64), jnp.int32), pltpu.VMEM((1, 64), jnp.int32),
             pltpu.VMEM((1, 64), jnp.int32), pltpu.VMEM((1, M), f32), pltpu.VMEM((1, 2, 4, 16384), f32),
             pltpu.VMEM((1, 16384), f32), pltpu.VMEM((SPAN, 128), bf16),
-            pltpu.VMEM((RANK, 64, 128), f32), pltpu.VMEM((RANK, 64, 128), f32),
+            pltpu.VMEM((64, 1024), f32), pltpu.VMEM((64, 1024), f32), pltpu.VMEM((64, 1024), f32),
+            pltpu.VMEM((64, 1024), f32), pltpu.VMEM((64, 128), f32), pltpu.VMEM((64, 128), f32),
+            pltpu.VMEM((256, 16), bf16),
             pltpu.VMEM((512, BLOCK), bf16), pltpu.VMEM((512, BLOCK), bf16), pltpu.VMEM((4, 512, 128), f32),
-            pltpu.SemaphoreType.DMA((8,)),
+            pltpu.SemaphoreType.DMA((8,)), pltpu.SemaphoreType.DMA((7,)),
         ],
         compiler_params=params(60),
         cost_estimate=pl.CostEstimate(flops=8 * 10**9, bytes_accessed=2 * 10**6, transcendentals=0),
@@ -537,7 +566,7 @@
             pltpu.VMEM((64, 1024), f32), pltpu.VMEM((64, 1024), f32), pltpu.VMEM((64, 128), f32),
             pltpu.VMEM((64, 128), f32), pltpu.VMEM((256, 16), bf16),
             pltpu.VMEM((1024, 1024), f8), pltpu.VMEM((16, 512), f32), pltpu.VMEM((16, 512), f32),
-            pltpu.VMEM((64, 1024), f32),
+            pltpu.VMEM((64, 1024), f32), pltpu.VMEM((64, 1024), bf16), pltpu.VMEM((64, 1024), bf16),
             pltpu.VMEM((512, 1024), f8), pltpu.VMEM((512, 1024), f8), pltpu.VMEM((2, 128, 512), f32),
             pltpu.SemaphoreType.DMA((12,)),
         ],
@@ -566,10 +595,10 @@
         out_specs=hbm,
         out_shape=shape((1, 2, 512, 1024), f32),
         scratch_shapes=[
-            pltpu.VMEM((128 * CHUNKS, 128), f32), pltpu.VMEM((256, 2048), bf16), pltpu.VMEM((256, 2048), bf16),
+            pltpu.VMEM((128 * CHUNKS, 128), f32), pltpu.VMEM((256, 1024), bf16), pltpu.VMEM((256, 1024), bf16),
             pltpu.VMEM((64, 1024), f32), pltpu.VMEM((64, 1024), f32), pltpu.VMEM((512, 1024), bf16),
             pltpu.VMEM((512, 1024), bf16), pltpu.VMEM((1024, 2048), bf16), pltpu.VMEM((512, 1024), f32),
-            pltpu.VMEM((256, 256), bf16), pltpu.VMEM((128, 256), bf16), pltpu.VMEM((2, 512, 1024), f32),
+            pltpu.VMEM((2, 256, 256), bf16), pltpu.VMEM((2, 128, 256), bf16), pltpu.VMEM((2, 512, 1024), f32),
             pltpu.SemaphoreType.DMA((7,)), pltpu.SemaphoreType.DMA((8,)),
         ],
         compiler_params=params(60),

time: 74.2 us -> 72.8 us (0.981)
  Pallas kernels: 42.6 us -> 38.6 us
  starting transfers between devices: 12.6 us -> 15 us
    pallas_call x1, Pallas kernels: 14.3 us -> 11.8 us  [per_device(): pl.pallas_call(_exact_kernel, in_specs=[hbm] * 8, out_specs=[hbm] * 7 + [...]
    all_to_all x1, starting transfers between devices: 8.14 us -> 10.6 us  [per_device(): lax.all_to_all(send.reshape(128, CHUNKS, 128), ('facet', 'rows'), split_a...]
    pallas_call x1, Pallas kernels: 12.5 us -> 11.4 us  [per_device(): pl.pallas_call(_residual_kernel, in_specs=[hbm, anywhere] + [hbm] * 10, o...]
  transfers between devices with their start and end apart: 2 -> 2, of which waited for: 1 -> 2; matrix products, arithmetic and copies ran while one was open for 0% -> 0% of each run, Pallas kernels for 30% -> 27%
where the time goes in v4:
time: 72.8 us; the launch traced here: 72.6 us
  Pallas kernels  38.6 us (53%)
  waiting for transfers between devices  16.8 us (23%)
  starting transfers between devices  15 us (21%)
  local copies, waits for them, and re-layouts  1.95 us (3%)
    all_to_all x1, waiting for transfers between devices, per_device(): lax.all_to_all(send.reshape(128, CHUNKS, 128), ('facet', 'rows'), split_a...  16.7 us
    pallas_call x1, Pallas kernels, per_device(): pl.pallas_call(_exact_kernel, in_specs=[hbm] * 8, out_specs=[hbm] * 7 + [...  11.8 us
    pallas_call x1, Pallas kernels, per_device(): pl.pallas_call(_residual_kernel, in_specs=[hbm, anywhere] + [hbm] * 10, o...  11.4 us
    all_to_all x1, starting transfers between devices, per_device(): lax.all_to_all(send.reshape(128, CHUNKS, 128), ('facet', 'rows'), split_a...  10.6 us
    pallas_call x1, Pallas kernels, per_device(): pl.pallas_call(_rows_kernel, in_specs=[anywhere] + [hbm] * 6, out_specs=h...  7.81 us
    pallas_call x1, Pallas kernels, per_device(): pl.pallas_call(_phase_kernel, in_specs=[vmem] * 3, out_shape=[shape((512,...  7.6 us
    ppermute x1, starting transfers between devices, per_device(): peer = lax.ppermute(facets, 'rows', [(0, 1), (1, 0)])  4.43 us
    unnamed x4, local copies, waits for them, and re-layouts  1.95 us
  transfers between devices with their start and end apart: 2, of which 2 were waited for; matrix products, arithmetic and copies ran while one was open for 0% of the time, Pallas kernels for 27%

profile of v4, /device:TPU:1, one launch (start us, length us, event | category | flops | bytes accessed | tf_op | source)
XLA Modules:
  0.0 72.6 jit_solution(7942803007501328237)
XLA Ops:
  0.0 4.4 %collective-permute-start = (f32[1,2,4,16384]{3,2,1,0:T(4,128)}, f32[1,2,4,16384]{3,2,1,0:T(4,128)S(1)}, u32[]{:S(2)}, u32[]{:S(2)}) collective-permute-start(f32[1,2,4,16384]{3,2,1,0:T(4,128)} %own_hbm.1), channel_id=1, source_target_pairs={{0,1},{1,0},{2,3},{3,2},{4,5},{5,4},{6,7},{7,6},{8,9},{9,8},{10,11... | collective-permute-start | bytes 1572872 | tf_op jit(solution)/shard_map/ppermute | solution.py:527
  4.4 11.8 %exact_part.1 = (f32[64,1024]{1,0:T(8,128)}, f32[64,1024]{1,0:T(8,128)}, f32[64,1024]{1,0:T(8,128)}, f32[64,1024]{1,0:T(8,128)}, f32[64,128]{1,0:T(8,128)}, /*in...) custom-call(s32[1,64]{1,0:T(1,128)} %bitcast.16, s32[2,64]{1,0:T(2,128)} %bitcast.13, ...), custom_call_target="tpu_custom_call" | custom-call | flops 8000000000 | bytes 2000000 | tf_op jit(solution)/shard_map/exact_part/pallas_call | solution.py:540
  16.2 0.1 collective-permute-done.peer_any
  16.3 0.0 copy-start.1
  16.3 0.8 %copy-done.1 = f32[1,2,4,16384]{3,2,1,0:T(4,128)} copy-done((f32[1,2,4,16384]{3,2,1,0:T(4,128)}, f32[1,2,4,16384]{3,2,1,0:T(4,128)S(1)}, u32[]{:S(2)}) %copy-start.1) | copy-done | bytes 524312
  17.1 11.4 %residual_part.1 = f32[3072,128]{1,0:T(8,128)} custom-call(f32[1,2,4,16384]{3,2,1,0:T(4,128)} %own_hbm.1, f32[1,2,4,16384]{3,2,1,0:T(4,128)} %copy-done.1, f32[1,16384]{1,0:T(1,128)} %bitcast.11, f32[64,1024]{1,0:T(8,128)} %get-tuple-element.15.lc_hbm, f32[64,1024]{1,0:T(8,128)} %get-tuple-element.16.ls_hbm, f32[64,128]{1,0:T(8,128)} %get-tuple-element.17.mc_hbm, ...), custom_call_target="tpu_custom_call" | custom-call | flops 8999999488 | bytes 4000000 | tf_op jit(solution)/shard_map/residual_part/pallas_call | solution.py:560
  28.5 10.6 %all-to-all-start = ((f32[128,24,128]{2,1,0:T(8,128)}), f32[128,24,128]{2,1,0:T(8,128)S(1)}, u32[]{:S(2)}, u32[]{:S(2)}) async-start(f32[128,24,128]{2,1,0:T(8,128)} %bitcast.9), calls=%async_computation | async-start | bytes 3145728 | tf_op jit(solution)/shard_map/all_to_all | solution.py:581
  39.1 7.6 %row_phases.1 = (bf16[512,1024]{1,0:T(8,128)(2,1)}, bf16[512,1024]{1,0:T(8,128)(2,1)}) custom-call(s32[1,64]{1,0:T(1,128)} %bitcast.17, s32[2,64]{1,0:T(2,128)} %bitcast.14, s32[1,64]{1,0:T(1,128)} %bitcast.19), custom_call_target="tpu_custom_call" | custom-call | flops 3000000000 | bytes 2000000 | tf_op jit(solution)/shard_map/row_phases/pallas_call | solution.py:582
  46.7 16.7 %all-to-all-done = f32[128,24,128]{2,1,0:T(8,128)S(1)} async-done(((f32[128,24,128]{2,1,0:T(8,128)}), f32[128,24,128]{2,1,0:T(8,128)S(1)}, u32[]{:S(2)}, u32[]{:S(2)}) %all-to-all-start) | async-done | bytes 1572896 | tf_op jit(solution)/shard_map/all_to_all | solution.py:581
  63.5 0.0 copy-start
  63.5 1.2 %copy-done = f32[128,24,128]{2,1,0:T(8,128)} copy-done((f32[128,24,128]{2,1,0:T(8,128)}, f32[128,24,128]{2,1,0:T(8,128)S(1)}, u32[]{:S(2)}) %copy-start) | copy-done | bytes 1572888
  64.6 7.8 %row_transform.1 = f32[1,2,512,1024]{3,2,1,0:T(8,128)} custom-call(f32[3072,128]{1,0:T(8,128)} %bitcast.8, bf16[256,1024]{1,0:T(8,128)(2,1)} %constant.16.clone.wh_hbm, bf16[256,1024]{1,0:T(8,128)(2,1)} %constant.17.clone.wl_hbm, f32[64,1024]{1,0:T(8,128)} %get-tuple-element.21.pc_hbm, f32[64,1024]{1,0:T(8,128)} %get-tuple-element.22.ps_hbm, ...), custom_call_target="tpu_custom_call" | custom-call | flops 5000000000 | bytes 12000000 | tf_op jit(solution)/shard_map/row_transform/pallas_call | solution.py:592
Async XLA Ops:
  0.0 16.3 %collective-permute-start = (f32[1,2,4,16384]{3,2,1,0:T(4,128)}, f32[1,2,4,16384]{3,2,1,0:T(4,128)S(1)}, u32[]{:S(2)}, u32[]{:S(2)}) collective-permute-start(f32[1,2,4,16384]{3,2,1,0:T(4,128)} %own_hbm.1), channel_id=1, source_target_pairs={{0,1},{1,0},{2,3},{3,2},{4,5},{5,4},{6,7},{7,6},{8,9},{9,8},{10,11... | collective-permute-start | bytes 1572872 | tf_op jit(solution)/shard_map/ppermute | solution.py:527
  16.3 0.8 %copy-start.1 = (f32[1,2,4,16384]{3,2,1,0:T(4,128)}, f32[1,2,4,16384]{3,2,1,0:T(4,128)S(1)}, u32[]{:S(2)}) copy-start(f32[1,2,4,16384]{3,2,1,0:T(4,128)S(1)} %collective-permute-done.peer_any) | copy-start | bytes 1572868
  28.5 34.9 %all-to-all-start = ((f32[128,24,128]{2,1,0:T(8,128)}), f32[128,24,128]{2,1,0:T(8,128)S(1)}, u32[]{:S(2)}, u32[]{:S(2)}) async-start(f32[128,24,128]{2,1,0:T(8,128)} %bitcast.9), calls=%async_computation | async-start | bytes 3145728 | tf_op jit(solution)/shard_map/all_to_all | solution.py:581
  63.5 1.2 %copy-start = (f32[128,24,128]{2,1,0:T(8,128)}, f32[128,24,128]{2,1,0:T(8,128)S(1)}, u32[]{:S(2)}) copy-start(f32[128,24,128]{2,1,0:T(8,128)S(1)} %all-to-all-done) | copy-start | bytes 4718596

commit v5 on v4

--- a/solution.py
+++ b/solution.py
@@ -19,6 +19,7 @@
 SPAN = 4096
 NODES = 32
 RANK = 4
+OWN_RANK = 3
 ERANK = 2
 ROW_SCALE = 4.0
 TABLE_SCALE = 32768.0
@@ -94,7 +95,7 @@
 
 
 COL_A, COL_SC8, COL_CF8, COL_ROW = 0, 16, 24, 32
-CHUNKS = 24
+CHUNKS = 22
 
 
 def _angle(product):
@@ -164,7 +165,7 @@
 def _exact_kernel(order_hbm, offsets_hbm, cols_hbm, rows_hbm, band_hbm, data_hbm, window_hbm, sample_hbm,
                   lc_hbm, ls_hbm, pc_hbm, ps_hbm, mc_hbm, ms_hbm, combine_hbm, out_ref,
                   order_ref, offsets_ref, cols_ref, rows_ref, band_ref, data_ref, window_ref, sample_ref,
-                  lc_ref, ls_ref, pc_ref, ps_ref, mc_ref, ms_ref, combine_ref,
+                  lc_ref, ls_ref, lc16_ref, ls16_ref, pc_ref, ps_ref, mc_ref, ms_ref, combine_ref,
                   even_ref, odd_ref, acc_ref, sems, out_sems):
     loads = [
         pltpu.make_async_copy(source, target, sems.at[i])
@@ -180,10 +181,12 @@
     acc_ref[...] = jnp.zeros_like(acc_ref)
     _prepare(lax.axis_index("facet"), lax.axis_index("rows"), order_ref, offsets_ref, cols_ref, rows_ref, band_ref,
              lc_ref, ls_ref, pc_ref, ps_ref, mc_ref, ms_ref, combine_ref)
+    lc16_ref[...] = lc_ref[...].astype(bf16)
+    ls16_ref[...] = ls_ref[...].astype(bf16)
     stores = [
         pltpu.make_async_copy(source, target, out_sems.at[i])
         for i, (source, target) in enumerate((
-            (lc_ref, lc_hbm), (ls_ref, ls_hbm), (pc_ref, pc_hbm), (ps_ref, ps_hbm), (mc_ref, mc_hbm), (ms_ref, ms_hbm),
+            (lc16_ref, lc_hbm), (ls16_ref, ls_hbm), (pc_ref, pc_hbm), (ps_ref, ps_hbm), (mc_ref, mc_hbm), (ms_ref, ms_hbm),
             (combine_ref, combine_hbm),
         ))
     ]
@@ -236,26 +239,25 @@
     first = lax.broadcasted_iota(jnp.int32, (64, 128), 1) < 64
     lane = lax.broadcasted_iota(jnp.int32, (64, 128), 1)
     sign = jnp.where(lax.bitwise_and(lane, 32) == 0, -1.0, 1.0).astype(f32)
-    half = lax.axis_index("rows")
-    places = [(8 * half + 2 * r - 7).astype(f32) * (0.5 / ROW_SCALE) for r in range(4)]
+    places = [(r - 1.5) / ROW_SCALE for r in range(4)]
     spins = [
         [jnp.broadcast_to(ref[:, COL_ROW + r:COL_ROW + r + 1], (64, 128)) for ref in (mc_ref, ms_ref)] for r in range(4)
     ]
     for pair in range(2):
         sums = []
         for span in (2 * pair, 2 * pair + 1):
-            direct, across = [None] * RANK, [None] * RANK
+            direct, across = [None] * OWN_RANK, [None] * OWN_RANK
             for r in range(4):
                 c, s = spins[r]
                 re = acc_ref[span, r * 64:(r + 1) * 64]
                 im = acc_ref[span, 256 + r * 64:256 + (r + 1) * 64]
                 one, two = c * re + s * im, c * im - s * re
-                for n in range(RANK):
+                for n in range(OWN_RANK):
                     direct[n] = one if r == 0 else direct[n] + one
                     across[n] = two if r == 0 else across[n] + two
                     one, two = one * places[r], two * places[r]
             sums.append((direct, across))
-        for n in range(RANK):
+        for n in range(OWN_RANK):
             folded = []
             for which in range(2):
                 a, b = sums[0][which][n], sums[1][which][n]
@@ -270,7 +272,7 @@
 def _residual_kernel(own_hbm, peer_any, window_hbm, lc_hbm, ls_hbm, mc_hbm, ms_hbm, combine_hbm,
                      table_hbm, tc_hbm, ts_hbm, nodes_hbm, out_ref,
                      own_ref, peer_ref, window_ref, lc_ref, ls_ref, mc_ref, ms_ref, combine_ref,
-                     table_ref, tc_ref, ts_ref, nodes_ref, cos_ref, sin_ref, even_ref, odd_ref, sum_ref, sems):
+                     table_ref, tc_ref, ts_ref, nodes_ref, even_ref, odd_ref, sum_ref, sems):
     loads = [
         pltpu.make_async_copy(source, target, sems.at[i])
         for i, (source, target) in enumerate((
@@ -297,8 +299,6 @@
     scale_out = largest * (1.0 / (DATA_SCALE * TABLE_SCALE))
     for load in loads[3:8]:
         load.wait()
-    cos_ref[...] = lc_ref[...].astype(bf16)
-    sin_ref[...] = ls_ref[...].astype(bf16)
 
     def mix(block, i):
         here = pl.ds(pl.multiple_of(block * BLOCK + i * 256, 256), 256)
@@ -310,7 +310,7 @@
 
     def build(z_ref, j, i, rows, bc, bs):
         cols = slice(i * 256, (i + 1) * 256)
-        lc, ls = cos_ref[:, cols], sin_ref[:, cols]
+        lc, ls = lc_ref[:, cols], ls_ref[:, cols]
         ec = bc * lc - bs * ls
         es = bs * lc + bc * ls
         rows = rows.astype(bf16)
@@ -327,8 +327,10 @@
 
     def stage(group, z_ref, following, next_ref):
         tasks = [(j, i) for j in range(2) for i in range(4)]
-        spins = [turns(following * 2 + j) for j in range(2)]
-        ready = mix(following * 2, 0)
+        building = following is not None
+        if building:
+            spins = [turns(following * 2 + j) for j in range(2)]
+            ready = mix(following * 2, 0)
         at = 0
         for j in range(2):
             for kc in range(2):
@@ -336,7 +338,7 @@
                 z = z_ref[j * 256:(j + 1) * 256, :]
                 by_c = jnp.dot(z, table_ref[:, cols], preferred_element_type=f32)
                 by_s = jnp.dot(z, table_ref[:, 512 + kc * 256:768 + kc * 256], preferred_element_type=f32)
-                for _ in range(2):
+                for _ in range(2 if building else 0):
                     bj, bi = tasks[at]
                     at += 1
                     coming = mix(following * 2 + tasks[at][0], tasks[at][1]) if at < 8 else None
@@ -358,13 +360,15 @@
 
     def body(pair, carry):
         stage(2 * pair, even_ref, 2 * pair + 1, odd_ref)
-        stage(2 * pair + 1, odd_ref, lax.rem(2 * pair + 2, 8), even_ref)
+        stage(2 * pair + 1, odd_ref, 2 * pair + 2, even_ref)
         return carry
 
-    lax.fori_loop(0, 4, body, 0)
+    lax.fori_loop(0, 3, body, 0)
+    stage(6, even_ref, 7, odd_ref)
+    stage(7, odd_ref, None, None)
 
     for copy in range(2):
-        for i in range(8):
+        for i in range(CHUNKS - 16):
             out_ref[pl.ds(copy * CHUNKS + 16 + i, 64, stride=2 * CHUNKS), :] = nodes_ref[:, i * 128:(i + 1) * 128]
         for n in range(ERANK):
             for part in range(2):
@@ -380,7 +384,8 @@
     return high, (value - high.astype(f32)).astype(bf16)
 
 
-def _phase_kernel(order_ref, offsets_ref, rows_ref, left_ref, gram_ref, all_ref, turned_ref):
+def _phase_kernel(order_ref, offsets_ref, rows_ref, out_ref, all_ref, turned_ref):
+    left_ref, gram_ref = out_ref.at[0:512], out_ref.at[512:1024]
     slot, half = lax.axis_index("facet"), lax.axis_index("rows")
     rf = _offset_row(order_ref, offsets_ref, 1).astype(jnp.int32)
     own_sr = _pick(rows_ref[...].astype(f32), slot).astype(jnp.int32)
@@ -423,35 +428,43 @@
     gram_ref[:, 768:1024] = high[:, 256:512]
 
 
-def _rows_kernel(got_any, wh_hbm, wl_hbm, pc_hbm, ps_hbm, gram_hbm, left_hbm, out_hbm,
+def _rows_kernel(got_any, wh_hbm, wl_hbm, pc_hbm, ps_hbm, phases_any, out_hbm,
                  got_ref, wh_ref, wl_ref, pc_ref, ps_ref, gram_ref, left_ref, right_ref, value_ref, high_ref, low_ref,
                  out_ref, sems, out_sems):
     loads = [
         pltpu.make_async_copy(source, target, sems.at[i])
         for i, (source, target) in enumerate((
             (got_any, got_ref), (wh_hbm, wh_ref), (wl_hbm, wl_ref), (pc_hbm, pc_ref), (ps_hbm, ps_ref),
-            (gram_hbm, gram_ref), (left_hbm, left_ref),
+            (phases_any.at[512:1024], gram_ref), (phases_any.at[0:512], left_ref),
         ))
     ]
     for load in loads:
         load.start()
     loads[0].wait()
     second = lax.bitwise_and(lax.broadcasted_iota(jnp.int32, (64, 128), 1), 32) != 0
-    for n in range(RANK):
-        for i in range(2):
-            chunk = 16 + n * 2 + i
-            value = (
-                got_ref[pl.ds(chunk, 64, stride=2 * CHUNKS), :]
-                + got_ref[pl.ds(CHUNKS + chunk, 64, stride=2 * CHUNKS), :]
-            )
-            high, low = _halves(value)
+    for i in range(2):
+        sums, diffs = [], []
+        for n in range(OWN_RANK):
+            parts = [got_ref[pl.ds(h * CHUNKS + 16 + n * 2 + i, 64, stride=2 * CHUNKS), :] for h in range(2)]
+            sums.append(parts[0] + parts[1])
+            diffs.append(parts[1] - parts[0])
+        d = 2.0 / ROW_SCALE
+        cube = 2.05 / (ROW_SCALE * ROW_SCALE)
+        terms = (
+            sums[0],
+            sums[1] + d * diffs[0],
+            sums[2] + (2 * d) * diffs[1] + (d * d) * sums[0],
+            (cube + 3 * d * d) * sums[1] + (3 * d) * diffs[2] + (d * d * d) * diffs[0],
+        )
+        cols = slice(i * 128, (i + 1) * 128)
+        for n, value in enumerate(terms):
             for part in range(2):
-                high_ref[part, n * 64:(n + 1) * 64, i * 128:(i + 1) * 128] = high.astype(bf16)
+                rows = slice(n * 64, (n + 1) * 64)
+                high, low = _halves(value)
+                high_ref[part, rows, cols] = high
                 if n < 2:
-                    low_ref[part, n * 64:(n + 1) * 64, i * 128:(i + 1) * 128] = low.astype(bf16)
-                high, low = (
-                    jnp.where(second, -pltpu.roll(v.astype(f32), 32, 1), pltpu.roll(v.astype(f32), 96, 1)) for v in (high, low)
-                )
+                    low_ref[part, rows, cols] = low
+                value = jnp.where(second, -pltpu.roll(value, 32, 1), pltpu.roll(value, 96, 1))
     for load in loads[1:5]:
         load.wait()
     for i in range(4):
@@ -536,19 +549,20 @@
     def params(mib):
         return pltpu.CompilerParams(vmem_limit_bytes=mib * 1024 * 1024)
 
-    wide, narrow = shape((64, 1024), f32), shape((64, 128), f32)
+    wide, wide16, narrow = shape((64, 1024), f32), shape((64, 1024), bf16), shape((64, 128), f32)
     lc, ls, pc, ps, mc, ms, combine, nodes = pl.pallas_call(
         _exact_kernel,
         in_specs=[hbm] * 8,
         out_specs=[hbm] * 7 + [vmem],
-        out_shape=[wide, wide, wide, wide, narrow, narrow, shape((256, 16), bf16), wide],
+        out_shape=[wide16, wide16, wide, wide, narrow, narrow, shape((256, 16), bf16),
+                   shape((64, 128 * (CHUNKS - 16)), f32)],
         scratch_shapes=[
             pltpu.VMEM((1, 64), jnp.int32), pltpu.VMEM((2, 64), jnp.int32), pltpu.VMEM((1, 64), jnp.int32),
             pltpu.VMEM((1, 64), jnp.int32), pltpu.VMEM((1, M), f32), pltpu.VMEM((1, 2, 4, 16384), f32),
             pltpu.VMEM((1, 16384), f32), pltpu.VMEM((SPAN, 128), bf16),
-            pltpu.VMEM((64, 1024), f32), pltpu.VMEM((64, 1024), f32), pltpu.VMEM((64, 1024), f32),
-            pltpu.VMEM((64, 1024), f32), pltpu.VMEM((64, 128), f32), pltpu.VMEM((64, 128), f32),
-            pltpu.VMEM((256, 16), bf16),
+            pltpu.VMEM((64, 1024), f32), pltpu.VMEM((64, 1024), f32), pltpu.VMEM((64, 1024), bf16),
+            pltpu.VMEM((64, 1024), bf16), pltpu.VMEM((64, 1024), f32), pltpu.VMEM((64, 1024), f32),
+            pltpu.VMEM((64, 128), f32), pltpu.VMEM((64, 128), f32), pltpu.VMEM((256, 16), bf16),
             pltpu.VMEM((512, BLOCK), bf16), pltpu.VMEM((512, BLOCK), bf16), pltpu.VMEM((4, 512, 128), f32),
             pltpu.SemaphoreType.DMA((8,)), pltpu.SemaphoreType.DMA((7,)),
         ],
@@ -563,10 +577,10 @@
         out_shape=shape((128 * CHUNKS, 128), f32),
         scratch_shapes=[
             pltpu.VMEM((1, 2, 4, 16384), f32), pltpu.VMEM((1, 2, 4, 16384), f32), pltpu.VMEM((1, 16384), f32),
-            pltpu.VMEM((64, 1024), f32), pltpu.VMEM((64, 1024), f32), pltpu.VMEM((64, 128), f32),
+            pltpu.VMEM((64, 1024), bf16), pltpu.VMEM((64, 1024), bf16), pltpu.VMEM((64, 128), f32),
             pltpu.VMEM((64, 128), f32), pltpu.VMEM((256, 16), bf16),
             pltpu.VMEM((1024, 1024), f8), pltpu.VMEM((16, 512), f32), pltpu.VMEM((16, 512), f32),
-            pltpu.VMEM((64, 1024), f32), pltpu.VMEM((64, 1024), bf16), pltpu.VMEM((64, 1024), bf16),
+            pltpu.VMEM((64, 128 * (CHUNKS - 16)), f32),
             pltpu.VMEM((512, 1024), f8), pltpu.VMEM((512, 1024), f8), pltpu.VMEM((2, 128, 512), f32),
             pltpu.SemaphoreType.DMA((12,)),
         ],
@@ -578,11 +592,11 @@
         jnp.asarray(tables["turn_s"]), nodes,
     )
 
-    got = lax.all_to_all(send.reshape(128, CHUNKS, 128), ("facet", "rows"), split_axis=0, concat_axis=0, tiled=True)
-    left, gram = pl.pallas_call(
+    got = lax.all_to_all(send.reshape(128, CHUNKS // 2, 2, 128), ("facet", "rows"), split_axis=0, concat_axis=0, tiled=True)
+    phases = pl.pallas_call(
         _phase_kernel,
         in_specs=[vmem] * 3,
-        out_shape=[shape((512, 1024), bf16), shape((512, 1024), bf16)],
+        out_shape=shape((1024, 1024), bf16),
         scratch_shapes=[pltpu.VMEM((2, 1024, 512), bf16), pltpu.VMEM((2, 1024, 512), bf16)],
         compiler_params=params(60),
         cost_estimate=pl.CostEstimate(flops=3 * 10**9, bytes_accessed=2 * 10**6, transcendentals=2 * 10**5),
@@ -591,7 +605,7 @@
 
     return pl.pallas_call(
         _rows_kernel,
-        in_specs=[anywhere] + [hbm] * 6,
+        in_specs=[anywhere] + [hbm] * 4 + [anywhere],
         out_specs=hbm,
         out_shape=shape((1, 2, 512, 1024), f32),
         scratch_shapes=[
@@ -604,7 +618,7 @@
         compiler_params=params(60),
         cost_estimate=pl.CostEstimate(flops=5 * 10**9, bytes_accessed=12 * 10**6, transcendentals=0),
         name="row_transform",
-    )(got.reshape(128 * CHUNKS, 128), jnp.asarray(tables["weave_hi"]), jnp.asarray(tables["weave_lo"]), pc, ps, gram, left)
+    )(got.reshape(128 * CHUNKS, 128), jnp.asarray(tables["weave_hi"]), jnp.asarray(tables["weave_lo"]), pc, ps, phases)
 
 
 def solution(mesh):

time: 72.8 us -> 70.4 us (0.967)
  waiting for transfers between devices: 16.8 us -> 15.3 us
  Pallas kernels: 38.6 us -> 37.7 us
    all_to_all x1, waiting for transfers between devices: 16.7 us -> 15.1 us  [per_device(): lax.all_to_all(send.reshape(128, CHUNKS // 2, 2, 128), ('facet', 'rows'),...]
    pallas_call x1, Pallas kernels: 11.4 us -> 10.6 us  [per_device(): pl.pallas_call(_residual_kernel, in_specs=[hbm, anywhere] + [hbm] * 10, o...]
  transfers between devices with their start and end apart: 2 -> 2, of which waited for: 2 -> 2; matrix products, arithmetic and copies ran while one was open for 0% -> 0% of each run, Pallas kernels for 27% -> 28%
where the time goes in v5:
time: 70.4 us; the launch traced here: 70.1 us
  Pallas kernels  37.7 us (54%)
  waiting for transfers between devices  15.3 us (22%)
  starting transfers between devices  15 us (21%)
  local copies, waits for them, and re-layouts  1.89 us (3%)
    all_to_all x1, waiting for transfers between devices, per_device(): lax.all_to_all(send.reshape(128, CHUNKS // 2, 2, 128), ('facet', 'rows'),...  15.1 us
    pallas_call x1, Pallas kernels, per_device(): pl.pallas_call(_exact_kernel, in_specs=[hbm] * 8, out_specs=[hbm] * 7 + [...  11.6 us
    all_to_all x1, starting transfers between devices, per_device(): lax.all_to_all(send.reshape(128, CHUNKS // 2, 2, 128), ('facet', 'rows'),...  10.6 us
    pallas_call x1, Pallas kernels, per_device(): pl.pallas_call(_residual_kernel, in_specs=[hbm, anywhere] + [hbm] * 10, o...  10.6 us
    pallas_call x1, Pallas kernels, per_device(): pl.pallas_call(_phase_kernel, in_specs=[vmem] * 3, out_shape=shape((1024,...  7.95 us
    pallas_call x1, Pallas kernels, per_device(): pl.pallas_call(_rows_kernel, in_specs=[anywhere] + [hbm] * 4 + [anywhere]...  7.59 us
    ppermute x1, starting transfers between devices, per_device(): peer = lax.ppermute(facets, 'rows', [(0, 1), (1, 0)])  4.43 us
    unnamed x4, local copies, waits for them, and re-layouts  1.89 us
  transfers between devices with their start and end apart: 2, of which 2 were waited for; matrix products, arithmetic and copies ran while one was open for 0% of the time, Pallas kernels for 28%

profile of v5, /device:TPU:1, one launch (start us, length us, event | category | flops | bytes accessed | tf_op | source)
XLA Modules:
  0.0 70.1 jit_solution(2817023085086956115)
XLA Ops:
  0.0 4.4 %collective-permute-start = (f32[1,2,4,16384]{3,2,1,0:T(4,128)}, f32[1,2,4,16384]{3,2,1,0:T(4,128)S(1)}, u32[]{:S(2)}, u32[]{:S(2)}) collective-permute-start(f32[1,2,4,16384]{3,2,1,0:T(4,128)} %own_hbm.1), channel_id=1, source_target_pairs={{0,1},{1,0},{2,3},{3,2},{4,5},{5,4},{6,7},{7,6},{8,9},{9,8},{10,11... | collective-permute-start | bytes 1572872 | tf_op jit(solution)/shard_map/ppermute | solution.py:540
  4.4 11.6 %exact_part.1 = (bf16[64,1024]{1,0:T(8,128)(2,1)}, bf16[64,1024]{1,0:T(8,128)(2,1)}, f32[64,1024]{1,0:T(8,128)}, f32[64,1024]{1,0:T(8,128)}, f32[64,128]{1,0:T(8...) custom-call(s32[1,64]{1,0:T(1,128)} %bitcast.16, s32[2,64]{1,0:T(2,128)} %bitcast.13, ...), custom_call_target="tpu_custom_call" | custom-call | flops 8000000000 | bytes 2000000 | tf_op jit(solution)/shard_map/exact_part/pallas_call | solution.py:553
  16.0 0.3 collective-permute-done.peer_any
  16.3 0.0 copy-start.1
  16.3 0.8 %copy-done.1 = f32[1,2,4,16384]{3,2,1,0:T(4,128)} copy-done((f32[1,2,4,16384]{3,2,1,0:T(4,128)}, f32[1,2,4,16384]{3,2,1,0:T(4,128)S(1)}, u32[]{:S(2)}) %copy-start.1) | copy-done | bytes 524312
  17.1 10.6 %residual_part.1 = f32[2816,128]{1,0:T(8,128)} custom-call(f32[1,2,4,16384]{3,2,1,0:T(4,128)} %own_hbm.1, f32[1,2,4,16384]{3,2,1,0:T(4,128)} %copy-done.1, f32[1,16384]{1,0:T(1,128)} %bitcast.11, bf16[64,1024]{1,0:T(8,128)(2,1)} %get-tuple-element.13.lc_hbm, bf16[64,1024]{1,0:T(8,128)(2,1)} %get-tuple-element.14.ls_hbm, f32[64,128]{1,0:T(8,128)} %get-tuple-element.15.mc_hbm, ...), custom_call_target="tpu_custom_call" | custom-call | flops 8999999488 | bytes 4000000 | tf_op jit(solution)/shard_map/residual_part/pallas_call | solution.py:574
  27.6 10.6 %all-to-all-start = ((f32[128,11,2,128]{3,2,1,0:T(2,128)}), f32[128,11,2,128]{3,2,1,0:T(2,128)S(1)}, u32[]{:S(2)}, u32[]{:S(2)}) async-start(f32[128,11,2,128]{3,2,1,0:T(2,128)} %bitcast.8), calls=%async_computation | async-start | bytes 2883584 | tf_op jit(solution)/shard_map/all_to_all | solution.py:595
  38.3 8.0 %row_phases.1.phases_any = bf16[1024,1024]{1,0:T(8,128)(2,1)} custom-call(s32[1,64]{1,0:T(1,128)} %bitcast.17, s32[2,64]{1,0:T(2,128)} %bitcast.14, s32[1,64]{1,0:T(1,128)} %bitcast.19), custom_call_target="tpu_custom_call" | custom-call | flops 3000000000 | bytes 2000000 | tf_op jit(solution)/shard_map/row_phases/pallas_call | solution.py:596
  46.2 15.1 %all-to-all-done = f32[128,11,2,128]{3,2,1,0:T(2,128)S(1)} async-done(((f32[128,11,2,128]{3,2,1,0:T(2,128)}), f32[128,11,2,128]{3,2,1,0:T(2,128)S(1)}, u32[]{:S(2)}, u32[]{:S(2)}) %all-to-all-start) | async-done | bytes 1441824 | tf_op jit(solution)/shard_map/all_to_all | solution.py:595
  61.3 0.0 copy-start
  61.3 1.1 %copy-done = f32[128,11,2,128]{3,2,1,0:T(2,128)} copy-done((f32[128,11,2,128]{3,2,1,0:T(2,128)}, f32[128,11,2,128]{3,2,1,0:T(2,128)S(1)}, u32[]{:S(2)}) %copy-start) | copy-done | bytes 1441816
  62.4 7.6 %row_transform.1 = f32[1,2,512,1024]{3,2,1,0:T(8,128)} custom-call(f32[2816,128]{1,0:T(8,128)} %bitcast.9, bf16[256,1024]{1,0:T(8,128)(2,1)} %constant.16.clone.wh_hbm, bf16[256,1024]{1,0:T(8,128)(2,1)} %constant.17.clone.wl_hbm, f32[64,1024]{1,0:T(8,128)} %get-tuple-element.19.pc_hbm, f32[64,1024]{1,0:T(8,128)} %get-tuple-element.20.ps_hbm, ...), custom_call_target="tpu_custom_call" | custom-call | flops 5000000000 | bytes 12000000 | tf_op jit(solution)/shard_map/row_transform/pallas_call | solution.py:606
Async XLA Ops:
  0.0 16.3 %collective-permute-start = (f32[1,2,4,16384]{3,2,1,0:T(4,128)}, f32[1,2,4,16384]{3,2,1,0:T(4,128)S(1)}, u32[]{:S(2)}, u32[]{:S(2)}) collective-permute-start(f32[1,2,4,16384]{3,2,1,0:T(4,128)} %own_hbm.1), channel_id=1, source_target_pairs={{0,1},{1,0},{2,3},{3,2},{4,5},{5,4},{6,7},{7,6},{8,9},{9,8},{10,11... | collective-permute-start | bytes 1572872 | tf_op jit(solution)/shard_map/ppermute | solution.py:540
  16.3 0.8 %copy-start.1 = (f32[1,2,4,16384]{3,2,1,0:T(4,128)}, f32[1,2,4,16384]{3,2,1,0:T(4,128)S(1)}, u32[]{:S(2)}) copy-start(f32[1,2,4,16384]{3,2,1,0:T(4,128)S(1)} %collective-permute-done.peer_any) | copy-start | bytes 1572868
  27.6 33.6 %all-to-all-start = ((f32[128,11,2,128]{3,2,1,0:T(2,128)}), f32[128,11,2,128]{3,2,1,0:T(2,128)S(1)}, u32[]{:S(2)}, u32[]{:S(2)}) async-start(f32[128,11,2,128]{3,2,1,0:T(2,128)} %bitcast.8), calls=%async_computation | async-start | bytes 2883584 | tf_op jit(solution)/shard_map/all_to_all | solution.py:595
  61.3 1.1 %copy-start = (f32[128,11,2,128]{3,2,1,0:T(2,128)}, f32[128,11,2,128]{3,2,1,0:T(2,128)S(1)}, u32[]{:S(2)}) copy-start(f32[128,11,2,128]{3,2,1,0:T(2,128)S(1)} %all-to-all-done) | copy-start | bytes 4325380

commit v6 on v5

--- a/solution.py
+++ b/solution.py
@@ -18,6 +18,8 @@
 BLOCK = 1024
 SPAN = 4096
 NODES = 32
+WIDTH = 16384
+ALL_NODES = 85
 RANK = 4
 OWN_RANK = 3
 ERANK = 2
@@ -73,29 +75,45 @@
         [np.concatenate([resid_c[:, h * half:(h + 1) * half], resid_s[:, h * half:(h + 1) * half]], 1) for h in range(2)]
     )
     resid = (resid * TABLE_SCALE).astype(np.float32).astype(ml_dtypes.float8_e4m3fn)
-    i = np.arange(NODES)
-    nodes = 511.5 + 512 * 1.05 * (0.25 * ((2 * i + 1) / NODES - 1) - 0.75 * np.cos(np.pi * (i + 0.5) / NODES))
-    gram = _kernel_sum(nodes[:, None] - nodes[None, :], SPAN) + 1e-13 * SPAN * np.eye(NODES)
-    interp = _solve(gram, _kernel_sum(nodes[:, None] - bands[None, :], SPAN))
+    def spread(count, width, even):
+        i = np.arange(count)
+        return 511.5 + 512 * width * (even * ((2 * i + 1) / count - 1) - (1 - even) * np.cos(np.pi * (i + 0.5) / count))
+
+    def interpolate(nodes, targets, columns):
+        gram = _kernel_sum(nodes[:, None] - nodes[None, :], columns) + 1e-13 * columns * np.eye(len(nodes))
+        return _solve(gram, _kernel_sum(nodes[:, None] - targets[None, :], columns))
+
+    nodes, all_nodes = spread(NODES, 1.05, 0.25), spread(ALL_NODES, 1.04, 0.6)
     centre = (SPAN - 1) / 2
     at = scale * (np.arange(SPAN) - centre)[:, None] * nodes[None, :]
     sample = np.concatenate([np.cos(at), -np.sin(at)], 1)
     sample = np.concatenate(_split(sample), 1)
+    middle = (WIDTH - 1) / 2
+    interp = interpolate(nodes, all_nodes, SPAN)
     rows = []
-    for span in range(16384 // SPAN):
-        turn = scale * (span * SPAN + centre) * bands
-        rows += [interp * np.cos(turn), interp * np.sin(turn)]
-    weave = np.concatenate(rows, 0)
+    for span in range(WIDTH // SPAN):
+        turn = scale * (span * SPAN + centre - middle) * all_nodes
+        re, im = interp * np.cos(turn), -interp * np.sin(turn)
+        rows += [np.concatenate([re, im], 1), np.concatenate([-im, re], 1)]
+    joined = np.concatenate(rows, 0)
+    join = np.zeros((OWN_RANK * 256, 512))
+    for n in range(OWN_RANK):
+        join[n * 256:(n + 1) * 256, n * 2 * ALL_NODES:(n + 1) * 2 * ALL_NODES] = joined
+    join_hi, join_lo = _split(join)
+    interp = interpolate(all_nodes, bands.astype(np.float64), WIDTH)
+    turn = scale * middle * bands
+    weave = np.zeros((256, M))
+    weave[:2 * ALL_NODES] = np.concatenate([interp * np.cos(turn), interp * np.sin(turn)], 0)
     weave_hi, weave_lo = _split(weave)
     turn = TWO_PI * ((np.arange(16)[:, None] * (bands[None, :half] % 256)) % 256) / 256
     return dict(
-        resid=resid, sample=sample, weave_hi=weave_hi, weave_lo=weave_lo,
+        resid=resid, sample=sample, join_hi=join_hi, join_lo=join_lo, weave_hi=weave_hi, weave_lo=weave_lo,
         turn_c=np.cos(turn).astype(np.float32), turn_s=np.sin(turn).astype(np.float32),
     )
 
 
 COL_A, COL_SC8, COL_CF8, COL_ROW = 0, 16, 24, 32
-CHUNKS = 22
+CHUNKS = 20
 
 
 def _angle(product):
@@ -162,16 +180,17 @@
         power = power * rho
 
 
-def _exact_kernel(order_hbm, offsets_hbm, cols_hbm, rows_hbm, band_hbm, data_hbm, window_hbm, sample_hbm,
+def _exact_kernel(order_hbm, offsets_hbm, cols_hbm, rows_hbm, band_hbm, data_hbm, window_hbm, sample_hbm, jh_hbm, jl_hbm,
                   lc_hbm, ls_hbm, pc_hbm, ps_hbm, mc_hbm, ms_hbm, combine_hbm, out_ref,
-                  order_ref, offsets_ref, cols_ref, rows_ref, band_ref, data_ref, window_ref, sample_ref,
+                  order_ref, offsets_ref, cols_ref, rows_ref, band_ref, data_ref, window_ref, sample_ref, jh_ref, jl_ref,
                   lc_ref, ls_ref, lc16_ref, ls16_ref, pc_ref, ps_ref, mc_ref, ms_ref, combine_ref,
-                  even_ref, odd_ref, acc_ref, sems, out_sems):
+                  even_ref, odd_ref, acc_ref, terms_ref, sems, out_sems):
     loads = [
         pltpu.make_async_copy(source, target, sems.at[i])
         for i, (source, target) in enumerate((
             (order_hbm, order_ref), (offsets_hbm, offsets_ref), (cols_hbm, cols_ref), (rows_hbm, rows_ref),
             (band_hbm, band_ref), (data_hbm, data_ref), (window_hbm, window_ref), (sample_hbm, sample_ref),
+            (jh_hbm, jh_ref), (jl_hbm, jl_ref),
         ))
     ]
     for load in loads:
@@ -192,7 +211,7 @@
     ]
     for store in stores:
         store.start()
-    for load in loads[5:]:
+    for load in loads[5:8]:
         load.wait()
 
     def build(block, x_ref, bc, bs, i):
@@ -263,8 +282,15 @@
                 a, b = sums[0][which][n], sums[1][which][n]
                 folded.append(jnp.where(first, a, b) + pltpu.roll(jnp.where(first, b, a), 64, 1))
             at = n * 256 + pair * 128
-            out_ref[:, at:at + 128] = folded[0] + jnp.where(
+            terms_ref[:, at:at + 128] = folded[0] + jnp.where(
                 sign < 0, -pltpu.roll(folded[1], 96, 1), pltpu.roll(folded[1], 32, 1))
+    for load in loads[8:]:
+        load.wait()
+    high, low = _halves(terms_ref[...])
+    out_ref[...] = (
+        jnp.dot(high, jh_ref[...], preferred_element_type=f32)
+        + (jnp.dot(high, jl_ref[...], preferred_element_type=f32) + jnp.dot(low, jh_ref[...], preferred_element_type=f32))
+    )
     for store in stores:
         store.wait()
 
@@ -441,30 +467,34 @@
     for load in loads:
         load.start()
     loads[0].wait()
-    second = lax.bitwise_and(lax.broadcasted_iota(jnp.int32, (64, 128), 1), 32) != 0
-    for i in range(2):
-        sums, diffs = [], []
-        for n in range(OWN_RANK):
-            parts = [got_ref[pl.ds(h * CHUNKS + 16 + n * 2 + i, 64, stride=2 * CHUNKS), :] for h in range(2)]
-            sums.append(parts[0] + parts[1])
-            diffs.append(parts[1] - parts[0])
-        d = 2.0 / ROW_SCALE
-        cube = 2.05 / (ROW_SCALE * ROW_SCALE)
-        terms = (
-            sums[0],
-            sums[1] + d * diffs[0],
-            sums[2] + (2 * d) * diffs[1] + (d * d) * sums[0],
-            (cube + 3 * d * d) * sums[1] + (3 * d) * diffs[2] + (d * d * d) * diffs[0],
-        )
-        cols = slice(i * 128, (i + 1) * 128)
-        for n, value in enumerate(terms):
-            for part in range(2):
-                rows = slice(n * 64, (n + 1) * 64)
-                high, low = _halves(value)
-                high_ref[part, rows, cols] = high
-                if n < 2:
-                    low_ref[part, rows, cols] = low
-                value = jnp.where(second, -pltpu.roll(value, 32, 1), pltpu.roll(value, 96, 1))
+    parts = [
+        jnp.concatenate([got_ref[pl.ds(h * CHUNKS + 16 + i, 64, stride=2 * CHUNKS), :] for i in range(4)], 1)
+        for h in range(2)
+    ]
+    both, between = parts[0] + parts[1], parts[1] - parts[0]
+    sums, diffs = [
+        [(pltpu.roll(v, 512 - n * 2 * ALL_NODES, 1) if n else v)[:, 0:256] for n in range(OWN_RANK)]
+        for v in (both, between)
+    ]
+    d = 2.0 / ROW_SCALE
+    cube = 2.05 / (ROW_SCALE * ROW_SCALE)
+    terms = (
+        sums[0],
+        sums[1] + d * diffs[0],
+        sums[2] + (2 * d) * diffs[1] + (d * d) * sums[0],
+        (cube + 3 * d * d) * sums[1] + (3 * d) * diffs[2] + (d * d * d) * diffs[0],
+    )
+    lane = lax.broadcasted_iota(jnp.int32, (64, 256), 1)
+    for n, value in enumerate(terms):
+        rows = slice(n * 64, (n + 1) * 64)
+        value = jnp.where(lane < 2 * ALL_NODES, value, 0.0)
+        for part in range(2):
+            high, low = _halves(value)
+            high_ref[part, rows, :] = high
+            if n < 2:
+                low_ref[part, rows, :] = low
+            value = jnp.where(
+                lane < ALL_NODES, pltpu.roll(value, 256 - ALL_NODES, 1), -pltpu.roll(value, ALL_NODES, 1))
     for load in loads[1:5]:
         load.wait()
     for i in range(4):
@@ -552,7 +582,7 @@
     wide, wide16, narrow = shape((64, 1024), f32), shape((64, 1024), bf16), shape((64, 128), f32)
     lc, ls, pc, ps, mc, ms, combine, nodes = pl.pallas_call(
         _exact_kernel,
-        in_specs=[hbm] * 8,
+        in_specs=[hbm] * 10,
         out_specs=[hbm] * 7 + [vmem],
         out_shape=[wide16, wide16, wide, wide, narrow, narrow, shape((256, 16), bf16),
                    shape((64, 128 * (CHUNKS - 16)), f32)],
@@ -560,16 +590,19 @@
             pltpu.VMEM((1, 64), jnp.int32), pltpu.VMEM((2, 64), jnp.int32), pltpu.VMEM((1, 64), jnp.int32),
             pltpu.VMEM((1, 64), jnp.int32), pltpu.VMEM((1, M), f32), pltpu.VMEM((1, 2, 4, 16384), f32),
             pltpu.VMEM((1, 16384), f32), pltpu.VMEM((SPAN, 128), bf16),
+            pltpu.VMEM((OWN_RANK * 256, 512), bf16), pltpu.VMEM((OWN_RANK * 256, 512), bf16),
             pltpu.VMEM((64, 1024), f32), pltpu.VMEM((64, 1024), f32), pltpu.VMEM((64, 1024), bf16),
             pltpu.VMEM((64, 1024), bf16), pltpu.VMEM((64, 1024), f32), pltpu.VMEM((64, 1024), f32),
             pltpu.VMEM((64, 128), f32), pltpu.VMEM((64, 128), f32), pltpu.VMEM((256, 16), bf16),
             pltpu.VMEM((512, BLOCK), bf16), pltpu.VMEM((512, BLOCK), bf16), pltpu.VMEM((4, 512, 128), f32),
-            pltpu.SemaphoreType.DMA((8,)), pltpu.SemaphoreType.DMA((7,)),
+            pltpu.VMEM((64, OWN_RANK * 256), f32),
+            pltpu.SemaphoreType.DMA((10,)), pltpu.SemaphoreType.DMA((7,)),
         ],
         compiler_params=params(60),
         cost_estimate=pl.CostEstimate(flops=8 * 10**9, bytes_accessed=2 * 10**6, transcendentals=0),
         name="exact_part",
-    )(order, offsets, cols, rows, band_window.reshape(1, M), facets, window, jnp.asarray(tables["sample"]))
+    )(order, offsets, cols, rows, band_window.reshape(1, M), facets, window, jnp.asarray(tables["sample"]),
+      jnp.asarray(tables["join_hi"]), jnp.asarray(tables["join_lo"]))
 
     send = pl.pallas_call(
         _residual_kernel,
@@ -592,7 +625,7 @@
         jnp.asarray(tables["turn_s"]), nodes,
     )
 
-    got = lax.all_to_all(send.reshape(128, CHUNKS // 2, 2, 128), ("facet", "rows"), split_axis=0, concat_axis=0, tiled=True)
+    got = lax.all_to_all(send.reshape(128, CHUNKS // 4, 4, 128), ("facet", "rows"), split_axis=0, concat_axis=0, tiled=True)
     phases = pl.pallas_call(
         _phase_kernel,
         in_specs=[vmem] * 3,

time: 70.4 us -> 69.1 us (0.982)
  waiting for transfers between devices: 15.3 us -> 13.8 us
    all_to_all x1, waiting for transfers between devices: 15.1 us -> 13.8 us  [per_device(): lax.all_to_all(send.reshape(128, CHUNKS // 4, 4, 128), ('facet', 'rows'),...]
  transfers between devices with their start and end apart: 2 -> 2, of which waited for: 2 -> 1; matrix products, arithmetic and copies ran while one was open for 0% -> 0% of each run, Pallas kernels for 28% -> 29%
where the time goes in v6:
time: 69.1 us; the launch traced here: 68.9 us
  Pallas kernels  38.3 us (55%)
  starting transfers between devices  14.8 us (21%)
  waiting for transfers between devices  13.8 us (20%)
  local copies, waits for them, and re-layouts  1.83 us (3%)
    all_to_all x1, waiting for transfers between devices, per_device(): lax.all_to_all(send.reshape(128, CHUNKS // 4, 4, 128), ('facet', 'rows'),...  13.8 us
    pallas_call x1, Pallas kernels, per_device(): pl.pallas_call(_exact_kernel, in_specs=[hbm] * 10, out_specs=[hbm] * 7 +...  12.1 us
    pallas_call x1, Pallas kernels, per_device(): pl.pallas_call(_residual_kernel, in_specs=[hbm, anywhere] + [hbm] * 10, o...  10.6 us
    all_to_all x1, starting transfers between devices, per_device(): lax.all_to_all(send.reshape(128, CHUNKS // 4, 4, 128), ('facet', 'rows'),...  10.3 us
    pallas_call x1, Pallas kernels, per_device(): pl.pallas_call(_phase_kernel, in_specs=[vmem] * 3, out_shape=shape((1024,...  7.95 us
    pallas_call x1, Pallas kernels, per_device(): pl.pallas_call(_rows_kernel, in_specs=[anywhere] + [hbm] * 4 + [anywhere]...  7.65 us
    ppermute x1, starting transfers between devices, per_device(): peer = lax.ppermute(facets, 'rows', [(0, 1), (1, 0)])  4.43 us
    unnamed x4, local copies, waits for them, and re-layouts  1.83 us
  transfers between devices with their start and end apart: 2, of which 1 were waited for; matrix products, arithmetic and copies ran while one was open for 0% of the time, Pallas kernels for 29%

profile of v6, /device:TPU:1, one launch (start us, length us, event | category | flops | bytes accessed | tf_op | source)
XLA Modules:
  0.0 68.9 jit_solution(14793111571574498997)
XLA Ops:
  0.0 4.4 %collective-permute-start = (f32[1,2,4,16384]{3,2,1,0:T(4,128)}, f32[1,2,4,16384]{3,2,1,0:T(4,128)S(1)}, u32[]{:S(2)}, u32[]{:S(2)}) collective-permute-start(f32[1,2,4,16384]{3,2,1,0:T(4,128)} %own_hbm.1), channel_id=1, source_target_pairs={{0,1},{1,0},{2,3},{3,2},{4,5},{5,4},{6,7},{7,6},{8,9},{9,8},{10,11... | collective-permute-start | bytes 1572872 | tf_op jit(solution)/shard_map/ppermute | solution.py:570
  4.4 12.1 %exact_part.1 = (bf16[64,1024]{1,0:T(8,128)(2,1)}, bf16[64,1024]{1,0:T(8,128)(2,1)}, f32[64,1024]{1,0:T(8,128)}, f32[64,1024]{1,0:T(8,128)}, f32[64,128]{1,0:T(8...) custom-call(s32[1,64]{1,0:T(1,128)} %bitcast.16, s32[2,64]{1,0:T(2,128)} %bitcast.13, ...), custom_call_target="tpu_custom_call" | custom-call | flops 8000000000 | bytes 2000000 | tf_op jit(solution)/shard_map/exact_part/pallas_call | solution.py:583
  16.5 0.0 collective-permute-done.peer_any
  16.5 0.0 copy-start.1
  16.6 0.8 %copy-done.1 = f32[1,2,4,16384]{3,2,1,0:T(4,128)} copy-done((f32[1,2,4,16384]{3,2,1,0:T(4,128)}, f32[1,2,4,16384]{3,2,1,0:T(4,128)S(1)}, u32[]{:S(2)}) %copy-start.1) | copy-done | bytes 524312
  17.3 10.6 %residual_part.1 = f32[2560,128]{1,0:T(8,128)} custom-call(f32[1,2,4,16384]{3,2,1,0:T(4,128)} %own_hbm.1, f32[1,2,4,16384]{3,2,1,0:T(4,128)} %copy-done.1, f32[1,16384]{1,0:T(1,128)} %bitcast.11, bf16[64,1024]{1,0:T(8,128)(2,1)} %get-tuple-element.13.lc_hbm, bf16[64,1024]{1,0:T(8,128)(2,1)} %get-tuple-element.14.ls_hbm, f32[64,128]{1,0:T(8,128)} %get-tuple-element.15.mc_hbm, ...), custom_call_target="tpu_custom_call" | custom-call | flops 8999999488 | bytes 4000000 | tf_op jit(solution)/shard_map/residual_part/pallas_call | solution.py:607
  28.0 10.3 %all-to-all-start = ((f32[128,5,4,128]{3,2,1,0:T(4,128)}), f32[128,5,4,128]{3,2,1,0:T(4,128)S(1)}, u32[]{:S(2)}, u32[]{:S(2)}) async-start(f32[128,5,4,128]{3,2,1,0:T(4,128)} %bitcast.8), calls=%async_computation | async-start | bytes 2621440 | tf_op jit(solution)/shard_map/all_to_all | solution.py:628
  38.3 7.9 %row_phases.1.phases_any = bf16[1024,1024]{1,0:T(8,128)(2,1)} custom-call(s32[1,64]{1,0:T(1,128)} %bitcast.17, s32[2,64]{1,0:T(2,128)} %bitcast.14, s32[1,64]{1,0:T(1,128)} %bitcast.19), custom_call_target="tpu_custom_call" | custom-call | flops 3000000000 | bytes 2000000 | tf_op jit(solution)/shard_map/row_phases/pallas_call | solution.py:629
  46.3 13.8 %all-to-all-done = f32[128,5,4,128]{3,2,1,0:T(4,128)S(1)} async-done(((f32[128,5,4,128]{3,2,1,0:T(4,128)}), f32[128,5,4,128]{3,2,1,0:T(4,128)S(1)}, u32[]{:S(2)}, u32[]{:S(2)}) %all-to-all-start) | async-done | bytes 1310752 | tf_op jit(solution)/shard_map/all_to_all | solution.py:628
  60.0 0.0 copy-start
  60.0 1.1 %copy-done = f32[128,5,4,128]{3,2,1,0:T(4,128)} copy-done((f32[128,5,4,128]{3,2,1,0:T(4,128)}, f32[128,5,4,128]{3,2,1,0:T(4,128)S(1)}, u32[]{:S(2)}) %copy-start) | copy-done | bytes 1310744
  61.1 7.7 %row_transform.1 = f32[1,2,512,1024]{3,2,1,0:T(8,128)} custom-call(f32[2560,128]{1,0:T(8,128)} %bitcast.9, bf16[256,1024]{1,0:T(8,128)(2,1)} %constant.22.clone.wh_hbm, bf16[256,1024]{1,0:T(8,128)(2,1)} %constant.23.clone.wl_hbm, f32[64,1024]{1,0:T(8,128)} %get-tuple-element.19.pc_hbm, f32[64,1024]{1,0:T(8,128)} %get-tuple-element.20.ps_hbm, ...), custom_call_target="tpu_custom_call" | custom-call | flops 5000000000 | bytes 12000000 | tf_op jit(solution)/shard_map/row_transform/pallas_call | solution.py:639
Async XLA Ops:
  0.0 16.5 %collective-permute-start = (f32[1,2,4,16384]{3,2,1,0:T(4,128)}, f32[1,2,4,16384]{3,2,1,0:T(4,128)S(1)}, u32[]{:S(2)}, u32[]{:S(2)}) collective-permute-start(f32[1,2,4,16384]{3,2,1,0:T(4,128)} %own_hbm.1), channel_id=1, source_target_pairs={{0,1},{1,0},{2,3},{3,2},{4,5},{5,4},{6,7},{7,6},{8,9},{9,8},{10,11... | collective-permute-start | bytes 1572872 | tf_op jit(solution)/shard_map/ppermute | solution.py:570
  16.5 0.8 %copy-start.1 = (f32[1,2,4,16384]{3,2,1,0:T(4,128)}, f32[1,2,4,16384]{3,2,1,0:T(4,128)S(1)}, u32[]{:S(2)}) copy-start(f32[1,2,4,16384]{3,2,1,0:T(4,128)S(1)} %collective-permute-done.peer_any) | copy-start | bytes 1572868
  28.0 32.1 %all-to-all-start = ((f32[128,5,4,128]{3,2,1,0:T(4,128)}), f32[128,5,4,128]{3,2,1,0:T(4,128)S(1)}, u32[]{:S(2)}, u32[]{:S(2)}) async-start(f32[128,5,4,128]{3,2,1,0:T(4,128)} %bitcast.8), calls=%async_computation | async-start | bytes 2621440 | tf_op jit(solution)/shard_map/all_to_all | solution.py:628
  60.0 1.1 %copy-start = (f32[128,5,4,128]{3,2,1,0:T(4,128)}, f32[128,5,4,128]{3,2,1,0:T(4,128)S(1)}, u32[]{:S(2)}) copy-start(f32[128,5,4,128]{3,2,1,0:T(4,128)S(1)} %all-to-all-done) | copy-start | bytes 3932164

commit v7 on v6

--- a/solution.py
+++ b/solution.py
@@ -454,19 +454,18 @@
     gram_ref[:, 768:1024] = high[:, 256:512]
 
 
-def _rows_kernel(got_any, wh_hbm, wl_hbm, pc_hbm, ps_hbm, phases_any, out_hbm,
-                 got_ref, wh_ref, wl_ref, pc_ref, ps_ref, gram_ref, left_ref, right_ref, value_ref, high_ref, low_ref,
+def _rows_kernel(got_ref, wh_hbm, wl_hbm, pc_hbm, ps_hbm, phases_any, out_hbm,
+                 wh_ref, wl_ref, pc_ref, ps_ref, gram_ref, left_ref, right_ref, value_ref, high_ref, low_ref,
                  out_ref, sems, out_sems):
     loads = [
         pltpu.make_async_copy(source, target, sems.at[i])
         for i, (source, target) in enumerate((
-            (got_any, got_ref), (wh_hbm, wh_ref), (wl_hbm, wl_ref), (pc_hbm, pc_ref), (ps_hbm, ps_ref),
+            (wh_hbm, wh_ref), (wl_hbm, wl_ref), (pc_hbm, pc_ref), (ps_hbm, ps_ref),
             (phases_any.at[512:1024], gram_ref), (phases_any.at[0:512], left_ref),
         ))
     ]
     for load in loads:
         load.start()
-    loads[0].wait()
     parts = [
         jnp.concatenate([got_ref[pl.ds(h * CHUNKS + 16 + i, 64, stride=2 * CHUNKS), :] for i in range(4)], 1)
         for h in range(2)
@@ -495,7 +494,7 @@
                 low_ref[part, rows, :] = low
             value = jnp.where(
                 lane < ALL_NODES, pltpu.roll(value, 256 - ALL_NODES, 1), -pltpu.roll(value, ALL_NODES, 1))
-    for load in loads[1:5]:
+    for load in loads[0:4]:
         load.wait()
     for i in range(4):
         cols = slice(i * 256, (i + 1) * 256)
@@ -541,7 +540,7 @@
                 right_ref[256 + at:256 + at + 64, turned] = ci_low
                 right_ref[256 + at + 64:256 + at + 128, turned] = -cr_low
 
-    loads[5].wait()
+    loads[4].wait()
     total = jnp.zeros((8, 256), f32)
     for i in range(4):
         cols = slice(i * 256, (i + 1) * 256)
@@ -550,7 +549,7 @@
     mean = jnp.maximum(jnp.sum(total), 0.0) / (2.0 * SUBROWS * M)
     factor = lax.rsqrt(jnp.full((8, 128), mean, f32) + 1e-06)[0:1, 0:1]
 
-    loads[6].wait()
+    loads[5].wait()
     stores = []
     for part in range(2):
         for i in range(4):
@@ -638,17 +637,17 @@
 
     return pl.pallas_call(
         _rows_kernel,
-        in_specs=[anywhere] + [hbm] * 4 + [anywhere],
+        in_specs=[vmem] + [hbm] * 4 + [anywhere],
         out_specs=hbm,
         out_shape=shape((1, 2, 512, 1024), f32),
         scratch_shapes=[
-            pltpu.VMEM((128 * CHUNKS, 128), f32), pltpu.VMEM((256, 1024), bf16), pltpu.VMEM((256, 1024), bf16),
+            pltpu.VMEM((256, 1024), bf16), pltpu.VMEM((256, 1024), bf16),
             pltpu.VMEM((64, 1024), f32), pltpu.VMEM((64, 1024), f32), pltpu.VMEM((512, 1024), bf16),
             pltpu.VMEM((512, 1024), bf16), pltpu.VMEM((1024, 2048), bf16), pltpu.VMEM((512, 1024), f32),
             pltpu.VMEM((2, 256, 256), bf16), pltpu.VMEM((2, 128, 256), bf16), pltpu.VMEM((2, 512, 1024), f32),
             pltpu.SemaphoreType.DMA((7,)), pltpu.SemaphoreType.DMA((8,)),
         ],
-        compiler_params=params(60),
+        compiler_params=params(50),
         cost_estimate=pl.CostEstimate(flops=5 * 10**9, bytes_accessed=12 * 10**6, transcendentals=0),
         name="row_transform",
     )(got.reshape(128 * CHUNKS, 128), jnp.asarray(tables["weave_hi"]), jnp.asarray(tables["weave_lo"]), pc, ps, phases)

time: 69.1 us -> 66.9 us (0.968)
  Pallas kernels: 38.3 us -> 37.2 us
  local copies, waits for them, and re-layouts: 1.83 us -> 0.82 us
    pallas_call x1, Pallas kernels: 7.65 us -> 6.42 us  [per_device(): pl.pallas_call(_rows_kernel, in_specs=[vmem] + [hbm] * 4 + [anywhere], ou...]
    unnamed x4 -> x10, local copies, waits for them, and re-layouts: 1.83 us -> 0.82 us
  transfers between devices with their start and end apart: 2 -> 2, of which waited for: 1 -> 1; matrix products, arithmetic and copies ran while one was open for 0% -> 0% of each run, Pallas kernels for 29% -> 30%
where the time goes in v7:
time: 66.9 us; the launch traced here: 66.7 us
  Pallas kernels  37.2 us (56%)
  starting transfers between devices  14.8 us (22%)
  waiting for transfers between devices  13.6 us (20%)
  local copies, waits for them, and re-layouts  0.82 us (1%)
    all_to_all x1, waiting for transfers between devices, per_device(): lax.all_to_all(send.reshape(128, CHUNKS // 4, 4, 128), ('facet', 'rows'),...  13.6 us
    pallas_call x1, Pallas kernels, per_device(): pl.pallas_call(_exact_kernel, in_specs=[hbm] * 10, out_specs=[hbm] * 7 +...  12.1 us
    pallas_call x1, Pallas kernels, per_device(): pl.pallas_call(_residual_kernel, in_specs=[hbm, anywhere] + [hbm] * 10, o...  10.6 us
    all_to_all x1, starting transfers between devices, per_device(): lax.all_to_all(send.reshape(128, CHUNKS // 4, 4, 128), ('facet', 'rows'),...  10.3 us
    pallas_call x1, Pallas kernels, per_device(): pl.pallas_call(_phase_kernel, in_specs=[vmem] * 3, out_shape=shape((1024,...  8.06 us
    pallas_call x1, Pallas kernels, per_device(): pl.pallas_call(_rows_kernel, in_specs=[vmem] + [hbm] * 4 + [anywhere], ou...  6.42 us
    ppermute x1, starting transfers between devices, per_device(): peer = lax.ppermute(facets, 'rows', [(0, 1), (1, 0)])  4.43 us
  transfers between devices with their start and end apart: 2, of which 1 were waited for; matrix products, arithmetic and copies ran while one was open for 0% of the time, Pallas kernels for 30%

profile of v7, /device:TPU:1, one launch (start us, length us, event | category | flops | bytes accessed | tf_op | source)
XLA Modules:
  0.0 66.7 jit_solution(12429359349198470367)
XLA Ops:
  0.0 4.4 %collective-permute-start = (f32[1,2,4,16384]{3,2,1,0:T(4,128)}, f32[1,2,4,16384]{3,2,1,0:T(4,128)S(1)}, u32[]{:S(2)}, u32[]{:S(2)}) collective-permute-start(f32[1,2,4,16384]{3,2,1,0:T(4,128)} %own_hbm.1), channel_id=1, source_target_pairs={{0,1},{1,0},{2,3},{3,2},{4,5},{5,4},{6,7},{7,6},{8,9},{9,8},{10,11... | collective-permute-start | bytes 1572872 | tf_op jit(solution)/shard_map/ppermute | solution.py:569
  4.4 12.1 %exact_part.1 = (bf16[64,1024]{1,0:T(8,128)(2,1)}, bf16[64,1024]{1,0:T(8,128)(2,1)}, f32[64,1024]{1,0:T(8,128)}, f32[64,1024]{1,0:T(8,128)}, f32[64,128]{1,0:T(8...) custom-call(s32[1,64]{1,0:T(1,128)} %bitcast.16, s32[2,64]{1,0:T(2,128)} %bitcast.13, ...), custom_call_target="tpu_custom_call" | custom-call | flops 8000000000 | bytes 2000000 | tf_op jit(solution)/shard_map/exact_part/pallas_call | solution.py:582
  16.5 0.0 collective-permute-done.peer_any
  16.5 0.0 copy-start.4
  16.6 0.8 %copy-done.4 = f32[1,2,4,16384]{3,2,1,0:T(4,128)} copy-done((f32[1,2,4,16384]{3,2,1,0:T(4,128)}, f32[1,2,4,16384]{3,2,1,0:T(4,128)S(1)}, u32[]{:S(2)}) %copy-start.4) | copy-done | bytes 524312
  17.4 10.6 %residual_part.1 = f32[2560,128]{1,0:T(8,128)} custom-call(f32[1,2,4,16384]{3,2,1,0:T(4,128)} %own_hbm.1, f32[1,2,4,16384]{3,2,1,0:T(4,128)} %copy-done.4, f32[1,16384]{1,0:T(1,128)} %bitcast.11, bf16[64,1024]{1,0:T(8,128)(2,1)} %get-tuple-element.13.lc_hbm, bf16[64,1024]{1,0:T(8,128)(2,1)} %get-tuple-element.14.ls_hbm, f32[64,128]{1,0:T(8,128)} %get-tuple-element.15.mc_hbm, ...), custom_call_target="tpu_custom_call" | custom-call | flops 8999999488 | bytes 4000000 | tf_op jit(solution)/shard_map/residual_part/pallas_call | solution.py:606
  28.0 10.3 %all-to-all-start = ((f32[128,5,4,128]{3,2,1,0:T(4,128)}), f32[128,5,4,128]{3,2,1,0:T(4,128)S(1)}, u32[]{:S(2)}, u32[]{:S(2)}) async-start(f32[128,5,4,128]{3,2,1,0:T(4,128)} %bitcast.9), calls=%async_computation | async-start | bytes 2621440 | tf_op jit(solution)/shard_map/all_to_all | solution.py:627
  38.3 0.0 copy-start
  38.3 0.0 copy-start.1
  38.4 0.0 copy-start.2
  38.4 0.0 copy-start.3
  38.4 8.1 %row_phases.1.phases_any = bf16[1024,1024]{1,0:T(8,128)(2,1)} custom-call(s32[1,64]{1,0:T(1,128)} %bitcast.17, s32[2,64]{1,0:T(2,128)} %bitcast.14, s32[1,64]{1,0:T(1,128)} %bitcast.19), custom_call_target="tpu_custom_call" | custom-call | flops 3000000000 | bytes 2000000 | tf_op jit(solution)/shard_map/row_phases/pallas_call | solution.py:628
  46.4 13.6 %all-to-all-done = f32[128,5,4,128]{3,2,1,0:T(4,128)S(1)} async-done(((f32[128,5,4,128]{3,2,1,0:T(4,128)}), f32[128,5,4,128]{3,2,1,0:T(4,128)S(1)}, u32[]{:S(2)}, u32[]{:S(2)}) %all-to-all-start) | async-done | bytes 1310752 | tf_op jit(solution)/shard_map/all_to_all | solution.py:627
  60.1 0.0 copy-done
  60.1 0.0 copy-done.1
  60.1 0.0 copy-done.2
  60.1 0.0 copy-done.3
  60.1 6.4 %row_transform.1 = f32[1,2,512,1024]{3,2,1,0:T(8,128)} custom-call(f32[2560,128]{1,0:T(8,128)S(1)} %bitcast.8, bf16[256,1024]{1,0:T(8,128)(2,1)S(1)} %copy-done.1, bf16[256,1024]{1,0:T(8,128)(2,1)S(1)} %copy-done, f32[64,1024]{1,0:T(8,128)S(1)} %copy-done.2, f32[64,1024]{1,0:T(8,128)S(1)} %copy-done.3, bf16[1024,1024]{1,0:T(8,128)(2,1)} %row_phases.1.phases_any), custom_call_target="tpu_custom_call" | custom-call | flops 5000000000 | bytes 12000000 | tf_op jit(solution)/shard_map/row_transform/pallas_call | solution.py:638
Async XLA Ops:
  0.0 16.5 %collective-permute-start = (f32[1,2,4,16384]{3,2,1,0:T(4,128)}, f32[1,2,4,16384]{3,2,1,0:T(4,128)S(1)}, u32[]{:S(2)}, u32[]{:S(2)}) collective-permute-start(f32[1,2,4,16384]{3,2,1,0:T(4,128)} %own_hbm.1), channel_id=1, source_target_pairs={{0,1},{1,0},{2,3},{3,2},{4,5},{5,4},{6,7},{7,6},{8,9},{9,8},{10,11... | collective-permute-start | bytes 1572872 | tf_op jit(solution)/shard_map/ppermute | solution.py:569
  16.5 0.8 %copy-start.4 = (f32[1,2,4,16384]{3,2,1,0:T(4,128)}, f32[1,2,4,16384]{3,2,1,0:T(4,128)S(1)}, u32[]{:S(2)}) copy-start(f32[1,2,4,16384]{3,2,1,0:T(4,128)S(1)} %collective-permute-done.peer_any) | copy-start | bytes 1572868
  28.0 32.1 %all-to-all-start = ((f32[128,5,4,128]{3,2,1,0:T(4,128)}), f32[128,5,4,128]{3,2,1,0:T(4,128)S(1)}, u32[]{:S(2)}, u32[]{:S(2)}) async-start(f32[128,5,4,128]{3,2,1,0:T(4,128)} %bitcast.9), calls=%async_computation | async-start | bytes 2621440 | tf_op jit(solution)/shard_map/all_to_all | solution.py:627
  38.3 21.7 %copy-start = (bf16[256,1024]{1,0:T(8,128)(2,1)S(1)}, bf16[256,1024]{1,0:T(8,128)(2,1)}, u32[]{:S(2)}) copy-start(bf16[256,1024]{1,0:T(8,128)(2,1)} %constant.23.clone.wl_hbm) | copy-start | bytes 1572868
  38.3 21.7 %copy-start.1 = (bf16[256,1024]{1,0:T(8,128)(2,1)S(1)}, bf16[256,1024]{1,0:T(8,128)(2,1)}, u32[]{:S(2)}) copy-start(bf16[256,1024]{1,0:T(8,128)(2,1)} %constant.22.clone.wh_hbm) | copy-start | bytes 1572868
  38.4 21.7 %copy-start.2 = (f32[64,1024]{1,0:T(8,128)S(1)}, f32[64,1024]{1,0:T(8,128)}, u32[]{:S(2)}) copy-start(f32[64,1024]{1,0:T(8,128)} %get-tuple-element.19.pc_hbm) | copy-start | bytes 786436
  38.4 21.7 %copy-start.3 = (f32[64,1024]{1,0:T(8,128)S(1)}, f32[64,1024]{1,0:T(8,128)}, u32[]{:S(2)}) copy-start(f32[64,1024]{1,0:T(8,128)} %get-tuple-element.20.ps_hbm) | copy-start | bytes 786436

commit v8 on v7

--- a/solution.py
+++ b/solution.py
@@ -113,6 +113,7 @@
 
 
 COL_A, COL_SC8, COL_CF8, COL_ROW = 0, 16, 24, 32
+PACK = ((0, 1024), (1024, 2048), (2048, 2176), (2176, 2304), (2304, 2816))
 CHUNKS = 20
 
 
@@ -138,7 +139,7 @@
 
 
 def _prepare(slot, half, order_ref, offsets_ref, cols_ref, rows_ref, band_ref,
-             lc_ref, ls_ref, pc_ref, ps_ref, mc_ref, ms_ref, combine_ref):
+             lc_ref, ls_ref, pc_ref, ps_ref, mc_ref, ms_ref):
     cf_row = _offset_row(order_ref, offsets_ref, 0)
     own_cf = _pick(cf_row, slot).astype(jnp.int32)
     cf = _to_column(cf_row).astype(jnp.int32)
@@ -169,22 +170,24 @@
         band = band_ref[:, i * 128:(i + 1) * 128]
         pc_ref[:, i * 128:(i + 1) * 128] = (c * low_c - s * low_s) * band
         ps_ref[:, i * 128:(i + 1) * 128] = (s * low_c + c * low_s) * band
-    rho = odd.astype(f32) * (0.5 / ROW_SCALE)
-    power = jnp.ones((64, 128), f32)
+
+
+def _combine(mc, ms, combine_ref):
+    lane = lax.broadcasted_iota(jnp.int32, (64, 128), 1)
+    row = 4 * lax.axis_index("rows") + 4 * lax.bitwise_and(lane // 8, 1) + lax.bitwise_and(lane, 3)
+    place = (2 * lax.bitwise_and(row, 7) - 7).astype(f32) * (0.5 / ROW_SCALE)
     first = lax.bitwise_and(lane, 4) == 0
     to_re, to_im = jnp.where(first, mc, ms), jnp.where(first, -ms, mc)
     for n in range(ERANK):
         for part, value in ((0, to_re), (1, to_im)):
             base = part * 128 + n * 64
-            combine_ref[base:base + 64, :] = (value * power)[:, COL_ROW:COL_ROW + 16].astype(bf16)
-        power = power * rho
+            combine_ref[base:base + 64, :] = (value * place if n else value)[:, COL_ROW:COL_ROW + 16].astype(bf16)
 
 
 def _exact_kernel(order_hbm, offsets_hbm, cols_hbm, rows_hbm, band_hbm, data_hbm, window_hbm, sample_hbm, jh_hbm, jl_hbm,
-                  lc_hbm, ls_hbm, pc_hbm, ps_hbm, mc_hbm, ms_hbm, combine_hbm, out_ref,
+                  pc_hbm, ps_hbm, pack_hbm,
                   order_ref, offsets_ref, cols_ref, rows_ref, band_ref, data_ref, window_ref, sample_ref, jh_ref, jl_ref,
-                  lc_ref, ls_ref, lc16_ref, ls16_ref, pc_ref, ps_ref, mc_ref, ms_ref, combine_ref,
-                  even_ref, odd_ref, acc_ref, terms_ref, sems, out_sems):
+                  pc_ref, ps_ref, out_ref, even_ref, odd_ref, acc_ref, terms_ref, sems, out_sems):
     loads = [
         pltpu.make_async_copy(source, target, sems.at[i])
         for i, (source, target) in enumerate((
@@ -198,15 +201,14 @@
     for load in loads[:5]:
         load.wait()
     acc_ref[...] = jnp.zeros_like(acc_ref)
+    lc_ref, ls_ref, mc_ref, ms_ref, nodes_ref = (out_ref.at[:, a:b] for a, b in PACK)
     _prepare(lax.axis_index("facet"), lax.axis_index("rows"), order_ref, offsets_ref, cols_ref, rows_ref, band_ref,
-             lc_ref, ls_ref, pc_ref, ps_ref, mc_ref, ms_ref, combine_ref)
-    lc16_ref[...] = lc_ref[...].astype(bf16)
-    ls16_ref[...] = ls_ref[...].astype(bf16)
+             lc_ref, ls_ref, pc_ref, ps_ref, mc_ref, ms_ref)
     stores = [
         pltpu.make_async_copy(source, target, out_sems.at[i])
         for i, (source, target) in enumerate((
-            (lc16_ref, lc_hbm), (ls16_ref, ls_hbm), (pc_ref, pc_hbm), (ps_ref, ps_hbm), (mc_ref, mc_hbm), (ms_ref, ms_hbm),
-            (combine_ref, combine_hbm),
+            (pc_ref, pc_hbm), (ps_ref, ps_hbm),
+            (out_ref.at[:, 0:PACK[-1][0]], pack_hbm.at[:, 0:PACK[-1][0]]),
         ))
     ]
     for store in stores:
@@ -287,31 +289,34 @@
     for load in loads[8:]:
         load.wait()
     high, low = _halves(terms_ref[...])
-    out_ref[...] = (
+    nodes_ref[...] = (
         jnp.dot(high, jh_ref[...], preferred_element_type=f32)
         + (jnp.dot(high, jl_ref[...], preferred_element_type=f32) + jnp.dot(low, jh_ref[...], preferred_element_type=f32))
     )
+    last = pltpu.make_async_copy(nodes_ref, pack_hbm.at[:, PACK[-1][0]:PACK[-1][1]], out_sems.at[3])
+    last.start()
     for store in stores:
         store.wait()
-
-
-def _residual_kernel(own_hbm, peer_any, window_hbm, lc_hbm, ls_hbm, mc_hbm, ms_hbm, combine_hbm,
-                     table_hbm, tc_hbm, ts_hbm, nodes_hbm, out_ref,
-                     own_ref, peer_ref, window_ref, lc_ref, ls_ref, mc_ref, ms_ref, combine_ref,
-                     table_ref, tc_ref, ts_ref, nodes_ref, even_ref, odd_ref, sum_ref, sems):
+    last.wait()
+
+
+def _residual_kernel(own_hbm, peer_ref, window_hbm, pack_ref, table_hbm, tc_hbm, ts_hbm, out_ref,
+                     own_ref, window_ref, lc_ref, ls_ref, combine_ref, table_ref, tc_ref, ts_ref, even_ref, odd_ref, sum_ref, sems):
     loads = [
         pltpu.make_async_copy(source, target, sems.at[i])
         for i, (source, target) in enumerate((
-            (own_hbm, own_ref), (peer_any, peer_ref), (window_hbm, window_ref), (lc_hbm, lc_ref), (ls_hbm, ls_ref),
-            (mc_hbm, mc_ref), (ms_hbm, ms_ref), (combine_hbm, combine_ref),
+            (own_hbm, own_ref), (window_hbm, window_ref),
             (table_hbm.at[lax.axis_index("rows")], table_ref), (tc_hbm, tc_ref), (ts_hbm, ts_ref),
-            (nodes_hbm, nodes_ref),
         ))
     ]
     for load in loads:
         load.start()
     sum_ref[...] = jnp.zeros_like(sum_ref)
-    for load in loads[:3]:
+    mc_ref, ms_ref, nodes_ref = (pack_ref.at[:, a:b] for a, b in PACK[2:])
+    lc_ref[...] = pack_ref[:, PACK[0][0]:PACK[0][1]].astype(bf16)
+    ls_ref[...] = pack_ref[:, PACK[1][0]:PACK[1][1]].astype(bf16)
+    _combine(mc_ref[...], ms_ref[...], combine_ref)
+    for load in loads[:2]:
         load.wait()
     largest = jnp.zeros((4, 2048), f32)
     for i in range(8):
@@ -323,8 +328,6 @@
     largest = jnp.maximum(jnp.max(jnp.max(largest, axis=1, keepdims=True), axis=0, keepdims=True), 1e-30)
     scale_in = DATA_SCALE / largest
     scale_out = largest * (1.0 / (DATA_SCALE * TABLE_SCALE))
-    for load in loads[3:8]:
-        load.wait()
 
     def mix(block, i):
         here = pl.ds(pl.multiple_of(block * BLOCK + i * 256, 256), 256)
@@ -381,7 +384,7 @@
         spin = turns(j)
         for i in range(4):
             build(even_ref, j, i, mix(j, i), *spin)
-    for load in loads[8:]:
+    for load in loads[2:]:
         load.wait()
 
     def body(pair, carry):
@@ -578,24 +581,21 @@
     def params(mib):
         return pltpu.CompilerParams(vmem_limit_bytes=mib * 1024 * 1024)
 
-    wide, wide16, narrow = shape((64, 1024), f32), shape((64, 1024), bf16), shape((64, 128), f32)
-    lc, ls, pc, ps, mc, ms, combine, nodes = pl.pallas_call(
+    wide = shape((64, 1024), f32)
+    pc, ps, pack = pl.pallas_call(
         _exact_kernel,
         in_specs=[hbm] * 10,
-        out_specs=[hbm] * 7 + [vmem],
-        out_shape=[wide16, wide16, wide, wide, narrow, narrow, shape((256, 16), bf16),
-                   shape((64, 128 * (CHUNKS - 16)), f32)],
+        out_specs=[hbm] * 3,
+        out_shape=[wide, wide, shape((64, PACK[-1][1]), f32)],
         scratch_shapes=[
             pltpu.VMEM((1, 64), jnp.int32), pltpu.VMEM((2, 64), jnp.int32), pltpu.VMEM((1, 64), jnp.int32),
             pltpu.VMEM((1, 64), jnp.int32), pltpu.VMEM((1, M), f32), pltpu.VMEM((1, 2, 4, 16384), f32),
             pltpu.VMEM((1, 16384), f32), pltpu.VMEM((SPAN, 128), bf16),
             pltpu.VMEM((OWN_RANK * 256, 512), bf16), pltpu.VMEM((OWN_RANK * 256, 512), bf16),
-            pltpu.VMEM((64, 1024), f32), pltpu.VMEM((64, 1024), f32), pltpu.VMEM((64, 1024), bf16),
-            pltpu.VMEM((64, 1024), bf16), pltpu.VMEM((64, 1024), f32), pltpu.VMEM((64, 1024), f32),
-            pltpu.VMEM((64, 128), f32), pltpu.VMEM((64, 128), f32), pltpu.VMEM((256, 16), bf16),
+            pltpu.VMEM((64, 1024), f32), pltpu.VMEM((64, 1024), f32), pltpu.VMEM((64, PACK[-1][1]), f32),
             pltpu.VMEM((512, BLOCK), bf16), pltpu.VMEM((512, BLOCK), bf16), pltpu.VMEM((4, 512, 128), f32),
             pltpu.VMEM((64, OWN_RANK * 256), f32),
-            pltpu.SemaphoreType.DMA((10,)), pltpu.SemaphoreType.DMA((7,)),
+            pltpu.SemaphoreType.DMA((10,)), pltpu.SemaphoreType.DMA((4,)),
         ],
         compiler_params=params(60),
         cost_estimate=pl.CostEstimate(flops=8 * 10**9, bytes_accessed=2 * 10**6, transcendentals=0),
@@ -605,23 +605,21 @@
 
     send = pl.pallas_call(
         _residual_kernel,
-        in_specs=[hbm, anywhere] + [hbm] * 10,
+        in_specs=[hbm, vmem, hbm, vmem] + [hbm] * 3,
         out_shape=shape((128 * CHUNKS, 128), f32),
         scratch_shapes=[
-            pltpu.VMEM((1, 2, 4, 16384), f32), pltpu.VMEM((1, 2, 4, 16384), f32), pltpu.VMEM((1, 16384), f32),
-            pltpu.VMEM((64, 1024), bf16), pltpu.VMEM((64, 1024), bf16), pltpu.VMEM((64, 128), f32),
-            pltpu.VMEM((64, 128), f32), pltpu.VMEM((256, 16), bf16),
+            pltpu.VMEM((1, 2, 4, 16384), f32), pltpu.VMEM((1, 16384), f32),
+            pltpu.VMEM((64, 1024), bf16), pltpu.VMEM((64, 1024), bf16), pltpu.VMEM((256, 16), bf16),
             pltpu.VMEM((1024, 1024), f8), pltpu.VMEM((16, 512), f32), pltpu.VMEM((16, 512), f32),
-            pltpu.VMEM((64, 128 * (CHUNKS - 16)), f32),
             pltpu.VMEM((512, 1024), f8), pltpu.VMEM((512, 1024), f8), pltpu.VMEM((2, 128, 512), f32),
-            pltpu.SemaphoreType.DMA((12,)),
+            pltpu.SemaphoreType.DMA((5,)),
         ],
-        compiler_params=params(60),
+        compiler_params=params(44),
         cost_estimate=pl.CostEstimate(flops=9 * 10**9, bytes_accessed=4 * 10**6, transcendentals=0),
         name="residual_part",
     )(
-        facets, peer, window, lc, ls, mc, ms, combine, jnp.asarray(tables["resid"]), jnp.asarray(tables["turn_c"]),
-        jnp.asarray(tables["turn_s"]), nodes,
+        facets, peer, window, pack, jnp.asarray(tables["resid"]), jnp.asarray(tables["turn_c"]),
+        jnp.asarray(tables["turn_s"]),
     )
 
     got = lax.all_to_all(send.reshape(128, CHUNKS // 4, 4, 128), ("facet", "rows"), split_axis=0, concat_axis=0, tiled=True)

time: 66.9 us -> 66.3 us (level)
  Pallas kernels: 37.2 us -> 36.4 us
    pallas_call x2, Pallas kernels: 22.7 us -> 21.9 us  [the longest x1 12.2 us: per_device(): pl.pallas_call(_exact_kernel, in_specs=[hbm] * 10, out_specs=[hbm] * 3, o...]
  transfers between devices with their start and end apart: 2 -> 2, of which waited for: 1 -> 1; matrix products, arithmetic and copies ran while one was open for 0% -> 0% of each run, Pallas kernels for 30% -> 31%
where the time goes in v8:
time: 66.3 us; the launch traced here: 66.1 us
  Pallas kernels  36.4 us (55%)
  starting transfers between devices  14.7 us (22%)
  waiting for transfers between devices  13.6 us (21%)
  local copies, waits for them, and re-layouts  1.15 us (2%)
    all_to_all x1, waiting for transfers between devices, per_device(): lax.all_to_all(send.reshape(128, CHUNKS // 4, 4, 128), ('facet', 'rows'),...  13.6 us
    pallas_call x1, Pallas kernels, per_device(): pl.pallas_call(_exact_kernel, in_specs=[hbm] * 10, out_specs=[hbm] * 3, o...  12.2 us
    all_to_all x1, starting transfers between devices, per_device(): lax.all_to_all(send.reshape(128, CHUNKS // 4, 4, 128), ('facet', 'rows'),...  10.2 us
    pallas_call x1, Pallas kernels, per_device(): pl.pallas_call(_residual_kernel, in_specs=[hbm, vmem, hbm, vmem] + [hbm]...  9.71 us
    pallas_call x1, Pallas kernels, per_device(): pl.pallas_call(_phase_kernel, in_specs=[vmem] * 3, out_shape=shape((1024,...  8.05 us
    pallas_call x1, Pallas kernels, per_device(): pl.pallas_call(_rows_kernel, in_specs=[vmem] + [hbm] * 4 + [anywhere], ou...  6.42 us
    ppermute x1, starting transfers between devices, per_device(): peer = lax.ppermute(facets, 'rows', [(0, 1), (1, 0)])  4.43 us
  transfers between devices with their start and end apart: 2, of which 1 were waited for; matrix products, arithmetic and copies ran while one was open for 0% of the time, Pallas kernels for 31%

profile of v8, /device:TPU:1, one launch (start us, length us, event | category | flops | bytes accessed | tf_op | source)
XLA Modules:
  0.0 66.1 jit_solution(2451951154138040125)
XLA Ops:
  0.0 4.4 %collective-permute-start = (f32[1,2,4,16384]{3,2,1,0:T(4,128)}, f32[1,2,4,16384]{3,2,1,0:T(4,128)S(1)}, u32[]{:S(2)}, u32[]{:S(2)}) collective-permute-start(f32[1,2,4,16384]{3,2,1,0:T(4,128)} %own_hbm.1), channel_id=1, source_target_pairs={{0,1},{1,0},{2,3},{3,2},{4,5},{5,4},{6,7},{7,6},{8,9},{9,8},{10,11... | collective-permute-start | bytes 1572872 | tf_op jit(solution)/shard_map/ppermute | solution.py:572
  4.4 0.0 copy-start.6
  4.5 12.2 %exact_part.1 = (f32[64,1024]{1,0:T(8,128)}, f32[64,1024]{1,0:T(8,128)}, f32[64,2816]{1,0:T(8,128)}) custom-call(s32[1,64]{1,0:T(1,128)} %bitcast.15, s32[2,64]{1,0:T(2,128)} %bitcast.12, s32[1,64]{1,0:T(1,128)} %bitcast.14, s32[1,64]{1,0:T(1,128)} %bitcast.17, f32[1,1024]{1,0:T(1,128)} %bitcast.11, f32[1,2,4,16384]{3,2,1,0:T(4,128)} %own_hbm.1, ...), custom_call_target="tpu_custom_call" | custom-call | flops 8000000000 | bytes 2000000 | tf_op jit(solution)/shard_map/exact_part/pallas_call | solution.py:585
  16.6 0.0 collective-permute-done.peer_ref
  16.6 0.0 copy-done
  16.7 0.0 copy-done.1
  16.7 0.0 copy-done.2
  16.7 0.0 copy-done.5
  16.7 0.0 copy-done.6
  16.7 0.0 copy-start.9
  16.7 1.1 %copy-done.9 = f32[64,2816]{1,0:T(8,128)S(1)} copy-done((f32[64,2816]{1,0:T(8,128)S(1)}, f32[64,2816]{1,0:T(8,128)}, u32[]{:S(2)}) %copy-start.9) | copy-done | bytes 720920
  17.8 9.7 %residual_part.1 = f32[2560,128]{1,0:T(8,128)} custom-call(f32[1,2,4,16384]{3,2,1,0:T(4,128)S(1)} %copy-done, f32[1,2,4,16384]{3,2,1,0:T(4,128)S(1)} %collective-permute-done.peer_ref, f32[1,16384]{1,0:T(1,128)S(1)} %bitcast.10, f32[64,2816]{1,0:T(8,128)S(1)} %copy-done.9, f8e4m3fn[2,1024,1024]{2,1,0:T(32,128)(4,1)S(1)} %copy-done.2, ...), custom_call_target="tpu_custom_call" | custom-call | flops 8999999488 | bytes 4000000 | tf_op jit(solution)/shard_map/residual_part/pallas_call | solution.py:606
  27.5 10.2 %all-to-all-start = ((f32[128,5,4,128]{3,2,1,0:T(4,128)}), f32[128,5,4,128]{3,2,1,0:T(4,128)S(1)}, u32[]{:S(2)}, u32[]{:S(2)}) async-start(f32[128,5,4,128]{3,2,1,0:T(4,128)} %bitcast.6), calls=%async_computation | async-start | bytes 2621440 | tf_op jit(solution)/shard_map/all_to_all | solution.py:625
  37.8 0.0 copy-start.3
  37.8 0.0 copy-start.4
  37.8 0.0 copy-start.7
  37.8 0.0 copy-start.8
  37.8 8.1 %row_phases.1.phases_any = bf16[1024,1024]{1,0:T(8,128)(2,1)} custom-call(s32[1,64]{1,0:T(1,128)} %bitcast.16, s32[2,64]{1,0:T(2,128)} %bitcast.13, s32[1,64]{1,0:T(1,128)} %bitcast.18), custom_call_target="tpu_custom_call" | custom-call | flops 3000000000 | bytes 2000000 | tf_op jit(solution)/shard_map/row_phases/pallas_call | solution.py:626
  45.9 13.6 %all-to-all-done = f32[128,5,4,128]{3,2,1,0:T(4,128)S(1)} async-done(((f32[128,5,4,128]{3,2,1,0:T(4,128)}), f32[128,5,4,128]{3,2,1,0:T(4,128)S(1)}, u32[]{:S(2)}, u32[]{:S(2)}) %all-to-all-start) | async-done | bytes 1310752 | tf_op jit(solution)/shard_map/all_to_all | solution.py:625
  59.5 0.0 copy-done.3
  59.5 0.0 copy-done.4
  59.5 0.0 copy-done.7
  59.5 0.0 copy-done.8
  59.5 6.4 %row_transform.1 = f32[1,2,512,1024]{3,2,1,0:T(8,128)} custom-call(f32[2560,128]{1,0:T(8,128)S(1)} %bitcast.8, bf16[256,1024]{1,0:T(8,128)(2,1)S(1)} %copy-done.4, bf16[256,1024]{1,0:T(8,128)(2,1)S(1)} %copy-done.3, f32[64,1024]{1,0:T(8,128)S(1)} %copy-done.7, f32[64,1024]{1,0:T(8,128)S(1)} %copy-done.8, bf16[1024,1024]{1,0:T(8,128)(2,1)} %row_phases.1.phases_any), custom_call_target="tpu_custom_call" | custom-call | flops 5000000000 | bytes 12000000 | tf_op jit(solution)/shard_map/row_transform/pallas_call | solution.py:636
  (4 shorter events, 0.0 us)
Async XLA Ops:
  0.0 16.6 %collective-permute-start = (f32[1,2,4,16384]{3,2,1,0:T(4,128)}, f32[1,2,4,16384]{3,2,1,0:T(4,128)S(1)}, u32[]{:S(2)}, u32[]{:S(2)}) collective-permute-start(f32[1,2,4,16384]{3,2,1,0:T(4,128)} %own_hbm.1), channel_id=1, source_target_pairs={{0,1},{1,0},{2,3},{3,2},{4,5},{5,4},{6,7},{7,6},{8,9},{9,8},{10,11... | collective-permute-start | bytes 1572872 | tf_op jit(solution)/shard_map/ppermute | solution.py:572
  4.4 12.2 %copy-start = (f32[1,2,4,16384]{3,2,1,0:T(4,128)S(1)}, f32[1,2,4,16384]{3,2,1,0:T(4,128)}, u32[]{:S(2)}) copy-start(f32[1,2,4,16384]{3,2,1,0:T(4,128)} %own_hbm.1) | copy-start | bytes 1572868
  4.4 12.2 %copy-start.1 = (f32[16384]{0:T(1024)S(1)}, f32[16384]{0:T(1024)}, u32[]{:S(2)}) copy-start(f32[16384]{0:T(1024)} %param.16) | copy-start | bytes 196612
  4.4 12.2 %copy-start.2 = (f8e4m3fn[2,1024,1024]{2,1,0:T(32,128)(4,1)S(1)}, f8e4m3fn[2,1024,1024]{2,1,0:T(32,128)(4,1)}, u32[]{:S(2)}) copy-start(f8e4m3fn[2,1024,1024]{2,1,0:T(32,128)(4,1)} %constant.19.clone.table_hbm) | copy-start | bytes 6291460
  4.4 12.2 %copy-start.5 = (f32[16,512]{1,0:T(8,128)S(1)}, f32[16,512]{1,0:T(8,128)}, u32[]{:S(2)}) copy-start(f32[16,512]{1,0:T(8,128)} %constant.21.clone.ts_hbm) | copy-start | bytes 98308
  4.4 12.2 %copy-start.6 = (f32[16,512]{1,0:T(8,128)S(1)}, f32[16,512]{1,0:T(8,128)}, u32[]{:S(2)}) copy-start(f32[16,512]{1,0:T(8,128)} %constant.20.clone.tc_hbm) | copy-start | bytes 98308
  16.7 1.1 %copy-start.9 = (f32[64,2816]{1,0:T(8,128)S(1)}, f32[64,2816]{1,0:T(8,128)}, u32[]{:S(2)}) copy-start(f32[64,2816]{1,0:T(8,128)} %get-tuple-element.8.pack_ref) | copy-start | bytes 2162692
  27.5 32.0 %all-to-all-start = ((f32[128,5,4,128]{3,2,1,0:T(4,128)}), f32[128,5,4,128]{3,2,1,0:T(4,128)S(1)}, u32[]{:S(2)}, u32[]{:S(2)}) async-start(f32[128,5,4,128]{3,2,1,0:T(4,128)} %bitcast.6), calls=%async_computation | async-start | bytes 2621440 | tf_op jit(solution)/shard_map/all_to_all | solution.py:625
  37.8 21.7 %copy-start.3 = (bf16[256,1024]{1,0:T(8,128)(2,1)S(1)}, bf16[256,1024]{1,0:T(8,128)(2,1)}, u32[]{:S(2)}) copy-start(bf16[256,1024]{1,0:T(8,128)(2,1)} %constant.23.clone.wl_hbm) | copy-start | bytes 1572868
  37.8 21.7 %copy-start.4 = (bf16[256,1024]{1,0:T(8,128)(2,1)S(1)}, bf16[256,1024]{1,0:T(8,128)(2,1)}, u32[]{:S(2)}) copy-start(bf16[256,1024]{1,0:T(8,128)(2,1)} %constant.22.clone.wh_hbm) | copy-start | bytes 1572868
  37.8 21.7 %copy-start.7 = (f32[64,1024]{1,0:T(8,128)S(1)}, f32[64,1024]{1,0:T(8,128)}, u32[]{:S(2)}) copy-start(f32[64,1024]{1,0:T(8,128)} %get-tuple-element.9.pc_hbm) | copy-start | bytes 786436
  37.8 21.7 %copy-start.8 = (f32[64,1024]{1,0:T(8,128)S(1)}, f32[64,1024]{1,0:T(8,128)}, u32[]{:S(2)}) copy-start(f32[64,1024]{1,0:T(8,128)} %get-tuple-element.10.ps_hbm) | copy-start | bytes 786436

commit v9 on v8

--- a/solution.py
+++ b/solution.py
@@ -72,7 +72,7 @@
     resid_s = np.sin(angle).astype(np.float32).astype(ml_dtypes.bfloat16).astype(np.float64) - np.sin(exact)
     half = M // 2
     resid = np.stack(
-        [np.concatenate([resid_c[:, h * half:(h + 1) * half], resid_s[:, h * half:(h + 1) * half]], 1) for h in range(2)]
+        [np.concatenate([v[:, h * half:(h + 1) * half] for v in (resid_c, resid_s - resid_c, resid_s + resid_c)], 1) for h in range(2)]
     )
     resid = (resid * TABLE_SCALE).astype(np.float32).astype(ml_dtypes.float8_e4m3fn)
     def spread(count, width, even):
@@ -345,9 +345,11 @@
         rows = rows.astype(bf16)
         for n in range(ERANK):
             gr, gi = rows[n * 64:(n + 1) * 64], rows[128 + n * 64:128 + (n + 1) * 64]
-            at = j * 256 + n * 64
-            z_ref[at:at + 64, cols] = (gr * ec + gi * es).astype(z_ref.dtype)
-            z_ref[at + 128:at + 192, cols] = (gi * ec - gr * es).astype(z_ref.dtype)
+            at = j * 128 + n * 64
+            zr, zi = gr * ec + gi * es, gi * ec - gr * es
+            z_ref[at:at + 64, cols] = (zr + zi).astype(z_ref.dtype)
+            z_ref[256 + at:256 + at + 64, cols] = zi.astype(z_ref.dtype)
+            z_ref[512 + at:512 + at + 64, cols] = zr.astype(z_ref.dtype)
 
     def turns(block):
         return tuple(
@@ -361,24 +363,25 @@
             spins = [turns(following * 2 + j) for j in range(2)]
             ready = mix(following * 2, 0)
         at = 0
-        for j in range(2):
-            for kc in range(2):
+        for kc in range(2):
+            for _ in range(1):
                 cols = slice(kc * 256, (kc + 1) * 256)
-                z = z_ref[j * 256:(j + 1) * 256, :]
-                by_c = jnp.dot(z, table_ref[:, cols], preferred_element_type=f32)
-                by_s = jnp.dot(z, table_ref[:, 512 + kc * 256:768 + kc * 256], preferred_element_type=f32)
-                for _ in range(2 if building else 0):
+                one = jnp.dot(z_ref[0:256], table_ref[:, cols], preferred_element_type=f32)
+                two = jnp.dot(z_ref[256:512], table_ref[:, 512 + kc * 256:768 + kc * 256], preferred_element_type=f32)
+                three = jnp.dot(z_ref[512:768], table_ref[:, 1024 + kc * 256:1280 + kc * 256], preferred_element_type=f32)
+                for _ in range(4 if building else 0):
                     bj, bi = tasks[at]
                     at += 1
                     coming = mix(following * 2 + tasks[at][0], tasks[at][1]) if at < 8 else None
                     build(next_ref, bj, bi, ready, *spins[bj])
                     ready = coming
-                re = by_c[0:128] + by_s[128:256]
-                im = by_c[128:256] - by_s[0:128]
-                tc = tc_ref[pl.ds(group * 2 + j, 1), cols]
-                ts = ts_ref[pl.ds(group * 2 + j, 1), cols]
-                sum_ref[0, :, cols] = sum_ref[0, :, cols] + (re * tc + im * ts)
-                sum_ref[1, :, cols] = sum_ref[1, :, cols] + (im * tc - re * ts)
+                re2, im2 = one + two, one - three
+                for j in range(2):
+                    re, im = re2[j * 128:(j + 1) * 128], im2[j * 128:(j + 1) * 128]
+                    tc = tc_ref[pl.ds(group * 2 + j, 1), cols]
+                    ts = ts_ref[pl.ds(group * 2 + j, 1), cols]
+                    sum_ref[0, :, cols] = sum_ref[0, :, cols] + (re * tc + im * ts)
+                    sum_ref[1, :, cols] = sum_ref[1, :, cols] + (im * tc - re * ts)
 
     for j in range(2):
         spin = turns(j)
@@ -610,8 +613,8 @@
         scratch_shapes=[
             pltpu.VMEM((1, 2, 4, 16384), f32), pltpu.VMEM((1, 16384), f32),
             pltpu.VMEM((64, 1024), bf16), pltpu.VMEM((64, 1024), bf16), pltpu.VMEM((256, 16), bf16),
-            pltpu.VMEM((1024, 1024), f8), pltpu.VMEM((16, 512), f32), pltpu.VMEM((16, 512), f32),
-            pltpu.VMEM((512, 1024), f8), pltpu.VMEM((512, 1024), f8), pltpu.VMEM((2, 128, 512), f32),
+            pltpu.VMEM((1024, 1536), f8), pltpu.VMEM((16, 512), f32), pltpu.VMEM((16, 512), f32),
+            pltpu.VMEM((768, 1024), f8), pltpu.VMEM((768, 1024), f8), pltpu.VMEM((2, 128, 512), f32),
             pltpu.SemaphoreType.DMA((5,)),
         ],
         compiler_params=params(44),

time: 66.3 us -> 67.8 us (1.023)
  local copies, waits for them, and re-layouts: 1.15 us -> 3.03 us
    unnamed x20, local copies, waits for them, and re-layouts: 1.15 us -> 3.03 us
  transfers between devices with their start and end apart: 2 -> 2, of which waited for: 1 -> 1; matrix products, arithmetic and copies ran while one was open for 0% -> 0% of each run, Pallas kernels for 31% -> 30%
where the time goes in v9:
time: 67.8 us; the launch traced here: 67.5 us
  Pallas kernels  35.8 us (53%)
  starting transfers between devices  14.7 us (22%)
  waiting for transfers between devices  13.6 us (20%)
  local copies, waits for them, and re-layouts  3.03 us (4%)
    all_to_all x1, waiting for transfers between devices, per_device(): lax.all_to_all(send.reshape(128, CHUNKS // 4, 4, 128), ('facet', 'rows'),...  13.6 us
    pallas_call x1, Pallas kernels, per_device(): pl.pallas_call(_exact_kernel, in_specs=[hbm] * 10, out_specs=[hbm] * 3, o...  12.1 us
    all_to_all x1, starting transfers between devices, per_device(): lax.all_to_all(send.reshape(128, CHUNKS // 4, 4, 128), ('facet', 'rows'),...  10.3 us
    pallas_call x1, Pallas kernels, per_device(): pl.pallas_call(_residual_kernel, in_specs=[hbm, vmem, hbm, vmem] + [hbm]...  9.26 us
    pallas_call x1, Pallas kernels, per_device(): pl.pallas_call(_phase_kernel, in_specs=[vmem] * 3, out_shape=shape((1024,...  8.04 us
    pallas_call x1, Pallas kernels, per_device(): pl.pallas_call(_rows_kernel, in_specs=[vmem] + [hbm] * 4 + [anywhere], ou...  6.42 us
    ppermute x1, starting transfers between devices, per_device(): peer = lax.ppermute(facets, 'rows', [(0, 1), (1, 0)])  4.43 us
    unnamed x20, local copies, waits for them, and re-layouts  3.03 us
  transfers between devices with their start and end apart: 2, of which 1 were waited for; matrix products, arithmetic and copies ran while one was open for 0% of the time, Pallas kernels for 30%

profile of v9, /device:TPU:1, one launch (start us, length us, event | category | flops | bytes accessed | tf_op | source)
XLA Modules:
  0.0 67.5 jit_solution(14710670282385314494)
XLA Ops:
  0.0 4.4 %collective-permute-start = (f32[1,2,4,16384]{3,2,1,0:T(4,128)}, f32[1,2,4,16384]{3,2,1,0:T(4,128)S(1)}, u32[]{:S(2)}, u32[]{:S(2)}) collective-permute-start(f32[1,2,4,16384]{3,2,1,0:T(4,128)} %own_hbm.1), channel_id=1, source_target_pairs={{0,1},{1,0},{2,3},{3,2},{4,5},{5,4},{6,7},{7,6},{8,9},{9,8},{10,11... | collective-permute-start | bytes 1572872 | tf_op jit(solution)/shard_map/ppermute | solution.py:575
  4.4 0.0 copy-start
  4.4 12.1 %exact_part.1 = (f32[64,1024]{1,0:T(8,128)}, f32[64,1024]{1,0:T(8,128)}, f32[64,2816]{1,0:T(8,128)}) custom-call(s32[1,64]{1,0:T(1,128)} %bitcast.15, s32[2,64]{1,0:T(2,128)} %bitcast.12, s32[1,64]{1,0:T(1,128)} %bitcast.14, s32[1,64]{1,0:T(1,128)} %bitcast.17, f32[1,1024]{1,0:T(1,128)} %bitcast.11, f32[1,2,4,16384]{3,2,1,0:T(4,128)} %own_hbm.1, ...), custom_call_target="tpu_custom_call" | custom-call | flops 8000000000 | bytes 2000000 | tf_op jit(solution)/shard_map/exact_part/pallas_call | solution.py:588
  16.5 0.0 collective-permute-done.peer_ref
  16.6 0.0 copy-done
  16.6 0.0 copy-done.1
  16.6 0.0 copy-done.5
  16.6 0.0 copy-done.6
  16.6 0.0 copy-start.2
  16.6 1.9 %copy-done.2 = f8e4m3fn[2,1024,1536]{2,1,0:T(32,128)(4,1)S(1)} copy-done((f8e4m3fn[2,1024,1536]{2,1,0:T(32,128)(4,1)S(1)}, f8e4m3fn[2,1024,1536]{2,1,0:T(32,128)(4,1)}, u32[]{:S(2)}) %copy-start.2) | copy-done | bytes 3145752
  18.5 1.1 %copy-done.9 = f32[64,2816]{1,0:T(8,128)S(1)} copy-done((f32[64,2816]{1,0:T(8,128)S(1)}, f32[64,2816]{1,0:T(8,128)}, u32[]{:S(2)}) %copy-start.9) | copy-done | bytes 720920
  19.6 9.3 %residual_part.1 = f32[2560,128]{1,0:T(8,128)} custom-call(f32[1,2,4,16384]{3,2,1,0:T(4,128)S(1)} %copy-done, f32[1,2,4,16384]{3,2,1,0:T(4,128)S(1)} %collective-permute-done.peer_ref, f32[1,16384]{1,0:T(1,128)S(1)} %bitcast.10, f32[64,2816]{1,0:T(8,128)S(1)} %copy-done.9, f8e4m3fn[2,1024,1536]{2,1,0:T(32,128)(4,1)S(1)} %copy-done.2, ...), custom_call_target="tpu_custom_call" | custom-call | flops 8999999488 | bytes 4000000 | tf_op jit(solution)/shard_map/residual_part/pallas_call | solution.py:609
  28.9 10.3 %all-to-all-start = ((f32[128,5,4,128]{3,2,1,0:T(4,128)}), f32[128,5,4,128]{3,2,1,0:T(4,128)S(1)}, u32[]{:S(2)}, u32[]{:S(2)}) async-start(f32[128,5,4,128]{3,2,1,0:T(4,128)} %bitcast.6), calls=%async_computation | async-start | bytes 2621440 | tf_op jit(solution)/shard_map/all_to_all | solution.py:628
  39.2 0.0 copy-start.3
  39.2 0.0 copy-start.4
  39.2 0.0 copy-start.7
  39.2 0.0 copy-start.8
  39.2 8.0 %row_phases.1.phases_any = bf16[1024,1024]{1,0:T(8,128)(2,1)} custom-call(s32[1,64]{1,0:T(1,128)} %bitcast.16, s32[2,64]{1,0:T(2,128)} %bitcast.13, s32[1,64]{1,0:T(1,128)} %bitcast.18), custom_call_target="tpu_custom_call" | custom-call | flops 3000000000 | bytes 2000000 | tf_op jit(solution)/shard_map/row_phases/pallas_call | solution.py:629
  47.3 13.6 %all-to-all-done = f32[128,5,4,128]{3,2,1,0:T(4,128)S(1)} async-done(((f32[128,5,4,128]{3,2,1,0:T(4,128)}), f32[128,5,4,128]{3,2,1,0:T(4,128)S(1)}, u32[]{:S(2)}, u32[]{:S(2)}) %all-to-all-start) | async-done | bytes 1310752 | tf_op jit(solution)/shard_map/all_to_all | solution.py:628
  60.9 0.0 copy-done.3
  60.9 0.0 copy-done.4
  60.9 0.0 copy-done.7
  60.9 0.0 copy-done.8
  60.9 6.4 %row_transform.1 = f32[1,2,512,1024]{3,2,1,0:T(8,128)} custom-call(f32[2560,128]{1,0:T(8,128)S(1)} %bitcast.8, bf16[256,1024]{1,0:T(8,128)(2,1)S(1)} %copy-done.4, bf16[256,1024]{1,0:T(8,128)(2,1)S(1)} %copy-done.3, f32[64,1024]{1,0:T(8,128)S(1)} %copy-done.7, f32[64,1024]{1,0:T(8,128)S(1)} %copy-done.8, bf16[1024,1024]{1,0:T(8,128)(2,1)} %row_phases.1.phases_any), custom_call_target="tpu_custom_call" | custom-call | flops 5000000000 | bytes 12000000 | tf_op jit(solution)/shard_map/row_transform/pallas_call | solution.py:639
  (4 shorter events, 0.0 us)
Async XLA Ops:
  0.0 16.5 %collective-permute-start = (f32[1,2,4,16384]{3,2,1,0:T(4,128)}, f32[1,2,4,16384]{3,2,1,0:T(4,128)S(1)}, u32[]{:S(2)}, u32[]{:S(2)}) collective-permute-start(f32[1,2,4,16384]{3,2,1,0:T(4,128)} %own_hbm.1), channel_id=1, source_target_pairs={{0,1},{1,0},{2,3},{3,2},{4,5},{5,4},{6,7},{7,6},{8,9},{9,8},{10,11... | collective-permute-start | bytes 1572872 | tf_op jit(solution)/shard_map/ppermute | solution.py:575
  4.4 12.1 %copy-start = (f32[1,2,4,16384]{3,2,1,0:T(4,128)S(1)}, f32[1,2,4,16384]{3,2,1,0:T(4,128)}, u32[]{:S(2)}) copy-start(f32[1,2,4,16384]{3,2,1,0:T(4,128)} %own_hbm.1) | copy-start | bytes 1572868
  4.4 12.1 %copy-start.1 = (f32[16384]{0:T(1024)S(1)}, f32[16384]{0:T(1024)}, u32[]{:S(2)}) copy-start(f32[16384]{0:T(1024)} %param.16) | copy-start | bytes 196612
  4.4 12.1 %copy-start.5 = (f32[16,512]{1,0:T(8,128)S(1)}, f32[16,512]{1,0:T(8,128)}, u32[]{:S(2)}) copy-start(f32[16,512]{1,0:T(8,128)} %constant.21.clone.ts_hbm) | copy-start | bytes 98308
  4.4 12.1 %copy-start.6 = (f32[16,512]{1,0:T(8,128)S(1)}, f32[16,512]{1,0:T(8,128)}, u32[]{:S(2)}) copy-start(f32[16,512]{1,0:T(8,128)} %constant.20.clone.tc_hbm) | copy-start | bytes 98308
  16.6 1.9 %copy-start.2 = (f8e4m3fn[2,1024,1536]{2,1,0:T(32,128)(4,1)S(1)}, f8e4m3fn[2,1024,1536]{2,1,0:T(32,128)(4,1)}, u32[]{:S(2)}) copy-start(f8e4m3fn[2,1024,1536]{2,1,0:T(32,128)(4,1)} %constant.19.clone.table_hbm) | copy-start | bytes 9437188
  18.5 1.1 %copy-start.9 = (f32[64,2816]{1,0:T(8,128)S(1)}, f32[64,2816]{1,0:T(8,128)}, u32[]{:S(2)}) copy-start(f32[64,2816]{1,0:T(8,128)} %get-tuple-element.8.pack_ref) | copy-start | bytes 2162692
  28.9 32.1 %all-to-all-start = ((f32[128,5,4,128]{3,2,1,0:T(4,128)}), f32[128,5,4,128]{3,2,1,0:T(4,128)S(1)}, u32[]{:S(2)}, u32[]{:S(2)}) async-start(f32[128,5,4,128]{3,2,1,0:T(4,128)} %bitcast.6), calls=%async_computation | async-start | bytes 2621440 | tf_op jit(solution)/shard_map/all_to_all | solution.py:628
  39.2 21.7 %copy-start.3 = (bf16[256,1024]{1,0:T(8,128)(2,1)S(1)}, bf16[256,1024]{1,0:T(8,128)(2,1)}, u32[]{:S(2)}) copy-start(bf16[256,1024]{1,0:T(8,128)(2,1)} %constant.23.clone.wl_hbm) | copy-start | bytes 1572868
  39.2 21.7 %copy-start.4 = (bf16[256,1024]{1,0:T(8,128)(2,1)S(1)}, bf16[256,1024]{1,0:T(8,128)(2,1)}, u32[]{:S(2)}) copy-start(bf16[256,1024]{1,0:T(8,128)(2,1)} %constant.22.clone.wh_hbm) | copy-start | bytes 1572868
  39.2 21.7 %copy-start.7 = (f32[64,1024]{1,0:T(8,128)S(1)}, f32[64,1024]{1,0:T(8,128)}, u32[]{:S(2)}) copy-start(f32[64,1024]{1,0:T(8,128)} %get-tuple-element.9.pc_hbm) | copy-start | bytes 786436
  39.2 21.7 %copy-start.8 = (f32[64,1024]{1,0:T(8,128)S(1)}, f32[64,1024]{1,0:T(8,128)}, u32[]{:S(2)}) copy-start(f32[64,1024]{1,0:T(8,128)} %get-tuple-element.10.ps_hbm) | copy-start | bytes 786436
